TPU v7x, 32 devices: a whole 2x2x4 slice. The times are simulated.
32 devices in a mesh: aux: 8 (over y, x, core), vir: 4 (over z).
Axes of the slice: x: 2, y: 2, z: 4, core: 2. Of those that a mesh axis runs over, the one named last changes fastest.
Arguments:
- integrals: float32 [4096, 128, 1024], P('aux', None, 'vir'), may hold values from -0.024964112 to 0.024964112, as said below
- occupied_energy: float32 [128], P('aux'), may hold values from -3.5 to -2
- virtual_energy: float32 [1024], P('vir'), may hold values from 1.5 to 6
- right_side: float32 [1024, 128], P('vir', 'aux'), may hold values from -500 to 500
Outputs:
- solution: float32 [1024, 128], P('vir', 'aux')
- residual: float32 [1024, 128], P('vir', 'aux')
Inputs may be any that keep to these rules, and one draw needn't show every extreme that they name: Entries of the integrals are of order one over the fourth root of 536870912.
All inputs are finite; a program needn't handle non-finite values.
Results may differ from a plain program's by a relative error of at most 0.0003.
Values sent between devices are 32-bit elements; how exact they have to be, the bound alone decides.
No kernel may reach another device: no remote copies, remote signals or barrier semaphores. Data moves between devices by JAX's collectives and lax.ppermute only.
A program may use at most 320 MiB of HBM per device.

v0:
```python
import jax
import jax.numpy as jnp
from jax import lax
from jax.sharding import PartitionSpec as P

ITERS = 3


HIGHEST = lax.Precision.HIGHEST


def paired_totals(vector, image):
    return lax.psum((jnp.sum(vector * vector), jnp.sum(vector * image)), ("aux", "vir"))


def on_device(integrals, occupied_energy, virtual_energy, right_side):
    energy_gap = virtual_energy[:, None] - occupied_energy[None, :]
    regrouped = lax.all_to_all(integrals, "vir", split_axis=0, concat_axis=2, tiled=True)
    aux_width = regrouped.shape[0]
    first_aux = lax.axis_index("vir") * aux_width

    def apply_hessian(local_vec):
        trial_rows = lax.all_gather(local_vec, "aux", axis=1, tiled=True)
        trial_full = lax.all_gather(trial_rows, "vir", axis=0, tiled=True)
        coulomb_part = jnp.einsum("pia,ai->p", integrals, trial_rows, precision=HIGHEST)
        coulomb_all = lax.psum(coulomb_part, "vir")
        coulomb = lax.dynamic_slice_in_dim(coulomb_all, first_aux, aux_width)
        inter = jnp.einsum("pib,bj->pij", regrouped, trial_full, precision=HIGHEST)
        coulomb_term = jnp.einsum("pia,p->ai", regrouped, coulomb, precision=HIGHEST)
        exchange_term = jnp.einsum("pij,pja->ai", inter, regrouped, precision=HIGHEST)
        vir_rows = lax.psum_scatter(
            4.0 * coulomb_term - exchange_term, "vir", scatter_dimension=0, tiled=True
        )
        summed = lax.psum_scatter(vir_rows, "aux", scatter_dimension=1, tiled=True)
        return energy_gap * local_vec + summed

    solution = jnp.zeros_like(right_side)
    residual = right_side
    image = apply_hessian(residual)
    norm_now, product = paired_totals(residual, image)
    step_len = norm_now / product
    direction = residual
    along = image
    for step in range(ITERS):
        solution = solution + step_len * direction
        residual = residual - step_len * along
        if step + 1 < ITERS:
            image = apply_hessian(residual)
            norm_next, product = paired_totals(residual, image)
            ratio = norm_next / norm_now
            step_len = norm_next / (product - ratio * norm_next / step_len)
            direction = residual + ratio * direction
            along = image + ratio * along
            norm_now = norm_next
    return (solution, residual)


def solution(mesh):
    in_specs = (P("aux", None, "vir"), P("aux"), P("vir"), P("vir", "aux"))
    out_specs = (P("vir", "aux"), P("vir", "aux"))
    return jax.shard_map(
        on_device, mesh=mesh, in_specs=in_specs, out_specs=out_specs, check_vma=False
    )
```

profile of v0, /device:TPU:1, one launch (start us, length us, event | category | flops | bytes accessed | tf_op | source)
XLA Modules:
  0.0 2487.8 jit_solution(10199998293793201570)
XLA Ops:
  7.2 13.0 all-to-all-start
  20.2 0.0 reduce-scatter.7.cloned.1.call-start
  20.2 10.6 all_gather.18
  30.8 21.7 multiply_reduce_fusion.2
  52.5 1052.1 %psum.64 = f32[512]{0:T(512)S(1)} all-reduce(f32[512]{0:T(512)S(1)} %multiply_reduce_fusion.2), channel_id=1, replica_groups=mesh['aux'=8,'vir'=4] {'vir'}, use_global_device_ids=true, to_apply=%region_2.0 | all-reduce | flops 512 | bytes 4096 | tf_op jit(solution)/shard_map/psum | solution.py:26
  1104.6 371.2 %all_gather.19 = f32[1024,128]{0,1:T(8,128)S(1)} all-gather(f32[256,128]{0,1:T(8,128)S(1)} %all_gather.18), channel_id=1, replica_groups=mesh['aux'=8,'vir'=4] {'vir'}, dimensions={0}, use_global_device_ids=true | all-gather | bytes 655360 | tf_op jit(solution)/shard_map/all_gather | solution.py:24
  1475.8 73.2 %copy.36 = f32[4,128,128,256]{3,0,1,2:T(4,128)} copy(f32[4,128,128,256]{3,2,1,0:T(8,128)} %bitcast.4) | data formatting | bytes 134217728 | tf_op jit(solution)/shard_map/all_to_all | solution.py:18
  1549.0 80.1 %all_to_all.16 = f32[128,128,1024]{2,0,1:T(8,128)} reshape(f32[128,128,4,256]{3,2,0,1:T(4,128)} %bitcast.96) | data formatting | bytes 134217728 | tf_op jit(solution)/shard_map/all_to_all | solution.py:18
  1629.2 57.8 %fusion.28 = f32[128,128,128]{2,0,1:T(8,128)} fusion(f32[128,128,1024]{2,0,1:T(8,128)} %all_to_all.16, f32[1024,128]{0,1:T(8,128)S(1)} %all_gather.19), kind=kOutput, calls=%fused_computation.23 | convolution fusion | flops 25769803776 | bytes 76021760 | tf_op jit(solution)/shard_map/pib,bj->pij/dot_general | solution.py:28
  1687.0 9.3 copy.12
  1696.3 35.8 %fusion.37 = f32[1,128,1024]{2,0,1:T(1,128)S(1)} fusion(f32[128,128,1024]{2,0,1:T(8,128)} %all_to_all.16, f32[512]{0:T(512)S(1)} %psum.64, s32[]{:T(128)S(6)} %select_n.2), kind=kOutput, calls=%fused_computation.47 | convolution fusion | flops 201326592 | bytes 67633664 | tf_op jit(solution)/shard_map/pia,p->ai/dot_general | solution.py:29
  1732.1 42.6 %fusion.11 = f32[1024,128]{0,1:T(8,128)} fusion(f32[128,128,128]{0,1,2:T(8,128)S(1)} %copy-done.2, f32[128,128,1024]{2,0,1:T(8,128)} %all_to_all.16, f32[1,128,1024]{2,0,1:T(1,128)S(1)} %fusion.37), kind=kOutput, calls=%fused_computation.12 | convolution fusion | flops 25770065920 | bytes 76546048 | tf_op jit(solution)/shard_map/pij,pja->ai/dot_general | solution.py:30
  1774.7 0.0 reduce-scatter.9.cloned.1.call-start
  1774.8 24.0 reduce-scatter.7.cloned.1.call-done
  1798.9 0.0 reduce-scatter.11.cloned.1.call-start
  1798.9 63.1 %copy.18 = f32[128,128,1024]{1,2,0:T(8,128)} copy(f32[128,128,1024]{2,0,1:T(8,128)} %all_to_all.16) | data formatting | bytes 134217728 | tf_op jit(solution)/shard_map/all_to_all | solution.py:18
  1862.0 1.4 multiply_reduce_fusion.7
  1863.4 39.9 %all-reduce.2 = (f32[]{:T(128)}, f32[]{:T(128)}) all-reduce(f32[]{:T(128)} %get-tuple-element.7, f32[]{:T(128)} %get-tuple-element.6), channel_id=1, replica_groups=mesh['aux'=8,'vir'=4] {'aux','vir'}, use_global_device_ids=true, to_apply=%region_1.0 | all-reduce | flops 2 | bytes 16 | tf_op jit(solution)/shard_map/psum | solution.py:13
  1904.6 0.8 multiply_subtract_fusion.2
  1905.4 11.3 all_gather.20
  1916.7 13.1 all_gather.21
  1929.8 22.1 multiply_reduce_fusion.1
  1951.9 40.9 %fusion.26 = f32[128,128,128]{2,0,1:T(8,128)} fusion(f32[128,128,1024]{1,2,0:T(8,128)} %copy.18, f32[1024,128]{0,1:T(8,128)S(1)} %all_gather.21), kind=kOutput, calls=%fused_computation.20 | convolution fusion | flops 25769803776 | bytes 76021760 | tf_op jit(solution)/shard_map/pib,bj->pij/dot_general | solution.py:28
  1992.8 9.3 copy.19
  2002.1 8.7 psum.67
  2010.8 35.8 %fusion.35 = f32[1,128,1024]{2,0,1:T(1,128)S(1)} fusion(f32[128,128,1024]{2,0,1:T(8,128)} %all_to_all.16, f32[512]{0:T(512)S(1)} %psum.67, s32[]{:T(128)S(6)} %select_n.2), kind=kOutput, calls=%fused_computation.45 | convolution fusion | flops 201326592 | bytes 67633664 | tf_op jit(solution)/shard_map/pia,p->ai/dot_general | solution.py:29
  2046.7 42.3 %fusion.21 = f32[1024,128]{0,1:T(8,128)} fusion(f32[128,128,1024]{2,0,1:T(8,128)} %all_to_all.16, f32[128,128,128]{1,2,0:T(8,128)S(1)} %copy-done.1, f32[1,128,1024]{2,0,1:T(1,128)S(1)} %fusion.35), kind=kOutput, calls=%fused_computation.16 | convolution fusion | flops 25770065920 | bytes 76546048 | tf_op jit(solution)/shard_map/pij,pja->ai/dot_general | solution.py:30
  2089.0 0.0 reduce-scatter.13.cloned.1.call-start
  2089.1 21.9 reduce-scatter.11.cloned.1.call-done
  2111.0 0.0 reduce-scatter.15.cloned.1.call-start
  2111.0 36.0 %reduce-scatter.13.cloned.1.call-done = f32[256,16]{0,1:T(8,128)} async-done(((f32[256,128]{0,1:T(8,128)}), f32[256,16]{0,1:T(8,128)}) %reduce-scatter.13.cloned.1.call-update) | async-done | bytes 16400 | tf_op jit(solution)/shard_map/reduce_scatter | solution.py:34
  2147.1 1.4 multiply_reduce_fusion.5
  2148.5 39.4 %all-reduce.1 = (f32[]{:T(128)}, f32[]{:T(128)}) all-reduce(f32[]{:T(128)} %get-tuple-element.5, f32[]{:T(128)} %get-tuple-element.4), channel_id=1, replica_groups=mesh['aux'=8,'vir'=4] {'aux','vir'}, use_global_device_ids=true, to_apply=%region_8.0 | all-reduce | flops 2 | bytes 16 | tf_op jit(solution)/shard_map/psum | solution.py:13
  2192.5 0.8 multiply_subtract_fusion.1
  2193.3 11.3 all_gather.22
  2204.6 13.0 all_gather.23
  2217.6 21.9 multiply_reduce_fusion
  2239.5 40.9 %fusion.24 = f32[128,128,128]{2,0,1:T(8,128)} fusion(f32[128,128,1024]{1,2,0:T(8,128)} %copy.18, f32[1024,128]{0,1:T(8,128)S(1)} %all_gather.23), kind=kOutput, calls=%fused_computation.17 | convolution fusion | flops 25769803776 | bytes 76021760 | tf_op jit(solution)/shard_map/pib,bj->pij/dot_general | solution.py:28
  2280.4 9.3 copy.25
  2289.7 8.8 psum.70
  2298.5 35.8 %fusion.33 = f32[1,128,1024]{2,0,1:T(1,128)S(1)} fusion(f32[128,128,1024]{2,0,1:T(8,128)} %all_to_all.16, f32[512]{0:T(512)S(1)} %psum.70, s32[]{:T(128)S(6)} %select_n.2), kind=kOutput, calls=%fused_computation.43 | convolution fusion | flops 201326592 | bytes 67633664 | tf_op jit(solution)/shard_map/pia,p->ai/dot_general | solution.py:29
  2334.3 42.4 %fusion.15 = f32[1024,128]{0,1:T(8,128)} fusion(f32[128,128,1024]{2,0,1:T(8,128)} %all_to_all.16, f32[128,128,128]{1,2,0:T(8,128)S(1)} %copy-done, f32[1,128,1024]{2,0,1:T(1,128)S(1)} %fusion.33), kind=kOutput, calls=%fused_computation.14 | convolution fusion | flops 25770065920 | bytes 76546048 | tf_op jit(solution)/shard_map/pij,pja->ai/dot_general | solution.py:30
  2376.7 0.0 reduce-scatter.17.cloned.1.call-start
  2376.8 21.9 reduce-scatter.15.cloned.1.call-done
  2398.7 35.8 %reduce-scatter.17.cloned.1.call-done = f32[256,16]{0,1:T(8,128)} async-done(((f32[256,128]{0,1:T(8,128)}), f32[256,16]{0,1:T(8,128)}) %reduce-scatter.17.cloned.1.call-update) | async-done | bytes 16400 | tf_op jit(solution)/shard_map/reduce_scatter | solution.py:34
  2434.5 1.4 multiply_reduce_fusion.3
  2435.9 39.4 %all-reduce = (f32[]{:T(128)}, f32[]{:T(128)}) all-reduce(f32[]{:T(128)} %get-tuple-element.3, f32[]{:T(128)} %get-tuple-element.2), channel_id=1, replica_groups=mesh['aux'=8,'vir'=4] {'aux','vir'}, use_global_device_ids=true, to_apply=%region_15.0 | all-reduce | flops 2 | bytes 16 | tf_op jit(solution)/shard_map/psum | solution.py:13
  2479.3 1.4 multiply_subtract_fusion
  (24 shorter events, 0.1 us)
Async XLA Ops:
  7.2 13.1 copy-start.3
  7.2 1468.7 %all-to-all-start = ((f32[512,128,256]{2,1,0:T(8,128)}), f32[512,128,256]{2,1,0:T(8,128)}, u32[]{:S(2)}, u32[]{:S(2)}) async-start(f32[512,128,256]{2,1,0:T(8,128)} %param.4), calls=%async_computation | async-start | bytes 134217728 | tf_op jit(solution)/shard_map/all_to_all | solution.py:18
  20.2 1778.6 %reduce-scatter.7.cloned.1.call-start = ((), (), s32[]{:S(2)}) async-start(), calls=%async_computation.7 | async-start | bytes 655360 | tf_op jit(solution)/shard_map/reduce_scatter | solution.py:31
  1696.3 35.8 %copy-start.2 = (f32[128,128,128]{0,1,2:T(8,128)S(1)}, f32[128,128,128]{0,1,2:T(8,128)}, u32[]{:S(2)}) copy-start(f32[128,128,128]{0,1,2:T(8,128)} %copy.12) | copy-start | bytes 25165828
  1774.7 87.3 %reduce-scatter.9.cloned.1.call-start = ((), (), s32[]{:S(2)}) async-start(), calls=%async_computation.8 | async-start | bytes 147456 | tf_op jit(solution)/shard_map/reduce_scatter | solution.py:34
  1798.8 63.2 %copy-start.4 = (f32[256,16]{0,1:T(8,128)S(1)}, f32[256,16]{0,1:T(8,128)}, u32[]{:S(2)}) copy-start(f32[256,16]{0,1:T(8,128)} %param.7) | copy-start | bytes 49156
  1798.8 63.2 %copy-start.6 = (f32[256]{0:T(256)S(1)}, f32[256]{0:T(256)}, u32[]{:S(2)}) copy-start(f32[256]{0:T(256)} %param.6) | copy-start | bytes 3076
  1798.8 63.2 %copy-start.7 = (f32[16]{0:T(128)S(1)}, f32[16]{0:T(128)}, u32[]{:S(2)}) copy-start(f32[16]{0:T(128)} %param.5) | copy-start | bytes 196
  1798.9 312.1 %reduce-scatter.11.cloned.1.call-start = ((), (), s32[]{:S(2)}) async-start(), calls=%async_computation.9 | async-start | bytes 655360 | tf_op jit(solution)/shard_map/reduce_scatter | solution.py:31
  2010.8 35.8 %copy-start.1 = (f32[128,128,128]{1,2,0:T(8,128)S(1)}, f32[128,128,128]{1,2,0:T(8,128)}, u32[]{:S(2)}) copy-start(f32[128,128,128]{1,2,0:T(8,128)} %copy.19) | copy-start | bytes 25165828
  2010.8 181.6 %copy-start.5 = (f32[256,16]{0,1:T(8,128)S(1)}, f32[256,16]{0,1:T(8,128)}, u32[]{:S(2)}) copy-start(f32[256,16]{0,1:T(8,128)} %reduce-scatter.9.cloned.1.call-done) | copy-start | bytes 49156
  2089.0 58.0 %reduce-scatter.13.cloned.1.call-start = ((), (), s32[]{:S(2)}) async-start(), calls=%async_computation.10 | async-start | bytes 147456 | tf_op jit(solution)/shard_map/reduce_scatter | solution.py:34
  2111.0 287.7 %reduce-scatter.15.cloned.1.call-start = ((), (), s32[]{:S(2)}) async-start(), calls=%async_computation.11 | async-start | bytes 655360 | tf_op jit(solution)/shard_map/reduce_scatter | solution.py:31
  2298.5 35.8 %copy-start = (f32[128,128,128]{1,2,0:T(8,128)S(1)}, f32[128,128,128]{1,2,0:T(8,128)}, u32[]{:S(2)}) copy-start(f32[128,128,128]{1,2,0:T(8,128)} %copy.25) | copy-start | bytes 25165828
  2376.7 57.8 %reduce-scatter.17.cloned.1.call-start = ((), (), s32[]{:S(2)}) async-start(), calls=%async_computation.12 | async-start | bytes 147456 | tf_op jit(solution)/shard_map/reduce_scatter | solution.py:34
Sparse Core Ops, SparseCore 0:
  1774.8 23.9 reduce-scatter.6
  1801.8 32.9 reduce-scatter.8
  2089.2 21.7 reduce-scatter.10
  2114.1 32.9 reduce-scatter.12
  2376.8 21.7 reduce-scatter.14
  2401.5 32.9 reduce-scatter.16
where the time goes:
time: 2500 us; the launch traced here: 2490 us
  blocking collectives  1620 us (65%)
  matrix products  374 us (15%)
  local copies, waits for them, and re-layouts  244 us (10%)
  waiting for transfers between devices  140 us (6%)
  other arithmetic  72.9 us (3%)
    psum x3, blocking collectives, apply_hessian(): coulomb_all = lax.psum(coulomb_part, 'vir')  1070 us
    all_gather x3, blocking collectives, apply_hessian(): trial_full = lax.all_gather(trial_rows, 'vir', axis=0, tiled=True)  397 us
    all_to_all x3, local copies, waits for them, and re-layouts, on_device(): lax.all_to_all(integrals, 'vir', split_axis=0, concat_axis=2, tiled=True)  216 us
    dot_general x3, matrix products, apply_hessian(): inter = jnp.einsum('pib,bj->pij', regrouped, trial_full, precision=HIGHEST)  140 us
    dot_general x3, matrix products, apply_hessian(): jnp.einsum('pij,pja->ai', inter, regrouped, precision=HIGHEST)  127 us
    psum x3, blocking collectives, paired_totals(): lax.psum((jnp.sum(vector * vector), jnp.sum(vector * image)), ('aux', 'vi...  119 us
    dot_general x3, matrix products, apply_hessian(): jnp.einsum('pia,p->ai', regrouped, coulomb, precision=HIGHEST)  107 us
    reduce_scatter x3, waiting for transfers between devices, apply_hessian(): summed = lax.psum_scatter(vir_rows, 'aux', scatter_dimension=1, tiled=True)  71.8 us
  transfers between devices with their start and end apart: 7, of which 5 were waited for; matrix products, arithmetic and copies ran while one was open for 3% of the time, Pallas kernels for 0%

commit v1 on v0

v1 whole, which is shorter than its diff:
```python
import functools

import jax
import jax.numpy as jnp
from jax import lax
from jax.experimental import pallas as pl
from jax.experimental.pallas import tpu as pltpu
from jax.sharding import PartitionSpec as P

ITERS = 3
PARTS = (3, 6, 5, 2)
CARRIER = 1
BF16 = jnp.bfloat16
F32 = jnp.float32


def halves(value):
    high = value.astype(BF16)
    return high, (value - high.astype(F32)).astype(BF16)


def load_direction(direction, both):
    occ = direction.shape[0]
    high, low = halves(direction.T)
    both[:, :occ] = high
    both[:, occ:] = low


def coefficients(inter, count):
    occ = inter.shape[1]
    rows = lax.broadcasted_iota(jnp.int32, (occ, occ), 0)
    cols = lax.broadcasted_iota(jnp.int32, (occ, occ), 1)
    diagonal = rows == cols
    highs, lows = [], []
    for p in range(count):
        block = inter[p * occ : (p + 1) * occ]
        trace = jnp.sum(jnp.where(diagonal, block, 0.0))
        high, low = halves(jnp.where(diagonal, 4.0 * trace, 0.0) - block)
        highs.append(high)
        lows.append(low)
    return jnp.concatenate(highs, axis=1), jnp.concatenate(lows, axis=1)


def dot(a, b):
    return jnp.dot(a, b, preferred_element_type=F32)


def first_kernel(first, pieces, direction, *rest):
    if first:
        high_ref, low_ref, total, both = rest
    else:
        before, _, _, high_ref, low_ref, total, both = rest
    groups, count, occ, width = pieces.shape
    rows = count * occ

    @pl.when(pl.program_id(0) == 0)
    def _():
        load_direction(direction[...], both)
        total[...] = jnp.zeros_like(total) if first else before[...]

    inter = jnp.zeros((rows, occ), F32)
    for g in range(groups):
        span = slice(g * width, (g + 1) * width)
        high, low = halves(pieces[g].reshape(rows, width))
        high_ref[:, :, span] = high.reshape(count, occ, width)
        low_ref[:, :, span] = low.reshape(count, occ, width)
        wide = dot(high, both[span, :])
        inter += wide[:, :occ] + wide[:, occ:] + dot(low, both[span, :occ])
    coef_high, coef_low = coefficients(inter, count)
    coef = jnp.concatenate([coef_high, coef_low], axis=0)
    for g in range(groups):
        span = slice(g * width, (g + 1) * width)
        wide = dot(coef, high_ref[:, :, span].reshape(rows, width))
        narrow = dot(coef_high, low_ref[:, :, span].reshape(rows, width))
        total[:, span] += wide[:occ] + wide[occ:] + narrow


def first_part(pieces, direction, before, offset, held, count):
    groups, _, occ, width = pieces.shape
    whole = groups * width
    step = max(s for s in (8, 4, 2, 1) if count % s == 0 and offset % s == 0)
    fixed = pl.BlockSpec((occ, whole), lambda s: (0, 0))
    in_specs = [pl.BlockSpec((groups, step, occ, width), lambda s: (0, s, 0, 0)), fixed]
    args = [pieces, direction]
    aliases = {}
    first = not isinstance(before, tuple)
    if first:
        shape = jax.ShapeDtypeStruct((held, occ, whole), BF16)
    else:
        total, high, low = before
        in_specs += [fixed, pl.BlockSpec(memory_space=pl.ANY), pl.BlockSpec(memory_space=pl.ANY)]
        args += [total, high, low]
        aliases = {3: 0, 4: 1, 2: 2}
        shape = jax.ShapeDtypeStruct(high.shape, BF16)
    start = offset // step
    store = pl.BlockSpec((step, occ, whole), lambda s: (start + s, 0, 0))
    high, low, total = pl.pallas_call(
        functools.partial(first_kernel, first),
        grid=(count // step,),
        in_specs=in_specs,
        out_specs=[store, store, fixed],
        out_shape=[shape, shape, jax.ShapeDtypeStruct((occ, whole), F32)],
        scratch_shapes=[pltpu.VMEM((whole, 2 * occ), BF16)],
        input_output_aliases=aliases,
        compiler_params=pltpu.CompilerParams(vmem_limit_bytes=48 * 1024 * 1024),
    )(*args)
    return total, high, low


def advance(summed, gap, direction, residual, iterate):
    image = gap * direction + summed
    norm = jnp.sum(residual * residual)
    step = norm / jnp.sum(direction * image)
    return iterate + step * direction, residual - step * image, norm


def later_kernel(high_ref, low_ref, summed, gap, direction, residual, iterate,
                 total, new_direction, new_residual, new_iterate, both):
    count, occ, whole = high_ref.shape
    rows = count * occ

    @pl.when(pl.program_id(0) == 0)
    def _():
        point, left, norm = advance(summed[...], gap[...], direction[...], residual[...], iterate[...])
        along = left + (jnp.sum(left * left) / norm) * direction[...]
        new_iterate[...] = point
        new_residual[...] = left
        new_direction[...] = along
        load_direction(along, both)
        total[...] = jnp.zeros_like(total)

    high = high_ref[...].reshape(rows, whole)
    low = low_ref[...].reshape(rows, whole)
    wide = dot(high, both[...])
    inter = wide[:, :occ] + wide[:, occ:] + dot(low, both[:, :occ])
    coef_high, coef_low = coefficients(inter, count)
    coef = jnp.concatenate([coef_high, coef_low], axis=0)
    wide = dot(coef, high)
    total[...] += wide[:occ] + wide[occ:] + dot(coef_high, low)


def later_apply(high, low, *state):
    held, occ, whole = high.shape
    step = max(s for s in (8, 4, 2, 1) if held % s == 0)
    fixed = pl.BlockSpec((occ, whole), lambda s: (0, 0))
    block = pl.BlockSpec((step, occ, whole), lambda s: (s, 0, 0))
    return pl.pallas_call(
        later_kernel,
        grid=(held // step,),
        in_specs=[block, block] + [fixed] * 5,
        out_specs=[fixed] * 4,
        out_shape=[jax.ShapeDtypeStruct((occ, whole), F32)] * 4,
        scratch_shapes=[pltpu.VMEM((whole, 2 * occ), BF16)],
        compiler_params=pltpu.CompilerParams(vmem_limit_bytes=48 * 1024 * 1024),
    )(high, low, *state)


def on_device(groups, integrals, occupied_energy, virtual_energy, right_side):
    aux_rows, occ, width = integrals.shape
    whole = groups * width
    unit = aux_rows // groups // sum(PARTS)

    mine = occupied_energy.shape[0]
    sent = jnp.concatenate(
        [right_side.T, jnp.broadcast_to(occupied_energy[:, None], (mine, 128))], axis=1
    )
    columns = lax.all_gather(sent, "aux", axis=0, tiled=True)
    carried = jnp.stack(
        [columns[:, :width], virtual_energy[None, :] - columns[:, width : width + 1]]
    )

    received = []
    low_row = 0
    for k, share in enumerate(PARTS):
        count = share * unit
        part = integrals[low_row : low_row + groups * count].reshape(groups, count, occ, width)
        low_row += groups * count
        if k == CARRIER:
            extra = jnp.broadcast_to(carried[None], (groups,) + carried.shape)
            part = jnp.concatenate([part, extra], axis=1)
        if k >= 2:
            part, _ = lax.optimization_barrier((part, received[k - 2]))
        received.append(lax.all_to_all(part, "vir", split_axis=0, concat_axis=0, tiled=True))

    at = PARTS[CARRIER] * unit
    start, gap = (
        jnp.moveaxis(received[CARRIER][:, at + n], 0, 1).reshape(occ, whole) for n in range(2)
    )
    held = None
    offset = 0
    for k, share in enumerate(PARTS):
        count = share * unit
        held = first_part(received[k], start, held, offset, aux_rows // groups, count)
        offset += count
    total, high, low = held

    direction = residual = start
    iterate = jnp.zeros_like(start)
    for _ in range(ITERS - 1):
        summed = lax.psum(total, ("aux", "vir"))
        total, direction, residual, iterate = later_apply(
            high, low, summed, gap, direction, residual, iterate
        )
    summed = lax.psum(total, ("aux", "vir"))
    iterate, residual, _ = advance(summed, gap, direction, residual, iterate)

    def own(array):
        block = lax.dynamic_slice(
            array, (lax.axis_index("aux") * mine, lax.axis_index("vir") * width), (mine, width)
        )
        return block.T

    return own(iterate), own(residual)


def solution(mesh):
    in_specs = (P("aux", None, "vir"), P("aux"), P("vir"), P("vir", "aux"))
    out_specs = (P("vir", "aux"), P("vir", "aux"))
    return jax.shard_map(
        functools.partial(on_device, mesh.shape["vir"]),
        mesh=mesh,
        in_specs=in_specs,
        out_specs=out_specs,
        check_vma=False,
    )
```

time: 2500 us -> 2000 us (0.80)
  waiting for transfers between devices: 140 us -> 1750 us
  blocking collectives: 1620 us -> 10.9 us
  matrix products: 374 us -> 0 us
  local copies, waits for them, and re-layouts: 244 us -> 41.4 us
  Pallas kernels: 0 us -> 136 us
  other arithmetic: 72.9 us -> 14.8 us
    all_to_all x1 -> x4, waiting for transfers between devices: 0.01 us -> 1370 us  [on_device(): lax.all_to_all(part, 'vir', split_axis=0, concat_axis=0, tiled=True)]
    psum x6 -> x0, blocking collectives: 1190 us -> none  [the longest x3 1070 us: apply_hessian(): coulomb_all = lax.psum(coulomb_part, 'vir')]
    all_gather x6 -> x1, blocking collectives: 431 us -> 10.9 us  [on_device(): columns = lax.all_gather(sent, 'aux', axis=0, tiled=True)]
    psum x0 -> x3, waiting for transfers between devices: none -> 380 us  [on_device(): summed = lax.psum(total, ('aux', 'vir'))]
    dot_general x9 -> x0, matrix products: 374 us -> none  [the longest x3 140 us: apply_hessian(): inter = jnp.einsum('pib,bj->pij', regrouped, trial_full, precision=HIGHEST)]
    all_to_all x3 -> x0, local copies, waits for them, and re-layouts: 216 us -> none  [on_device(): lax.all_to_all(integrals, 'vir', split_axis=0, concat_axis=2, tiled=True)]
    reduce_scatter x6 -> x0, waiting for transfers between devices: 140 us -> none  [the longest x3 71.8 us: apply_hessian(): summed = lax.psum_scatter(vir_rows, 'aux', scatter_dimension=1, tiled=True)]
    pallas_call x0 -> x6, Pallas kernels: none -> 136 us  [the longest x2 76.8 us: later_apply(): pl.pallas_call(later_kernel, grid=(held // step,), in_specs=[block, block...]
  transfers between devices with their start and end apart: 7 -> 7, of which waited for: 5 -> 7; matrix products, arithmetic and copies ran while one was open for 3% -> 2% of each run, Pallas kernels for 0% -> 3%
where the time goes in v1:
time: 2000 us
  waiting for transfers between devices  1750 us (88%)
  Pallas kernels  136 us (7%)
  local copies, waits for them, and re-layouts  41.4 us (2%)
  starting transfers between devices  28.9 us (1%)
    all_to_all x4, waiting for transfers between devices, on_device(): lax.all_to_all(part, 'vir', split_axis=0, concat_axis=0, tiled=True)  1370 us
    psum x3, waiting for transfers between devices, on_device(): summed = lax.psum(total, ('aux', 'vir'))  380 us
    pallas_call x2, Pallas kernels, later_apply(): pl.pallas_call(later_kernel, grid=(held // step,), in_specs=[block, block...  76.8 us
    pallas_call x4, Pallas kernels, first_part(): pl.pallas_call(functools.partial(first_kernel, first), grid=(count // ste...  59.3 us
  transfers between devices with their start and end apart: 7, of which 7 were waited for; matrix products, arithmetic and copies ran while one was open for 2% of the time, Pallas kernels for 3%

profile of v1, /device:TPU:1, one launch (start us, length us, event | category | flops | bytes accessed | tf_op | source)
XLA Modules:
  0.0 2000.9 jit_solution(13694940925368587302)
XLA Ops:
  7.2 10.8 slice.30
  17.9 6.3 all-to-all-start.2
  24.3 0.0 copy-start.7
  24.3 0.0 copy-start.5
  24.3 0.0 copy-start.6
  24.3 0.0 slice-start
  24.3 0.6 copy-done.7
  24.9 0.1 broadcast_in_dim.6
  25.0 0.0 copy-done.5
  25.0 10.9 all_gather.3
  35.9 0.1 slice_reduce_fusion
  36.0 0.1 broadcast_subtract_fusion
  36.1 0.1 broadcast_in_dim.7
  36.2 0.0 slice-done
  36.2 10.8 pad_maximum_fusion
  47.0 250.7 %all-to-all-done.2.pieces = f32[4,24,128,256]{3,2,1,0:T(8,128)} async-done(((f32[4,24,128,256]{3,2,1,0:T(8,128)}), f32[4,24,128,256]{3,2,1,0:T(8,128)}, u32[]{:S(2)}, u32[]{:S(2)}) %all-to-all-start.2) | async-done | bytes 12582944 | tf_op jit(solution)/shard_map/all_to_all | solution.py:183
  297.7 8.6 all-to-all-start
  306.3 16.0 slice.29
  322.4 548.5 %all-to-all-done.pieces = f32[4,50,128,256]{3,2,1,0:T(8,128)} async-done(((f32[4,50,128,256]{3,2,1,0:T(8,128)}), f32[4,50,128,256]{3,2,1,0:T(8,128)}, u32[]{:S(2)}, u32[]{:S(2)}) %all-to-all-start) | async-done | bytes 26214432 | tf_op jit(solution)/shard_map/all_to_all | solution.py:183
  870.9 7.8 all-to-all-start.3
  878.8 7.7 slice.24
  886.5 444.5 %all-to-all-done.3.pieces = f32[4,40,128,256]{3,2,1,0:T(8,128)} async-done(((f32[4,40,128,256]{3,2,1,0:T(8,128)}), f32[4,40,128,256]{3,2,1,0:T(8,128)}, u32[]{:S(2)}, u32[]{:S(2)}) %all-to-all-start.3) | async-done | bytes 20971552 | tf_op jit(solution)/shard_map/all_to_all | solution.py:183
  1331.0 5.6 all-to-all-start.1
  1336.6 0.2 all-reduce.4.cloned.1.call-start
  1336.8 1.3 slice_bitcast_fusion
  1338.2 12.1 shard_map.59
  1350.3 20.5 %shard_map.60 = (bf16[128,128,1024]{2,1,0:T(8,128)(2,1)}, bf16[128,128,1024]{2,1,0:T(8,128)(2,1)}, f32[128,1024]{1,0:T(8,128)}) custom-call(f32[4,50,128,256]{3,2,1,0:T(8,128)} %all-to-all-done.pieces, f32[128,1024]{1,0:T(8,128)S(1)} %bitcast.24, f32[128,1024]{1,0:T(8,128)} %get-tuple-element.26.rest_0_, ...), custom_call_target="tpu_custom_call", output_to_operand_aliasing={{0}: (3, {}), {1}: (4, {}), {2}: (2, {})} | custom-call | tf_op jit(solution)/shard_map/pallas_call | solution.py:97
  1370.7 18.5 shard_map.61
  1389.2 130.0 %all-to-all-done.1.pieces = f32[4,16,128,256]{3,2,1,0:T(8,128)} async-done(((f32[4,16,128,256]{3,2,1,0:T(8,128)}), f32[4,16,128,256]{3,2,1,0:T(8,128)}, u32[]{:S(2)}, u32[]{:S(2)}) %all-to-all-start.1) | async-done | bytes 8388640 | tf_op jit(solution)/shard_map/all_to_all | solution.py:183
  1519.2 8.3 shard_map.62
  1527.5 0.0 all-reduce.4.cloned.1.call-update
  1527.5 0.0 all-reduce.6.cloned.1.call-start
  1527.6 126.8 %all-reduce.4.cloned.1.call-done.summed = f32[128,1024]{1,0:T(8,128)} async-done(((f32[128,1024]{1,0:T(8,128)}), f32[128,1024]{1,0:T(8,128)}) %all-reduce.4.cloned.1.call-update) | async-done | bytes 524304 | tf_op jit(solution)/shard_map/psum | solution.py:200
  1654.4 1.0 copy-done
  1655.5 38.4 %shard_map.63 = (f32[128,1024]{1,0:T(8,128)S(1)}, f32[128,1024]{1,0:T(8,128)S(1)}, f32[128,1024]{1,0:T(8,128)S(1)}, f32[128,1024]{1,0:T(8,128)S(1)}) custom-call(bf16[128,128,1024]{2,1,0:T(8,128)(2,1)} %get-tuple-element.35.high_ref, bf16[128,128,1024]{2,1,0:T(8,128)(2,1)} %get-tuple-element.36.low_ref, f32[128,1024]{1,0:T(8,128)S(1)} %copy-done, ...), custom_call_target="tpu_custom_call" | custom-call | tf_op jit(solution)/shard_map/pallas_call | solution.py:147
  1693.9 0.8 copy-done.3
  1694.7 0.0 all-reduce.6.cloned.1.call-update
  1694.7 0.3 all-reduce.8.cloned.1.call-start
  1695.0 126.7 %all-reduce.6.cloned.1.call-done.summed = f32[128,1024]{1,0:T(8,128)} async-done(((f32[128,1024]{1,0:T(8,128)}), f32[128,1024]{1,0:T(8,128)}) %all-reduce.6.cloned.1.call-update) | async-done | bytes 524304 | tf_op jit(solution)/shard_map/psum | solution.py:200
  1821.7 1.0 copy-done.1
  1822.7 38.4 %shard_map.64 = (f32[128,1024]{1,0:T(8,128)S(1)}, f32[128,1024]{1,0:T(8,128)S(1)}, f32[128,1024]{1,0:T(8,128)S(1)}, f32[128,1024]{1,0:T(8,128)S(1)}) custom-call(bf16[128,128,1024]{2,1,0:T(8,128)(2,1)} %get-tuple-element.35.high_ref, bf16[128,128,1024]{2,1,0:T(8,128)(2,1)} %get-tuple-element.36.low_ref, f32[128,1024]{1,0:T(8,128)S(1)} %copy-done.1, ...), custom_call_target="tpu_custom_call" | custom-call | tf_op jit(solution)/shard_map/pallas_call | solution.py:147
  1861.2 0.8 copy-done.2
  1861.9 0.8 copy-done.4
  1862.8 0.0 all-reduce.8.cloned.1.call-update
  1862.8 0.7 multiply_reduce_fusion.1
  1863.5 126.3 %all-reduce.8.cloned.1.call-done = f32[128,1024]{1,0:T(8,128)} async-done(((f32[128,1024]{1,0:T(8,128)}), f32[128,1024]{1,0:T(8,128)}) %all-reduce.8.cloned.1.call-update) | async-done | bytes 524304 | tf_op jit(solution)/shard_map/psum | solution.py:204
  1989.8 1.8 multiply_reduce_fusion
  1993.0 1.3 fusion
  (12 shorter events, 0.2 us)
Async XLA Ops:
  17.9 279.8 %all-to-all-start.2 = ((f32[4,24,128,256]{3,2,1,0:T(8,128)}), f32[4,24,128,256]{3,2,1,0:T(8,128)}, u32[]{:S(2)}, u32[]{:S(2)}) async-start(f32[4,24,128,256]{3,2,1,0:T(8,128)} %bitcast.34), calls=%async_computation.2 | async-start | bytes 25165824 | tf_op jit(solution)/shard_map/all_to_all | solution.py:183
  24.3 0.7 copy-start.7
  24.3 0.7 copy-start.5
  24.3 11.7 copy-start.6
  24.3 11.9 slice-start
  297.7 573.2 %all-to-all-start = ((f32[4,50,128,256]{3,2,1,0:T(8,128)}), f32[4,50,128,256]{3,2,1,0:T(8,128)}, u32[]{:S(2)}, u32[]{:S(2)}) async-start(f32[4,50,128,256]{3,2,1,0:T(8,128)} %pad_maximum_fusion), calls=%async_computation | async-start | bytes 52428800 | tf_op jit(solution)/shard_map/all_to_all | solution.py:183
  870.9 460.1 %all-to-all-start.3 = ((f32[4,40,128,256]{3,2,1,0:T(8,128)}), f32[4,40,128,256]{3,2,1,0:T(8,128)}, u32[]{:S(2)}, u32[]{:S(2)}) async-start(f32[4,40,128,256]{3,2,1,0:T(8,128)} %bitcast.33), calls=%async_computation.3 | async-start | bytes 41943040 | tf_op jit(solution)/shard_map/all_to_all | solution.py:183
  1331.0 188.2 %all-to-all-start.1 = ((f32[4,16,128,256]{3,2,1,0:T(8,128)}), f32[4,16,128,256]{3,2,1,0:T(8,128)}, u32[]{:S(2)}, u32[]{:S(2)}) async-start(f32[4,16,128,256]{3,2,1,0:T(8,128)} %bitcast.35), calls=%async_computation.1 | async-start | bytes 16777216 | tf_op jit(solution)/shard_map/all_to_all | solution.py:183
  1336.6 317.8 %all-reduce.4.cloned.1.call-start = ((), (), s32[]{:S(2)}) async-start(), calls=%async_computation.4 | async-start | bytes 1048576 | tf_op jit(solution)/shard_map/psum | solution.py:200
  1527.5 294.2 %all-reduce.6.cloned.1.call-start = ((), (), s32[]{:S(2)}) async-start(), calls=%async_computation.5 | async-start | bytes 1048576 | tf_op jit(solution)/shard_map/psum | solution.py:200
  1654.4 1.0 copy-start
  1693.9 0.8 copy-start.3
  1694.7 295.1 %all-reduce.8.cloned.1.call-start = ((), (), s32[]{:S(2)}) async-start(), calls=%async_computation.6 | async-start | bytes 1048576 | tf_op jit(solution)/shard_map/psum | solution.py:204
  1821.7 1.0 copy-start.1
  1861.1 0.8 copy-start.2
  1861.9 0.8 copy-start.4
Sparse Core Ops, SparseCore 0:
  1527.6 126.7 all-reduce.3
  1694.8 126.8 all-reduce.5
  1862.9 126.8 all-reduce.7

commit v2 on v1

--- a/solution.py
+++ b/solution.py
@@ -8,7 +8,7 @@
 from jax.sharding import PartitionSpec as P
 
 ITERS = 3
-PARTS = (3, 6, 5, 2)
+PARTS = (4, 4, 4, 2, 2)
 CARRIER = 1
 BF16 = jnp.bfloat16
 F32 = jnp.float32
@@ -45,13 +45,19 @@
     return jnp.dot(a, b, preferred_element_type=F32)
 
 
-def first_kernel(first, pieces, direction, *rest):
+def first_kernel(first, groups, *refs):
+    pieces, direction, rest = refs[:groups], refs[groups], refs[groups + 1 :]
     if first:
         high_ref, low_ref, total, both = rest
     else:
         before, _, _, high_ref, low_ref, total, both = rest
-    groups, count, occ, width = pieces.shape
+    count, occ, width = pieces[0].shape
     rows = count * occ
+    me = lax.axis_index("vir")
+
+    def columns(shift):
+        source = lax.rem(me - shift + groups, groups)
+        return pl.ds(pl.multiple_of(source * width, width), width)
 
     @pl.when(pl.program_id(0) == 0)
     def _():
@@ -59,43 +65,44 @@
         total[...] = jnp.zeros_like(total) if first else before[...]
 
     inter = jnp.zeros((rows, occ), F32)
-    for g in range(groups):
-        span = slice(g * width, (g + 1) * width)
-        high, low = halves(pieces[g].reshape(rows, width))
+    for shift in range(groups):
+        span = columns(shift)
+        high, low = halves(pieces[shift][...].reshape(rows, width))
         high_ref[:, :, span] = high.reshape(count, occ, width)
         low_ref[:, :, span] = low.reshape(count, occ, width)
         wide = dot(high, both[span, :])
         inter += wide[:, :occ] + wide[:, occ:] + dot(low, both[span, :occ])
     coef_high, coef_low = coefficients(inter, count)
     coef = jnp.concatenate([coef_high, coef_low], axis=0)
-    for g in range(groups):
-        span = slice(g * width, (g + 1) * width)
+    for shift in range(groups):
+        span = columns(shift)
         wide = dot(coef, high_ref[:, :, span].reshape(rows, width))
         narrow = dot(coef_high, low_ref[:, :, span].reshape(rows, width))
         total[:, span] += wide[:occ] + wide[occ:] + narrow
 
 
-def first_part(pieces, direction, before, offset, held, count):
-    groups, _, occ, width = pieces.shape
+def first_part(pieces, direction, before, offset, held):
+    groups = len(pieces)
+    count, occ, width = pieces[0].shape
     whole = groups * width
     step = max(s for s in (8, 4, 2, 1) if count % s == 0 and offset % s == 0)
     fixed = pl.BlockSpec((occ, whole), lambda s: (0, 0))
-    in_specs = [pl.BlockSpec((groups, step, occ, width), lambda s: (0, s, 0, 0)), fixed]
-    args = [pieces, direction]
+    in_specs = [pl.BlockSpec((step, occ, width), lambda s: (s, 0, 0))] * groups + [fixed]
+    args = [*pieces, direction]
     aliases = {}
-    first = not isinstance(before, tuple)
+    first = before is None
     if first:
         shape = jax.ShapeDtypeStruct((held, occ, whole), BF16)
     else:
         total, high, low = before
         in_specs += [fixed, pl.BlockSpec(memory_space=pl.ANY), pl.BlockSpec(memory_space=pl.ANY)]
         args += [total, high, low]
-        aliases = {3: 0, 4: 1, 2: 2}
+        aliases = {groups + 2: 0, groups + 3: 1, groups + 1: 2}
         shape = jax.ShapeDtypeStruct(high.shape, BF16)
     start = offset // step
     store = pl.BlockSpec((step, occ, whole), lambda s: (start + s, 0, 0))
     high, low, total = pl.pallas_call(
-        functools.partial(first_kernel, first),
+        functools.partial(first_kernel, first, groups),
         grid=(count // step,),
         in_specs=in_specs,
         out_specs=[store, store, fixed],
@@ -155,12 +162,34 @@
     )(high, low, *state)
 
 
+def add_over(pieces, axes):
+    return jnp.sum(lax.all_to_all(pieces, axes, split_axis=0, concat_axis=0, tiled=True), axis=0)
+
+
+def all_at_once(total, mine, width):
+    occ, whole = total.shape
+    blocks = jnp.swapaxes(total.reshape(occ // mine, mine, whole // width, width), 1, 2)
+    block = add_over(blocks.reshape(-1, mine, width), ("aux", "vir"))
+    blocks = lax.all_gather(block, ("aux", "vir"), axis=0)
+    blocks = blocks.reshape(occ // mine, whole // width, mine, width)
+    return jnp.swapaxes(blocks, 1, 2).reshape(occ, whole)
+
+
+def axis_by_axis(total, mine, width):
+    occ, whole = total.shape
+    rows = add_over(total.reshape(occ // mine, mine, whole), "aux")
+    block = add_over(jnp.swapaxes(rows.reshape(mine, whole // width, width), 0, 1), "vir")
+    rows = jnp.swapaxes(lax.all_gather(block, "vir", axis=0), 0, 1).reshape(mine, whole)
+    return lax.all_gather(rows, "aux", axis=0, tiled=True)
+
+
 def on_device(groups, integrals, occupied_energy, virtual_energy, right_side):
     aux_rows, occ, width = integrals.shape
     whole = groups * width
     unit = aux_rows // groups // sum(PARTS)
-
     mine = occupied_energy.shape[0]
+    me = lax.axis_index("vir")
+
     sent = jnp.concatenate(
         [right_side.T, jnp.broadcast_to(occupied_energy[:, None], (mine, 128))], axis=1
     )
@@ -169,48 +198,60 @@
         [columns[:, :width], virtual_energy[None, :] - columns[:, width : width + 1]]
     )
 
+    def shifted(array, shift):
+        return lax.ppermute(array, "vir", [(z, (z + shift) % groups) for z in range(groups)])
+
     received = []
     low_row = 0
     for k, share in enumerate(PARTS):
         count = share * unit
-        part = integrals[low_row : low_row + groups * count].reshape(groups, count, occ, width)
+        blocks = [
+            lax.dynamic_slice_in_dim(
+                integrals, low_row + lax.rem(me + shift, groups) * count, count, axis=0
+            )
+            for shift in range(groups)
+        ]
         low_row += groups * count
+        if k >= 2:
+            blocks, _ = lax.optimization_barrier((blocks, received[k - 2]))
+        received.append(blocks[:1] + [shifted(blocks[n], n) for n in range(1, groups)])
         if k == CARRIER:
-            extra = jnp.broadcast_to(carried[None], (groups,) + carried.shape)
-            part = jnp.concatenate([part, extra], axis=1)
-        if k >= 2:
-            part, _ = lax.optimization_barrier((part, received[k - 2]))
-        received.append(lax.all_to_all(part, "vir", split_axis=0, concat_axis=0, tiled=True))
-
-    at = PARTS[CARRIER] * unit
-    start, gap = (
-        jnp.moveaxis(received[CARRIER][:, at + n], 0, 1).reshape(occ, whole) for n in range(2)
-    )
+            spread = jnp.zeros((groups,) + carried.shape, F32)
+            for shift in range(groups):
+                piece = carried if shift == 0 else shifted(carried, shift)
+                source = lax.rem(me - shift + groups, groups)
+                spread = lax.dynamic_update_index_in_dim(spread, piece, source, 0)
+    start, gap = (jnp.moveaxis(spread[:, n], 0, 1).reshape(occ, whole) for n in range(2))
+
     held = None
     offset = 0
-    for k, share in enumerate(PARTS):
-        count = share * unit
-        held = first_part(received[k], start, held, offset, aux_rows // groups, count)
-        offset += count
+    for pieces in received:
+        held = first_part(pieces, start, held, offset, aux_rows // groups)
+        offset += pieces[0].shape[0]
     total, high, low = held
 
     direction = residual = start
     iterate = jnp.zeros_like(start)
-    for _ in range(ITERS - 1):
-        summed = lax.psum(total, ("aux", "vir"))
+    for step in range(ITERS - 1):
+        add_up = all_at_once if step == 0 else axis_by_axis
+        summed = add_up(total, mine, width)
         total, direction, residual, iterate = later_apply(
             high, low, summed, gap, direction, residual, iterate
         )
-    summed = lax.psum(total, ("aux", "vir"))
-    iterate, residual, _ = advance(summed, gap, direction, residual, iterate)
 
     def own(array):
-        block = lax.dynamic_slice(
-            array, (lax.axis_index("aux") * mine, lax.axis_index("vir") * width), (mine, width)
-        )
-        return block.T
-
-    return own(iterate), own(residual)
+        return lax.dynamic_slice(array, (lax.axis_index("aux") * mine, me * width), (mine, width))
+
+    product = jnp.full((occ // mine, groups, 1, width), jnp.sum(direction * total), F32)
+    blocks = jnp.swapaxes(total.reshape(occ // mine, mine, groups, width), 1, 2)
+    blocks = jnp.concatenate([blocks, product], axis=2).reshape(-1, mine + 1, width)
+    block = add_over(blocks, ("aux", "vir"))
+    product = block[mine, 0] + jnp.sum(gap * direction * direction)
+    size = jnp.sum(residual * residual) / product
+    image = own(gap) * own(direction) + block[:mine]
+    iterate = own(iterate) + size * own(direction)
+    residual = own(residual) - size * image
+    return iterate.T, residual.T
 
 
 def solution(mesh):

time: 2000 us -> 1750 us (0.88)
  waiting for transfers between devices: 1750 us -> 760 us
  starting transfers between devices: 28.9 us -> 643 us
  blocking collectives: 10.9 us -> 122 us
  local copies, waits for them, and re-layouts: 41.4 us -> 83.2 us
    all_to_all x4 -> x2, waiting for transfers between devices: 1370 us -> 34.4 us  [add_over(): lax.all_to_all(pieces, axes, split_axis=0, concat_axis=0, tiled=True)]
    ppermute x0 -> x18, waiting for transfers between devices: none -> 725 us  [shifted(): lax.ppermute(array, 'vir', [(z, (z + shift) % groups) for z in range(grou...]
    ppermute x0 -> x18, starting transfers between devices: none -> 592 us  [shifted(): lax.ppermute(array, 'vir', [(z, (z + shift) % groups) for z in range(grou...]
    psum x3 -> x0, waiting for transfers between devices: 380 us -> none  [on_device(): summed = lax.psum(total, ('aux', 'vir'))]
    all_gather x0 -> x3, blocking collectives: none -> 88.7 us  [the longest x1 64.5 us: all_at_once(): blocks = lax.all_gather(block, ('aux', 'vir'), axis=0)]
    dynamic_slice x0 -> x2, local copies, waits for them, and re-layouts: none -> 42.5 us  [on_device(): lax.dynamic_slice_in_dim(integrals, low_row + lax.rem(me + shift, groups)...]
    slice x5 -> x2, local copies, waits for them, and re-layouts: 34.5 us -> 1.55 us  [the longest x1 1 us: on_device(): spread[:, n]]
    all_to_all x0 -> x2, blocking collectives: none -> 23.6 us  [add_over(): lax.all_to_all(pieces, axes, split_axis=0, concat_axis=0, tiled=True)]
  transfers between devices with their start and end apart: 7 -> 20, of which waited for: 7 -> 9; matrix products, arithmetic and copies ran while one was open for 2% -> 2% of each run, Pallas kernels for 3% -> 3%
where the time goes in v2:
time: 1750 us
  waiting for transfers between devices  760 us (43%)
  starting transfers between devices  643 us (37%)
  Pallas kernels  136 us (8%)
  blocking collectives  122 us (7%)
  local copies, waits for them, and re-layouts  83.2 us (5%)
    ppermute x18, waiting for transfers between devices, shifted(): lax.ppermute(array, 'vir', [(z, (z + shift) % groups) for z in range(grou...  725 us
    ppermute x18, starting transfers between devices, shifted(): lax.ppermute(array, 'vir', [(z, (z + shift) % groups) for z in range(grou...  592 us
    pallas_call x2, Pallas kernels, later_apply(): pl.pallas_call(later_kernel, grid=(held // step,), in_specs=[block, block...  76.9 us
    all_gather x1, blocking collectives, all_at_once(): blocks = lax.all_gather(block, ('aux', 'vir'), axis=0)  64.5 us
    pallas_call x5, Pallas kernels, first_part(): pl.pallas_call(functools.partial(first_kernel, first, groups), grid=(coun...  59.4 us
    all_to_all x2, starting transfers between devices, add_over(): lax.all_to_all(pieces, axes, split_axis=0, concat_axis=0, tiled=True)  51.4 us
    dynamic_slice x2, local copies, waits for them, and re-layouts, on_device(): lax.dynamic_slice_in_dim(integrals, low_row + lax.rem(me + shift, groups)...  42.5 us
  transfers between devices with their start and end apart: 20, of which 9 were waited for; matrix products, arithmetic and copies ran while one was open for 2% of the time, Pallas kernels for 3%

profile of v2, /device:TPU:1, one launch (start us, length us, event | category | flops | bytes accessed | tf_op | source)
XLA Modules:
  0.0 1750.7 jit_solution(963213847512006878)
XLA Ops:
  0.7 31.7 %constant_dynamic-slice_fusion = (f32[32,128,256]{2,1,0:T(8,128)}, f32[32,128,256]{2,1,0:T(8,128)S(1)}, f32[32,128,256]{2,1,0:T(8,128)}, f32[32,128,256]{2,1,0:T...) fusion(f32[512,128,256]{2,1,0:T(8,128)} %param.4, ...), kind=kLoop, calls=%fused_computation.14 | loop fusion | bytes 100663344 | tf_op jit(solution)/shard_map/dynamic_slice | solution.py:209
  32.4 2.2 collective-permute-start
  34.5 2.3 collective-permute-start.1
  38.4 88.8 %collective-permute-done.refs_1_ = f32[32,128,256]{2,1,0:T(8,128)S(1)} collective-permute-done((f32[32,128,256]{2,1,0:T(8,128)}, f32[32,128,256]{2,1,0:T(8,128)S(1)}, u32[]{:S(2)}, u32[]{:S(2)}) %collective-permute-start) | collective-permute-done | bytes 4194336 | tf_op jit(solution)/shard_map/ppermute | solution.py:202
  128.2 180.2 %collective-permute-done.1.refs_2_ = f32[32,128,256]{2,1,0:T(8,128)S(1)} collective-permute-done((f32[32,128,256]{2,1,0:T(8,128)}, f32[32,128,256]{2,1,0:T(8,128)S(1)}, u32[]{:S(2)}, u32[]{:S(2)}) %collective-permute-start.1) | collective-permute-done | bytes 4194336 | tf_op jit(solution)/shard_map/ppermute | solution.py:202
  308.4 269.9 %collective-permute-start.3 = (f32[32,128,256]{2,1,0:T(8,128)}, f32[32,128,256]{2,1,0:T(8,128)}, u32[]{:S(2)}, u32[]{:S(2)}) collective-permute-start(f32[32,128,256]{2,1,0:T(8,128)} %get-tuple-element.38), channel_id=1, source_target_pairs={{0,1},{1,2},{2,3},{3,0},{4,5},{5,6},{6,7},{7,4},{8,9},{9,10},{10,1... | collective-permute-start | bytes 12582920 | tf_op jit(solution)/shard_map/ppermute | solution.py:202
  578.3 2.0 copy-done.12
  580.3 2.1 collective-permute-start.5
  582.4 10.8 constant_dynamic-slice_fusion.4
  593.2 253.9 %collective-permute-done.13.refs_2_ = f32[32,128,256]{2,1,0:T(8,128)} collective-permute-done((f32[32,128,256]{2,1,0:T(8,128)}, f32[32,128,256]{2,1,0:T(8,128)}, u32[]{:S(2)}, u32[]{:S(2)}) %collective-permute-start.13) | collective-permute-done | bytes 4194336 | tf_op jit(solution)/shard_map/ppermute | solution.py:202
  847.1 90.2 %collective-permute-start.15 = (f32[16,128,256]{2,1,0:T(8,128)S(1)}, f32[16,128,256]{2,1,0:T(8,128)S(1)}, u32[]{:S(2)}, u32[]{:S(2)}) collective-permute-start(f32[16,128,256]{2,1,0:T(8,128)S(1)} %get-tuple-element.46), channel_id=1, source_target_pairs={{0,1},{1,2},{2,3},{3,0},{4,5},{5,6},{6,7},{7,4},{8,9},{9,10},{10,1... | collective-permute-start | bytes 6291464 | tf_op jit(solution)/shard_map/ppermute | solution.py:202
  937.3 10.0 all_gather.18
  947.7 78.6 %collective-permute-start.10 = (f32[2,128,256]{2,1,0:T(8,128)S(1)}, f32[2,128,256]{2,1,0:T(8,128)S(1)}, u32[]{:S(2)}, u32[]{:S(2)}) collective-permute-start(f32[2,128,256]{2,1,0:T(8,128)S(1)} %get-tuple-element.98), channel_id=1, source_target_pairs={{0,2},{1,3},{2,0},{3,1},{4,6},{5,7},{6,4},{7,5},{8,10},{9,11},{10,... | collective-permute-start | bytes 786440 | tf_op jit(solution)/shard_map/ppermute | solution.py:202
  1026.2 56.8 %collective-permute-done.4.refs_2_ = f32[32,128,256]{2,1,0:T(8,128)} collective-permute-done((f32[32,128,256]{2,1,0:T(8,128)}, f32[32,128,256]{2,1,0:T(8,128)}, u32[]{:S(2)}, u32[]{:S(2)}) %collective-permute-start.4) | collective-permute-done | bytes 4194336 | tf_op jit(solution)/shard_map/ppermute | solution.py:202
  1083.0 39.6 %collective-permute-start.11 = (f32[2,128,256]{2,1,0:T(8,128)S(1)}, f32[2,128,256]{2,1,0:T(8,128)S(1)}, u32[]{:S(2)}, u32[]{:S(2)}) collective-permute-start(f32[2,128,256]{2,1,0:T(8,128)S(1)} %get-tuple-element.98), channel_id=1, source_target_pairs={{0,3},{1,0},{2,1},{3,2},{4,7},{5,4},{6,5},{7,6},{8,11},{9,8},{10,9... | collective-permute-start | bytes 786440 | tf_op jit(solution)/shard_map/ppermute | solution.py:202
  1122.6 49.6 %collective-permute-start.16 = (f32[16,128,256]{2,1,0:T(8,128)}, f32[16,128,256]{2,1,0:T(8,128)}, u32[]{:S(2)}, u32[]{:S(2)}) collective-permute-start(f32[16,128,256]{2,1,0:T(8,128)} %get-tuple-element.47), channel_id=1, source_target_pairs={{0,2},{1,3},{2,0},{3,1},{4,6},{5,7},{6,4},{7,5},{8,10},{9,11},{10,... | collective-permute-start | bytes 6291464 | tf_op jit(solution)/shard_map/ppermute | solution.py:202
  1172.2 3.1 collective-permute-start.17
  1175.3 48.1 %collective-permute-done.10 = f32[2,128,256]{2,1,0:T(8,128)S(1)} collective-permute-done((f32[2,128,256]{2,1,0:T(8,128)S(1)}, f32[2,128,256]{2,1,0:T(8,128)S(1)}, u32[]{:S(2)}, u32[]{:S(2)}) %collective-permute-start.10) | collective-permute-done | bytes 262176 | tf_op jit(solution)/shard_map/ppermute | solution.py:202
  1223.4 48.0 %collective-permute-start.6 = (f32[16,128,256]{2,1,0:T(8,128)}, f32[16,128,256]{2,1,0:T(8,128)}, u32[]{:S(2)}, u32[]{:S(2)}) collective-permute-start(f32[16,128,256]{2,1,0:T(8,128)} %get-tuple-element.42), channel_id=1, source_target_pairs={{0,1},{1,2},{2,3},{3,0},{4,5},{5,6},{6,7},{7,4},{8,9},{9,10},{10,1... | collective-permute-start | bytes 6291464 | tf_op jit(solution)/shard_map/ppermute | solution.py:202
  1271.4 3.1 collective-permute-start.7
  1276.7 3.8 dynamic_update_slice.13
  1280.5 1.9 copy.40
  1282.5 1.9 copy.41
  1285.6 5.3 dynamic_update_slice.14
  1290.9 5.3 dynamic_update_slice.15
  1296.3 3.8 dynamic_update_slice.16
  1301.2 2.2 copy-done
  1303.3 14.0 shard_map.59
  1317.3 2.2 copy-done.2
  1319.5 14.1 shard_map.60
  1333.7 14.2 shard_map.61
  1347.9 16.1 collective-permute-done.17.refs_3_
  1363.9 8.4 shard_map.62
  1372.3 81.5 %collective-permute-done.7.refs_2_ = f32[16,128,256]{2,1,0:T(8,128)} collective-permute-done((f32[16,128,256]{2,1,0:T(8,128)}, f32[16,128,256]{2,1,0:T(8,128)}, u32[]{:S(2)}, u32[]{:S(2)}) %collective-permute-start.7) | collective-permute-done | bytes 2097184 | tf_op jit(solution)/shard_map/ppermute | solution.py:202
  1453.9 8.7 shard_map.63
  1463.7 49.1 %all-to-all-start = ((f32[32,16,256]{2,1,0:T(8,128)}), f32[32,16,256]{2,1,0:T(8,128)S(1)}, u32[]{:S(2)}, u32[]{:S(2)}) async-start(f32[32,16,256]{2,1,0:T(8,128)} %bitcast.9), calls=%async_computation | async-start | bytes 1048576 | tf_op jit(solution)/shard_map/all_to_all | solution.py:166
  1513.9 14.2 all-to-all-done
  1528.1 64.5 %all-gather = f32[512,256]{1,0:T(8,128)S(1)} all-gather(f32[16,256]{1,0:T(8,128)S(1)} %reduce_sum.63), channel_id=2, replica_groups=mesh['aux'=8,'vir'=4] {'aux','vir'}, dimensions={0}, use_global_device_ids=true | all-gather | bytes 540672 | tf_op jit(solution)/shard_map/all_gather | solution.py:173
  1593.1 38.4 %shard_map.64 = (f32[128,1024]{1,0:T(8,128)S(1)}, f32[128,1024]{1,0:T(8,128)S(1)}, f32[128,1024]{1,0:T(8,128)S(1)}, f32[128,1024]{1,0:T(8,128)S(1)}) custom-call(bf16[128,128,1024]{2,1,0:T(8,128)(2,1)} %get-tuple-element.61.high_ref, bf16[128,128,1024]{2,1,0:T(8,128)(2,1)} %get-tuple-element.62.low_ref, f32[128,1024]{1,0:T(8,128)S(1)} %bitcast.53, ...), custom_call_target="tpu_custom_call" | custom-call | tf_op jit(solution)/shard_map/pallas_call | solution.py:154
  1632.4 16.5 all_to_all.20
  1649.0 7.1 all_to_all.21
  1656.1 10.6 all-gather.1
  1666.7 13.7 all_gather.23.summed
  1681.4 38.4 %shard_map.65 = (f32[128,1024]{1,0:T(8,128)S(1)}, f32[128,1024]{1,0:T(8,128)S(1)}, f32[128,1024]{1,0:T(8,128)S(1)}, f32[128,1024]{1,0:T(8,128)S(1)}) custom-call(bf16[128,128,1024]{2,1,0:T(8,128)(2,1)} %get-tuple-element.61.high_ref, bf16[128,128,1024]{2,1,0:T(8,128)(2,1)} %get-tuple-element.62.low_ref, f32[128,1024]{1,0:T(8,128)S(1)} %all_gather.23.summed, ...), custom_call_target="tpu_custom_call" | custom-call | tf_op jit(solution)/shard_map/pallas_call | solution.py:154
  1721.8 1.6 concatenate.7.clone
  1723.5 2.4 all-to-all-start.3
  1726.6 20.2 %all-to-all-done.3 = f32[32,17,256]{2,1,0:T(8,128)S(1)} async-done(((f32[32,17,256]{2,1,0:T(8,128)}), f32[32,17,256]{2,1,0:T(8,128)S(1)}, u32[]{:S(2)}, u32[]{:S(2)}) %all-to-all-start.3) | async-done | bytes 557088 | tf_op jit(solution)/shard_map/all_to_all | solution.py:166
  1749.3 1.3 fusion.3
  (82 shorter events, 15.6 us)
Async XLA Ops:
  32.4 94.8 %collective-permute-start = (f32[32,128,256]{2,1,0:T(8,128)}, f32[32,128,256]{2,1,0:T(8,128)S(1)}, u32[]{:S(2)}, u32[]{:S(2)}) collective-permute-start(f32[32,128,256]{2,1,0:T(8,128)} %get-tuple-element.79), channel_id=1, source_target_pairs={{0,1},{1,2},{2,3},{3,0},{4,5},{5,6},{6,7},{7,4},{8,9},{9,10},{10,1... | collective-permute-start | bytes 12582920 | tf_op jit(solution)/shard_map/ppermute | solution.py:202
  34.5 273.9 %collective-permute-start.1 = (f32[32,128,256]{2,1,0:T(8,128)}, f32[32,128,256]{2,1,0:T(8,128)S(1)}, u32[]{:S(2)}, u32[]{:S(2)}) collective-permute-start(f32[32,128,256]{2,1,0:T(8,128)} %get-tuple-element.78), channel_id=1, source_target_pairs={{0,2},{1,3},{2,0},{3,1},{4,6},{5,7},{6,4},{7,5},{8,10},{9,11},{10,... | collective-permute-start | bytes 12582920 | tf_op jit(solution)/shard_map/ppermute | solution.py:202
  36.8 271.5 %collective-permute-start.2 = (f32[32,128,256]{2,1,0:T(8,128)}, f32[32,128,256]{2,1,0:T(8,128)S(1)}, u32[]{:S(2)}, u32[]{:S(2)}) collective-permute-start(f32[32,128,256]{2,1,0:T(8,128)} %get-tuple-element.77), channel_id=1, source_target_pairs={{0,3},{1,0},{2,1},{3,2},{4,7},{5,4},{6,5},{7,6},{8,11},{9,8},{10,9... | collective-permute-start | bytes 12582920 | tf_op jit(solution)/shard_map/ppermute | solution.py:202
  37.9 540.4 %collective-permute-start.12 = (f32[32,128,256]{2,1,0:T(8,128)S(1)}, f32[32,128,256]{2,1,0:T(8,128)S(1)}, u32[]{:S(2)}, u32[]{:S(2)}) collective-permute-start(f32[32,128,256]{2,1,0:T(8,128)S(1)} %get-tuple-element.75), channel_id=1, source_target_pairs={{0,1},{1,2},{2,3},{3,0},{4,5},{5,6},{6,7},{7,4},{8,9},{9,10},{10,1... | collective-permute-start | bytes 12582920 | tf_op jit(solution)/shard_map/ppermute | solution.py:202
  38.3 808.8 %collective-permute-start.13 = (f32[32,128,256]{2,1,0:T(8,128)}, f32[32,128,256]{2,1,0:T(8,128)}, u32[]{:S(2)}, u32[]{:S(2)}) collective-permute-start(f32[32,128,256]{2,1,0:T(8,128)} %get-tuple-element.85), channel_id=1, source_target_pairs={{0,2},{1,3},{2,0},{3,1},{4,6},{5,7},{6,4},{7,5},{8,10},{9,11},{10,... | collective-permute-start | bytes 12582920 | tf_op jit(solution)/shard_map/ppermute | solution.py:202
  127.2 451.1 %copy-start.9 = (f32[32,128,256]{2,1,0:T(8,128)}, f32[32,128,256]{2,1,0:T(8,128)S(1)}, u32[]{:S(2)}) copy-start(f32[32,128,256]{2,1,0:T(8,128)S(1)} %collective-permute-done.refs_1_) | copy-start | bytes 12582916
  127.2 720.0 %collective-permute-start.14 = (f32[32,128,256]{2,1,0:T(8,128)}, f32[32,128,256]{2,1,0:T(8,128)}, u32[]{:S(2)}, u32[]{:S(2)}) collective-permute-start(f32[32,128,256]{2,1,0:T(8,128)} %get-tuple-element.74), channel_id=1, source_target_pairs={{0,3},{1,0},{2,1},{3,2},{4,7},{5,4},{6,5},{7,6},{8,11},{9,8},{10,9... | collective-permute-start | bytes 12582920 | tf_op jit(solution)/shard_map/ppermute | solution.py:202
  308.4 269.9 %copy-start.10 = (f32[32,128,256]{2,1,0:T(8,128)}, f32[32,128,256]{2,1,0:T(8,128)S(1)}, u32[]{:S(2)}) copy-start(f32[32,128,256]{2,1,0:T(8,128)S(1)} %collective-permute-done.1.refs_2_) | copy-start | bytes 12582916
  308.4 269.9 %copy-start.11 = (f32[32,128,256]{2,1,0:T(8,128)}, f32[32,128,256]{2,1,0:T(8,128)S(1)}, u32[]{:S(2)}) copy-start(f32[32,128,256]{2,1,0:T(8,128)S(1)} %collective-permute-done.2.refs_3_) | copy-start | bytes 12582916
  308.4 639.3 %collective-permute-start.3 = (f32[32,128,256]{2,1,0:T(8,128)}, f32[32,128,256]{2,1,0:T(8,128)}, u32[]{:S(2)}, u32[]{:S(2)}) collective-permute-start(f32[32,128,256]{2,1,0:T(8,128)} %get-tuple-element.38), channel_id=1, source_target_pairs={{0,1},{1,2},{2,3},{3,0},{4,5},{5,6},{6,7},{7,4},{8,9},{9,10},{10,1... | collective-permute-start | bytes 12582920 | tf_op jit(solution)/shard_map/ppermute | solution.py:202
  578.3 504.8 %collective-permute-start.4 = (f32[32,128,256]{2,1,0:T(8,128)}, f32[32,128,256]{2,1,0:T(8,128)}, u32[]{:S(2)}, u32[]{:S(2)}) collective-permute-start(f32[32,128,256]{2,1,0:T(8,128)} %get-tuple-element.39), channel_id=1, source_target_pairs={{0,2},{1,3},{2,0},{3,1},{4,6},{5,7},{6,4},{7,5},{8,10},{9,11},{10,... | collective-permute-start | bytes 12582920 | tf_op jit(solution)/shard_map/ppermute | solution.py:202
  578.3 2.0 copy-start.12
  580.3 542.3 %collective-permute-start.5 = (f32[32,128,256]{2,1,0:T(8,128)}, f32[32,128,256]{2,1,0:T(8,128)}, u32[]{:S(2)}, u32[]{:S(2)}) collective-permute-start(f32[32,128,256]{2,1,0:T(8,128)} %get-tuple-element.40), channel_id=1, source_target_pairs={{0,3},{1,0},{2,1},{3,2},{4,7},{5,4},{6,5},{7,6},{8,11},{9,8},{10,9... | collective-permute-start | bytes 12582920 | tf_op jit(solution)/shard_map/ppermute | solution.py:202
  582.4 354.9 %copy-start.18 = (f32[16]{0:T(128)S(1)}, f32[16]{0:T(128)}, u32[]{:S(2)}) copy-start(f32[16]{0:T(128)} %param.5) | copy-start | bytes 196
  582.4 355.0 %copy-start.16 = (f32[256,16]{0,1:T(8,128)S(1)}, f32[256,16]{0,1:T(8,128)}, u32[]{:S(2)}) copy-start(f32[256,16]{0,1:T(8,128)} %param.7) | copy-start | bytes 49156
  582.4 365.1 %copy-start.17 = (f32[256]{0:T(256)S(1)}, f32[256]{0:T(256)}, u32[]{:S(2)}) copy-start(f32[256]{0:T(256)} %param.6) | copy-start | bytes 3076
  847.1 427.4 %collective-permute-start.15 = (f32[16,128,256]{2,1,0:T(8,128)S(1)}, f32[16,128,256]{2,1,0:T(8,128)S(1)}, u32[]{:S(2)}, u32[]{:S(2)}) collective-permute-start(f32[16,128,256]{2,1,0:T(8,128)S(1)} %get-tuple-element.46), channel_id=1, source_target_pairs={{0,1},{1,2},{2,3},{3,0},{4,5},{5,6},{6,7},{7,4},{8,9},{9,10},{10,1... | collective-permute-start | bytes 6291464 | tf_op jit(solution)/shard_map/ppermute | solution.py:202
  947.6 224.6 %collective-permute-start.9 = (f32[2,128,256]{2,1,0:T(8,128)S(1)}, f32[2,128,256]{2,1,0:T(8,128)S(1)}, u32[]{:S(2)}, u32[]{:S(2)}) collective-permute-start(f32[2,128,256]{2,1,0:T(8,128)S(1)} %get-tuple-element.98), channel_id=1, source_target_pairs={{0,1},{1,2},{2,3},{3,0},{4,5},{5,6},{6,7},{7,4},{8,9},{9,10},{10,1... | collective-permute-start | bytes 786440 | tf_op jit(solution)/shard_map/ppermute | solution.py:202
  947.7 275.7 %collective-permute-start.10 = (f32[2,128,256]{2,1,0:T(8,128)S(1)}, f32[2,128,256]{2,1,0:T(8,128)S(1)}, u32[]{:S(2)}, u32[]{:S(2)}) collective-permute-start(f32[2,128,256]{2,1,0:T(8,128)S(1)} %get-tuple-element.98), channel_id=1, source_target_pairs={{0,2},{1,3},{2,0},{3,1},{4,6},{5,7},{6,4},{7,5},{8,10},{9,11},{10,... | collective-permute-start | bytes 786440 | tf_op jit(solution)/shard_map/ppermute | solution.py:202
  1083.0 188.3 %collective-permute-start.11 = (f32[2,128,256]{2,1,0:T(8,128)S(1)}, f32[2,128,256]{2,1,0:T(8,128)S(1)}, u32[]{:S(2)}, u32[]{:S(2)}) collective-permute-start(f32[2,128,256]{2,1,0:T(8,128)S(1)} %get-tuple-element.98), channel_id=1, source_target_pairs={{0,3},{1,0},{2,1},{3,2},{4,7},{5,4},{6,5},{7,6},{8,11},{9,8},{10,9... | collective-permute-start | bytes 786440 | tf_op jit(solution)/shard_map/ppermute | solution.py:202
  1122.6 225.2 %collective-permute-start.16 = (f32[16,128,256]{2,1,0:T(8,128)}, f32[16,128,256]{2,1,0:T(8,128)}, u32[]{:S(2)}, u32[]{:S(2)}) collective-permute-start(f32[16,128,256]{2,1,0:T(8,128)} %get-tuple-element.47), channel_id=1, source_target_pairs={{0,2},{1,3},{2,0},{3,1},{4,6},{5,7},{6,4},{7,5},{8,10},{9,11},{10,... | collective-permute-start | bytes 6291464 | tf_op jit(solution)/shard_map/ppermute | solution.py:202
  1172.2 102.3 %copy-start.13 = (f32[2,128,256]{2,1,0:T(8,128)}, f32[2,128,256]{2,1,0:T(8,128)S(1)}, u32[]{:S(2)}) copy-start(f32[2,128,256]{2,1,0:T(8,128)S(1)} %collective-permute-done.9) | copy-start | bytes 786436
  1172.2 191.7 %collective-permute-start.17 = (f32[16,128,256]{2,1,0:T(8,128)}, f32[16,128,256]{2,1,0:T(8,128)}, u32[]{:S(2)}, u32[]{:S(2)}) collective-permute-start(f32[16,128,256]{2,1,0:T(8,128)} %get-tuple-element.48), channel_id=1, source_target_pairs={{0,3},{1,0},{2,1},{3,2},{4,7},{5,4},{6,5},{7,6},{8,11},{9,8},{10,9... | collective-permute-start | bytes 6291464 | tf_op jit(solution)/shard_map/ppermute | solution.py:202
  1223.4 51.1 %copy-start.14 = (f32[2,128,256]{2,1,0:T(8,128)}, f32[2,128,256]{2,1,0:T(8,128)S(1)}, u32[]{:S(2)}) copy-start(f32[2,128,256]{2,1,0:T(8,128)S(1)} %collective-permute-done.10) | copy-start | bytes 786436
  1223.4 149.0 %collective-permute-start.6 = (f32[16,128,256]{2,1,0:T(8,128)}, f32[16,128,256]{2,1,0:T(8,128)}, u32[]{:S(2)}, u32[]{:S(2)}) collective-permute-start(f32[16,128,256]{2,1,0:T(8,128)} %get-tuple-element.42), channel_id=1, source_target_pairs={{0,1},{1,2},{2,3},{3,0},{4,5},{5,6},{6,7},{7,4},{8,9},{9,10},{10,1... | collective-permute-start | bytes 6291464 | tf_op jit(solution)/shard_map/ppermute | solution.py:202
  1271.4 3.1 copy-start.15
  1271.4 182.5 %collective-permute-start.7 = (f32[16,128,256]{2,1,0:T(8,128)}, f32[16,128,256]{2,1,0:T(8,128)}, u32[]{:S(2)}, u32[]{:S(2)}) collective-permute-start(f32[16,128,256]{2,1,0:T(8,128)} %get-tuple-element.43), channel_id=1, source_target_pairs={{0,2},{1,3},{2,0},{3,1},{4,6},{5,7},{6,4},{7,5},{8,10},{9,11},{10,... | collective-permute-start | bytes 6291464 | tf_op jit(solution)/shard_map/ppermute | solution.py:202
  1274.5 1.3 copy-start.4
  1275.8 178.0 %collective-permute-start.8 = (f32[16,128,256]{2,1,0:T(8,128)}, f32[16,128,256]{2,1,0:T(8,128)}, u32[]{:S(2)}, u32[]{:S(2)}) collective-permute-start(f32[16,128,256]{2,1,0:T(8,128)} %get-tuple-element.44), channel_id=1, source_target_pairs={{0,3},{1,0},{2,1},{3,2},{4,7},{5,4},{6,5},{7,6},{8,11},{9,8},{10,9... | collective-permute-start | bytes 6291464 | tf_op jit(solution)/shard_map/ppermute | solution.py:202
  1301.1 2.2 copy-start
  1317.3 2.2 copy-start.2
  1319.5 14.1 copy-start.1
  1333.6 30.3 %copy-start.3 = (f32[16,128,256]{2,1,0:T(8,128)S(1)}, f32[16,128,256]{2,1,0:T(8,128)}, u32[]{:S(2)}) copy-start(f32[16,128,256]{2,1,0:T(8,128)} %get-tuple-element.45.refs_0_) | copy-start | bytes 6291460
  1333.7 30.3 %copy-start.5 = (f32[16,128,256]{2,1,0:T(8,128)S(1)}, f32[16,128,256]{2,1,0:T(8,128)}, u32[]{:S(2)}) copy-start(f32[16,128,256]{2,1,0:T(8,128)} %copy-done.4) | copy-start | bytes 6291460
  1463.7 64.4 %all-to-all-start = ((f32[32,16,256]{2,1,0:T(8,128)}), f32[32,16,256]{2,1,0:T(8,128)S(1)}, u32[]{:S(2)}, u32[]{:S(2)}) async-start(f32[32,16,256]{2,1,0:T(8,128)} %bitcast.9), calls=%async_computation | async-start | bytes 1048576 | tf_op jit(solution)/shard_map/all_to_all | solution.py:166
  1631.5 0.8 copy-start.6
  1680.3 1.0 copy-start.7
  1719.8 0.8 copy-start.8
  1723.5 23.3 %all-to-all-start.3 = ((f32[32,17,256]{2,1,0:T(8,128)}), f32[32,17,256]{2,1,0:T(8,128)S(1)}, u32[]{:S(2)}, u32[]{:S(2)}) async-start(f32[32,17,256]{2,1,0:T(8,128)} %bitcast.19), calls=%async_computation.3 | async-start | bytes 1572864 | tf_op jit(solution)/shard_map/all_to_all | solution.py:166

commit v3 on v2

--- a/solution.py
+++ b/solution.py
@@ -8,7 +8,7 @@
 from jax.sharding import PartitionSpec as P
 
 ITERS = 3
-PARTS = (4, 4, 4, 2, 2)
+PARTS = (1, 4, 4, 4, 2, 1)
 CARRIER = 1
 BF16 = jnp.bfloat16
 F32 = jnp.float32
@@ -124,7 +124,6 @@
 def later_kernel(high_ref, low_ref, summed, gap, direction, residual, iterate,
                  total, new_direction, new_residual, new_iterate, both):
     count, occ, whole = high_ref.shape
-    rows = count * occ
 
     @pl.when(pl.program_id(0) == 0)
     def _():
@@ -136,19 +135,23 @@
         load_direction(along, both)
         total[...] = jnp.zeros_like(total)
 
-    high = high_ref[...].reshape(rows, whole)
-    low = low_ref[...].reshape(rows, whole)
-    wide = dot(high, both[...])
-    inter = wide[:, :occ] + wide[:, occ:] + dot(low, both[:, :occ])
-    coef_high, coef_low = coefficients(inter, count)
-    coef = jnp.concatenate([coef_high, coef_low], axis=0)
-    wide = dot(coef, high)
-    total[...] += wide[:occ] + wide[occ:] + dot(coef_high, low)
+    spans = [slice(n * (count // 2), (n + 1) * (count // 2)) for n in range(2)] if count > 1 else [slice(0, 1)]
+    inters = []
+    for span in spans:
+        wide = dot(high_ref[span].reshape(-1, whole), both[...])
+        narrow = dot(low_ref[span].reshape(-1, whole), both[:, :occ])
+        inters.append(wide[:, :occ] + wide[:, occ:] + narrow)
+    for span, inter in zip(spans, inters):
+        coef_high, coef_low = coefficients(inter, span.stop - span.start)
+        coef = jnp.concatenate([coef_high, coef_low], axis=0)
+        wide = dot(coef, high_ref[span].reshape(-1, whole))
+        narrow = dot(coef_high, low_ref[span].reshape(-1, whole))
+        total[...] += wide[:occ] + wide[occ:] + narrow
 
 
 def later_apply(high, low, *state):
     held, occ, whole = high.shape
-    step = max(s for s in (8, 4, 2, 1) if held % s == 0)
+    step = max(s for s in (16, 8, 4, 2, 1) if held % s == 0)
     fixed = pl.BlockSpec((occ, whole), lambda s: (0, 0))
     block = pl.BlockSpec((step, occ, whole), lambda s: (s, 0, 0))
     return pl.pallas_call(
@@ -166,20 +169,10 @@
     return jnp.sum(lax.all_to_all(pieces, axes, split_axis=0, concat_axis=0, tiled=True), axis=0)
 
 
-def all_at_once(total, mine, width):
-    occ, whole = total.shape
-    blocks = jnp.swapaxes(total.reshape(occ // mine, mine, whole // width, width), 1, 2)
-    block = add_over(blocks.reshape(-1, mine, width), ("aux", "vir"))
-    blocks = lax.all_gather(block, ("aux", "vir"), axis=0)
-    blocks = blocks.reshape(occ // mine, whole // width, mine, width)
-    return jnp.swapaxes(blocks, 1, 2).reshape(occ, whole)
-
-
-def axis_by_axis(total, mine, width):
+def add_up(total, mine, groups):
     occ, whole = total.shape
     rows = add_over(total.reshape(occ // mine, mine, whole), "aux")
-    block = add_over(jnp.swapaxes(rows.reshape(mine, whole // width, width), 0, 1), "vir")
-    rows = jnp.swapaxes(lax.all_gather(block, "vir", axis=0), 0, 1).reshape(mine, whole)
+    rows = add_over(jnp.broadcast_to(rows[None], (groups, mine, whole)), "vir")
     return lax.all_gather(rows, "aux", axis=0, tiled=True)
 
 
@@ -212,7 +205,9 @@
             for shift in range(groups)
         ]
         low_row += groups * count
-        if k >= 2:
+        if k == 0:
+            blocks, integrals = lax.optimization_barrier((blocks, integrals))
+        elif k >= 2:
             blocks, _ = lax.optimization_barrier((blocks, received[k - 2]))
         received.append(blocks[:1] + [shifted(blocks[n], n) for n in range(1, groups)])
         if k == CARRIER:
@@ -232,9 +227,8 @@
 
     direction = residual = start
     iterate = jnp.zeros_like(start)
-    for step in range(ITERS - 1):
-        add_up = all_at_once if step == 0 else axis_by_axis
-        summed = add_up(total, mine, width)
+    for _ in range(ITERS - 1):
+        summed = add_up(total, mine, groups)
         total, direction, residual, iterate = later_apply(
             high, low, summed, gap, direction, residual, iterate
         )

time: 1750 us -> 1700 us (0.971)
  waiting for transfers between devices: 760 us -> 619 us
  starting transfers between devices: 643 us -> 766 us
  blocking collectives: 122 us -> 69.4 us
    ppermute x18 -> x21, starting transfers between devices: 592 us -> 760 us  [shifted(): lax.ppermute(array, 'vir', [(z, (z + shift) % groups) for z in range(grou...]
    ppermute x18 -> x21, waiting for transfers between devices: 725 us -> 593 us  [shifted(): lax.ppermute(array, 'vir', [(z, (z + shift) % groups) for z in range(grou...]
    all_gather x3 -> x2, blocking collectives: 88.7 us -> 26.7 us  [add_up(): return lax.all_gather(rows, 'aux', axis=0, tiled=True)]
    all_to_all x2, starting transfers between devices: 51.4 us -> 5.99 us  [add_over(): lax.all_to_all(pieces, axes, split_axis=0, concat_axis=0, tiled=True)]
    dynamic_slice x2 -> x4, local copies, waits for them, and re-layouts: 42.5 us -> 46.2 us  [on_device(): lax.dynamic_slice_in_dim(integrals, low_row + lax.rem(me + shift, groups)...]
    pallas_call x5 -> x6, Pallas kernels: 59.4 us -> 61.7 us  [first_part(): pl.pallas_call(functools.partial(first_kernel, first, groups), grid=(coun...]
  transfers between devices with their start and end apart: 20 -> 23, of which waited for: 9 -> 7; matrix products, arithmetic and copies ran while one was open for 2% -> 3% of each run, Pallas kernels for 3% -> 3%
where the time goes in v3:
time: 1700 us; the launch traced here: 1690 us
  starting transfers between devices  766 us (45%)
  waiting for transfers between devices  619 us (36%)
  Pallas kernels  137 us (8%)
  local copies, waits for them, and re-layouts  96.3 us (6%)
  blocking collectives  69.4 us (4%)
    ppermute x21, starting transfers between devices, shifted(): lax.ppermute(array, 'vir', [(z, (z + shift) % groups) for z in range(grou...  760 us
    ppermute x21, waiting for transfers between devices, shifted(): lax.ppermute(array, 'vir', [(z, (z + shift) % groups) for z in range(grou...  593 us
    pallas_call x2, Pallas kernels, later_apply(): pl.pallas_call(later_kernel, grid=(held // step,), in_specs=[block, block...  75.1 us
    pallas_call x6, Pallas kernels, first_part(): pl.pallas_call(functools.partial(first_kernel, first, groups), grid=(coun...  61.7 us
    dynamic_slice x4, local copies, waits for them, and re-layouts, on_device(): lax.dynamic_slice_in_dim(integrals, low_row + lax.rem(me + shift, groups)...  46.2 us
  transfers between devices with their start and end apart: 23, of which 7 were waited for; matrix products, arithmetic and copies ran while one was open for 3% of the time, Pallas kernels for 3%

profile of v3, /device:TPU:1, one launch (start us, length us, event | category | flops | bytes accessed | tf_op | source)
XLA Modules:
  0.0 1693.7 jit_solution(16534995613232791561)
XLA Ops:
  0.7 3.9 constant_dynamic-slice_fusion.20
  4.6 31.7 %constant_dynamic-slice_fusion = (f32[32,128,256]{2,1,0:T(8,128)}, f32[32,128,256]{2,1,0:T(8,128)}, f32[32,128,256]{2,1,0:T(8,128)S(1)}, f32[32,128,256]{2,1,0:T...) fusion(f32[512,128,256]{2,1,0:T(8,128)} %param.4, ...), kind=kLoop, calls=%fused_computation.14 | loop fusion | bytes 100663344 | tf_op jit(solution)/shard_map/dynamic_slice | solution.py:202
  36.3 2.2 collective-permute-start
  40.9 2.3 collective-permute-start.14
  43.2 110.4 %collective-permute-done.12.refs_1_ = f32[8,128,256]{2,1,0:T(8,128)S(1)} collective-permute-done((f32[8,128,256]{2,1,0:T(8,128)}, f32[8,128,256]{2,1,0:T(8,128)S(1)}, u32[]{:S(2)}, u32[]{:S(2)}) %collective-permute-start.12) | collective-permute-done | bytes 1048608 | tf_op jit(solution)/shard_map/ppermute | solution.py:195
  155.7 44.3 %collective-permute-done.13.refs_2_ = f32[8,128,256]{2,1,0:T(8,128)S(1)} collective-permute-done((f32[8,128,256]{2,1,0:T(8,128)S(1)}, f32[8,128,256]{2,1,0:T(8,128)S(1)}, u32[]{:S(2)}, u32[]{:S(2)}) %collective-permute-start.13) | collective-permute-done | bytes 1048608 | tf_op jit(solution)/shard_map/ppermute | solution.py:195
  202.0 198.9 %collective-permute-start.15 = (f32[32,128,256]{2,1,0:T(8,128)S(1)}, f32[32,128,256]{2,1,0:T(8,128)S(1)}, u32[]{:S(2)}, u32[]{:S(2)}) collective-permute-start(f32[32,128,256]{2,1,0:T(8,128)S(1)} %get-tuple-element.63), channel_id=1, source_target_pairs={{0,1},{1,2},{2,3},{3,0},{4,5},{5,6},{6,7},{7,4},{8,9},{9,10},{10,1... | collective-permute-start | bytes 12582920 | tf_op jit(solution)/shard_map/ppermute | solution.py:195
  400.9 3.1 collective-permute-start.16
  404.0 267.4 %collective-permute-start.3 = (f32[32,128,256]{2,1,0:T(8,128)}, f32[32,128,256]{2,1,0:T(8,128)}, u32[]{:S(2)}, u32[]{:S(2)}) collective-permute-start(f32[32,128,256]{2,1,0:T(8,128)} %get-tuple-element.51), channel_id=1, source_target_pairs={{0,1},{1,2},{2,3},{3,0},{4,5},{5,6},{6,7},{7,4},{8,9},{9,10},{10,1... | collective-permute-start | bytes 12582920 | tf_op jit(solution)/shard_map/ppermute | solution.py:195
  671.5 1.9 copy-done.17
  673.4 2.1 collective-permute-start.5
  675.5 6.4 constant_dynamic-slice_fusion.4
  681.9 259.1 %collective-permute-done.16.refs_2_ = f32[32,128,256]{2,1,0:T(8,128)} collective-permute-done((f32[32,128,256]{2,1,0:T(8,128)}, f32[32,128,256]{2,1,0:T(8,128)}, u32[]{:S(2)}, u32[]{:S(2)}) %collective-permute-start.16) | collective-permute-done | bytes 4194336 | tf_op jit(solution)/shard_map/ppermute | solution.py:195
  941.0 90.2 %collective-permute-start.18 = (f32[16,128,256]{2,1,0:T(8,128)}, f32[16,128,256]{2,1,0:T(8,128)}, u32[]{:S(2)}, u32[]{:S(2)}) collective-permute-start(f32[16,128,256]{2,1,0:T(8,128)} %get-tuple-element.67), channel_id=1, source_target_pairs={{0,1},{1,2},{2,3},{3,0},{4,5},{5,6},{6,7},{7,4},{8,9},{9,10},{10,1... | collective-permute-start | bytes 6291464 | tf_op jit(solution)/shard_map/ppermute | solution.py:195
  1031.2 10.0 all_gather.9
  1041.5 39.8 %collective-permute-done.9 = f32[2,128,256]{2,1,0:T(8,128)S(1)} collective-permute-done((f32[2,128,256]{2,1,0:T(8,128)S(1)}, f32[2,128,256]{2,1,0:T(8,128)S(1)}, u32[]{:S(2)}, u32[]{:S(2)}) %collective-permute-start.9) | collective-permute-done | bytes 262176 | tf_op jit(solution)/shard_map/ppermute | solution.py:195
  1081.4 179.0 %collective-permute-start.19 = (f32[16,128,256]{2,1,0:T(8,128)}, f32[16,128,256]{2,1,0:T(8,128)}, u32[]{:S(2)}, u32[]{:S(2)}) collective-permute-start(f32[16,128,256]{2,1,0:T(8,128)} %get-tuple-element.68), channel_id=1, source_target_pairs={{0,2},{1,3},{2,0},{3,1},{4,6},{5,7},{6,4},{7,5},{8,10},{9,11},{10,... | collective-permute-start | bytes 6291464 | tf_op jit(solution)/shard_map/ppermute | solution.py:195
  1260.6 3.4 collective-permute-start.11
  1263.9 4.2 constant_dynamic-slice_fusion.16
  1268.2 139.5 %collective-permute-done.10 = f32[2,128,256]{2,1,0:T(8,128)S(1)} collective-permute-done((f32[2,128,256]{2,1,0:T(8,128)S(1)}, f32[2,128,256]{2,1,0:T(8,128)S(1)}, u32[]{:S(2)}, u32[]{:S(2)}) %collective-permute-start.10) | collective-permute-done | bytes 262176 | tf_op jit(solution)/shard_map/ppermute | solution.py:195
  1407.7 1.9 collective-permute-start.6
  1409.6 3.1 collective-permute-start.7
  1412.7 3.0 collective-permute-start.8
  1417.1 6.7 dynamic_update_slice.13
  1425.6 6.7 dynamic_update_slice.14
  1432.3 6.7 dynamic_update_slice.15
  1439.0 6.7 dynamic_update_slice.16
  1445.7 1.5 fusion.5
  1452.3 4.3 shard_map.59
  1456.6 14.5 shard_map.60
  1471.1 2.2 copy-done.1
  1473.3 14.1 shard_map.61
  1487.4 14.3 shard_map.62
  1501.7 8.8 shard_map.63
  1510.5 5.6 shard_map.64
  1516.2 13.1 all_to_all.25
  1530.1 3.4 all-to-all-start.1
  1533.6 5.8 all-to-all-done.1
  1539.4 13.5 all_gather.10.summed
  1552.9 37.6 %shard_map.65 = (f32[128,1024]{1,0:T(8,128)S(1)}, f32[128,1024]{1,0:T(8,128)S(1)}, f32[128,1024]{1,0:T(8,128)S(1)}, f32[128,1024]{1,0:T(8,128)S(1)}) custom-call(bf16[128,128,1024]{2,1,0:T(8,128)(2,1)} %get-tuple-element.85.high_ref, bf16[128,128,1024]{2,1,0:T(8,128)(2,1)} %get-tuple-element.86.low_ref, f32[128,1024]{1,0:T(8,128)S(1)} %all_gather.10.summed, ...), custom_call_target="tpu_custom_call" | custom-call | tf_op jit(solution)/shard_map/pallas_call | solution.py:157
  1591.4 11.1 all_to_all.26
  1602.6 8.4 all_to_all.27
  1611.0 13.3 all_gather.11.summed
  1625.3 37.4 %shard_map.66 = (f32[128,1024]{1,0:T(8,128)S(1)}, f32[128,1024]{1,0:T(8,128)S(1)}, f32[128,1024]{1,0:T(8,128)S(1)}, f32[128,1024]{1,0:T(8,128)S(1)}) custom-call(bf16[128,128,1024]{2,1,0:T(8,128)(2,1)} %get-tuple-element.85.high_ref, bf16[128,128,1024]{2,1,0:T(8,128)(2,1)} %get-tuple-element.86.low_ref, f32[128,1024]{1,0:T(8,128)S(1)} %all_gather.11.summed, ...), custom_call_target="tpu_custom_call" | custom-call | tf_op jit(solution)/shard_map/pallas_call | solution.py:157
  1664.7 1.6 concatenate.7.clone
  1666.3 2.6 all-to-all-start.4
  1669.7 20.1 %all-to-all-done.4 = f32[32,17,256]{2,1,0:T(8,128)S(1)} async-done(((f32[32,17,256]{2,1,0:T(8,128)}), f32[32,17,256]{2,1,0:T(8,128)S(1)}, u32[]{:S(2)}, u32[]{:S(2)}) %all-to-all-start.4) | async-done | bytes 557088 | tf_op jit(solution)/shard_map/all_to_all | solution.py:169
  1692.4 1.3 fusion.3
  (93 shorter events, 21.5 us)
Async XLA Ops:
  36.3 367.7 %collective-permute-start = (f32[32,128,256]{2,1,0:T(8,128)}, f32[32,128,256]{2,1,0:T(8,128)S(1)}, u32[]{:S(2)}, u32[]{:S(2)}) collective-permute-start(f32[32,128,256]{2,1,0:T(8,128)} %get-tuple-element.104), channel_id=1, source_target_pairs={{0,1},{1,2},{2,3},{3,0},{4,5},{5,6},{6,7},{7,4},{8,9},{9,10},{10,1... | collective-permute-start | bytes 12582920 | tf_op jit(solution)/shard_map/ppermute | solution.py:195
  38.5 115.1 %collective-permute-start.12 = (f32[8,128,256]{2,1,0:T(8,128)}, f32[8,128,256]{2,1,0:T(8,128)S(1)}, u32[]{:S(2)}, u32[]{:S(2)}) collective-permute-start(f32[8,128,256]{2,1,0:T(8,128)} %get-tuple-element.59), channel_id=1, source_target_pairs={{0,1},{1,2},{2,3},{3,0},{4,5},{5,6},{6,7},{7,4},{8,9},{9,10},{10,1... | collective-permute-start | bytes 3145736 | tf_op jit(solution)/shard_map/ppermute | solution.py:195
  39.8 160.2 %collective-permute-start.13 = (f32[8,128,256]{2,1,0:T(8,128)S(1)}, f32[8,128,256]{2,1,0:T(8,128)S(1)}, u32[]{:S(2)}, u32[]{:S(2)}) collective-permute-start(f32[8,128,256]{2,1,0:T(8,128)S(1)} %get-tuple-element.60), channel_id=1, source_target_pairs={{0,2},{1,3},{2,0},{3,1},{4,6},{5,7},{6,4},{7,5},{8,10},{9,11},{10,... | collective-permute-start | bytes 3145736 | tf_op jit(solution)/shard_map/ppermute | solution.py:195
  40.9 160.1 %collective-permute-start.14 = (f32[8,128,256]{2,1,0:T(8,128)S(1)}, f32[8,128,256]{2,1,0:T(8,128)S(1)}, u32[]{:S(2)}, u32[]{:S(2)}) collective-permute-start(f32[8,128,256]{2,1,0:T(8,128)S(1)} %get-tuple-element.61), channel_id=1, source_target_pairs={{0,3},{1,0},{2,1},{3,2},{4,7},{5,4},{6,5},{7,6},{8,11},{9,8},{10,9... | collective-permute-start | bytes 3145736 | tf_op jit(solution)/shard_map/ppermute | solution.py:195
  43.2 360.9 %collective-permute-start.1 = (f32[32,128,256]{2,1,0:T(8,128)}, f32[32,128,256]{2,1,0:T(8,128)S(1)}, u32[]{:S(2)}, u32[]{:S(2)}) collective-permute-start(f32[32,128,256]{2,1,0:T(8,128)} %get-tuple-element.103), channel_id=1, source_target_pairs={{0,2},{1,3},{2,0},{3,1},{4,6},{5,7},{6,4},{7,5},{8,10},{9,11},{10,... | collective-permute-start | bytes 12582920 | tf_op jit(solution)/shard_map/ppermute | solution.py:195
  153.6 1.1 copy-start.5
  154.7 249.4 %collective-permute-start.2 = (f32[32,128,256]{2,1,0:T(8,128)}, f32[32,128,256]{2,1,0:T(8,128)S(1)}, u32[]{:S(2)}, u32[]{:S(2)}) collective-permute-start(f32[32,128,256]{2,1,0:T(8,128)} %get-tuple-element.102), channel_id=1, source_target_pairs={{0,3},{1,0},{2,1},{3,2},{4,7},{5,4},{6,5},{7,6},{8,11},{9,8},{10,9... | collective-permute-start | bytes 12582920 | tf_op jit(solution)/shard_map/ppermute | solution.py:195
  200.0 1.0 copy-start.7
  201.0 1.0 copy-start.9
  202.0 469.5 %collective-permute-start.15 = (f32[32,128,256]{2,1,0:T(8,128)S(1)}, f32[32,128,256]{2,1,0:T(8,128)S(1)}, u32[]{:S(2)}, u32[]{:S(2)}) collective-permute-start(f32[32,128,256]{2,1,0:T(8,128)S(1)} %get-tuple-element.63), channel_id=1, source_target_pairs={{0,1},{1,2},{2,3},{3,0},{4,5},{5,6},{6,7},{7,4},{8,9},{9,10},{10,1... | collective-permute-start | bytes 12582920 | tf_op jit(solution)/shard_map/ppermute | solution.py:195
  400.9 540.1 %collective-permute-start.16 = (f32[32,128,256]{2,1,0:T(8,128)}, f32[32,128,256]{2,1,0:T(8,128)}, u32[]{:S(2)}, u32[]{:S(2)}) collective-permute-start(f32[32,128,256]{2,1,0:T(8,128)} %get-tuple-element.64), channel_id=1, source_target_pairs={{0,2},{1,3},{2,0},{3,1},{4,6},{5,7},{6,4},{7,5},{8,10},{9,11},{10,... | collective-permute-start | bytes 12582920 | tf_op jit(solution)/shard_map/ppermute | solution.py:195
  404.0 267.5 %copy-start.14 = (f32[32,128,256]{2,1,0:T(8,128)}, f32[32,128,256]{2,1,0:T(8,128)S(1)}, u32[]{:S(2)}) copy-start(f32[32,128,256]{2,1,0:T(8,128)S(1)} %collective-permute-done.refs_1_) | copy-start | bytes 12582916
  404.0 537.0 %collective-permute-start.17 = (f32[32,128,256]{2,1,0:T(8,128)}, f32[32,128,256]{2,1,0:T(8,128)}, u32[]{:S(2)}, u32[]{:S(2)}) collective-permute-start(f32[32,128,256]{2,1,0:T(8,128)} %get-tuple-element.65), channel_id=1, source_target_pairs={{0,3},{1,0},{2,1},{3,2},{4,7},{5,4},{6,5},{7,6},{8,11},{9,8},{10,9... | collective-permute-start | bytes 12582920 | tf_op jit(solution)/shard_map/ppermute | solution.py:195
  404.0 267.5 %copy-start.15 = (f32[32,128,256]{2,1,0:T(8,128)}, f32[32,128,256]{2,1,0:T(8,128)S(1)}, u32[]{:S(2)}) copy-start(f32[32,128,256]{2,1,0:T(8,128)S(1)} %collective-permute-done.1.refs_2_) | copy-start | bytes 12582916
  404.0 267.5 %copy-start.16 = (f32[32,128,256]{2,1,0:T(8,128)}, f32[32,128,256]{2,1,0:T(8,128)S(1)}, u32[]{:S(2)}) copy-start(f32[32,128,256]{2,1,0:T(8,128)S(1)} %collective-permute-done.2.refs_3_) | copy-start | bytes 12582916
  404.0 856.3 %collective-permute-start.3 = (f32[32,128,256]{2,1,0:T(8,128)}, f32[32,128,256]{2,1,0:T(8,128)}, u32[]{:S(2)}, u32[]{:S(2)}) collective-permute-start(f32[32,128,256]{2,1,0:T(8,128)} %get-tuple-element.51), channel_id=1, source_target_pairs={{0,1},{1,2},{2,3},{3,0},{4,5},{5,6},{6,7},{7,4},{8,9},{9,10},{10,1... | collective-permute-start | bytes 12582920 | tf_op jit(solution)/shard_map/ppermute | solution.py:195
  671.5 589.1 %collective-permute-start.4 = (f32[32,128,256]{2,1,0:T(8,128)}, f32[32,128,256]{2,1,0:T(8,128)}, u32[]{:S(2)}, u32[]{:S(2)}) collective-permute-start(f32[32,128,256]{2,1,0:T(8,128)} %get-tuple-element.52), channel_id=1, source_target_pairs={{0,2},{1,3},{2,0},{3,1},{4,6},{5,7},{6,4},{7,5},{8,10},{9,11},{10,... | collective-permute-start | bytes 12582920 | tf_op jit(solution)/shard_map/ppermute | solution.py:195
  671.5 1.9 copy-start.17
  673.4 587.1 %collective-permute-start.5 = (f32[32,128,256]{2,1,0:T(8,128)}, f32[32,128,256]{2,1,0:T(8,128)}, u32[]{:S(2)}, u32[]{:S(2)}) collective-permute-start(f32[32,128,256]{2,1,0:T(8,128)} %get-tuple-element.53), channel_id=1, source_target_pairs={{0,3},{1,0},{2,1},{3,2},{4,7},{5,4},{6,5},{7,6},{8,11},{9,8},{10,9... | collective-permute-start | bytes 12582920 | tf_op jit(solution)/shard_map/ppermute | solution.py:195
  675.5 355.6 %copy-start.21 = (f32[16]{0:T(128)S(1)}, f32[16]{0:T(128)}, u32[]{:S(2)}) copy-start(f32[16]{0:T(128)} %param.5) | copy-start | bytes 196
  675.5 355.7 %copy-start.19 = (f32[256,16]{0,1:T(8,128)S(1)}, f32[256,16]{0,1:T(8,128)}, u32[]{:S(2)}) copy-start(f32[256,16]{0,1:T(8,128)} %param.7) | copy-start | bytes 49156
  675.5 365.8 %copy-start.20 = (f32[256]{0:T(256)S(1)}, f32[256]{0:T(256)}, u32[]{:S(2)}) copy-start(f32[256]{0:T(256)} %param.6) | copy-start | bytes 3076
  941.0 471.7 %collective-permute-start.18 = (f32[16,128,256]{2,1,0:T(8,128)}, f32[16,128,256]{2,1,0:T(8,128)}, u32[]{:S(2)}, u32[]{:S(2)}) collective-permute-start(f32[16,128,256]{2,1,0:T(8,128)} %get-tuple-element.67), channel_id=1, source_target_pairs={{0,1},{1,2},{2,3},{3,0},{4,5},{5,6},{6,7},{7,4},{8,9},{9,10},{10,1... | collective-permute-start | bytes 6291464 | tf_op jit(solution)/shard_map/ppermute | solution.py:195
  1041.5 39.9 %collective-permute-start.9 = (f32[2,128,256]{2,1,0:T(8,128)S(1)}, f32[2,128,256]{2,1,0:T(8,128)S(1)}, u32[]{:S(2)}, u32[]{:S(2)}) collective-permute-start(f32[2,128,256]{2,1,0:T(8,128)S(1)} %get-tuple-element.126), channel_id=1, source_target_pairs={{0,1},{1,2},{2,3},{3,0},{4,5},{5,6},{6,7},{7,4},{8,9},{9,10},{10,1... | collective-permute-start | bytes 786440 | tf_op jit(solution)/shard_map/ppermute | solution.py:195
  1081.4 420.3 %collective-permute-start.19 = (f32[16,128,256]{2,1,0:T(8,128)}, f32[16,128,256]{2,1,0:T(8,128)}, u32[]{:S(2)}, u32[]{:S(2)}) collective-permute-start(f32[16,128,256]{2,1,0:T(8,128)} %get-tuple-element.68), channel_id=1, source_target_pairs={{0,2},{1,3},{2,0},{3,1},{4,6},{5,7},{6,4},{7,5},{8,10},{9,11},{10,... | collective-permute-start | bytes 6291464 | tf_op jit(solution)/shard_map/ppermute | solution.py:195
  1260.4 241.3 %collective-permute-start.20 = (f32[16,128,256]{2,1,0:T(8,128)}, f32[16,128,256]{2,1,0:T(8,128)}, u32[]{:S(2)}, u32[]{:S(2)}) collective-permute-start(f32[16,128,256]{2,1,0:T(8,128)} %get-tuple-element.69), channel_id=1, source_target_pairs={{0,3},{1,0},{2,1},{3,2},{4,7},{5,4},{6,5},{7,6},{8,11},{9,8},{10,9... | collective-permute-start | bytes 6291464 | tf_op jit(solution)/shard_map/ppermute | solution.py:195
  1260.6 147.1 %collective-permute-start.10 = (f32[2,128,256]{2,1,0:T(8,128)S(1)}, f32[2,128,256]{2,1,0:T(8,128)S(1)}, u32[]{:S(2)}, u32[]{:S(2)}) collective-permute-start(f32[2,128,256]{2,1,0:T(8,128)S(1)} %get-tuple-element.126), channel_id=1, source_target_pairs={{0,2},{1,3},{2,0},{3,1},{4,6},{5,7},{6,4},{7,5},{8,10},{9,11},{10,... | collective-permute-start | bytes 786440 | tf_op jit(solution)/shard_map/ppermute | solution.py:195
  1260.6 149.0 %collective-permute-start.11 = (f32[2,128,256]{2,1,0:T(8,128)S(1)}, f32[2,128,256]{2,1,0:T(8,128)S(1)}, u32[]{:S(2)}, u32[]{:S(2)}) collective-permute-start(f32[2,128,256]{2,1,0:T(8,128)S(1)} %get-tuple-element.126), channel_id=1, source_target_pairs={{0,3},{1,0},{2,1},{3,2},{4,7},{5,4},{6,5},{7,6},{8,11},{9,8},{10,9... | collective-permute-start | bytes 786440 | tf_op jit(solution)/shard_map/ppermute | solution.py:195
  1407.7 102.8 %collective-permute-start.6 = (f32[8,128,256]{2,1,0:T(8,128)}, f32[8,128,256]{2,1,0:T(8,128)}, u32[]{:S(2)}, u32[]{:S(2)}) collective-permute-start(f32[8,128,256]{2,1,0:T(8,128)} %get-tuple-element.55), channel_id=1, source_target_pairs={{0,1},{1,2},{2,3},{3,0},{4,5},{5,6},{6,7},{7,4},{8,9},{9,10},{10,1... | collective-permute-start | bytes 3145736 | tf_op jit(solution)/shard_map/ppermute | solution.py:195
  1409.6 6.1 copy-start.18
  1409.6 100.9 %collective-permute-start.7 = (f32[8,128,256]{2,1,0:T(8,128)}, f32[8,128,256]{2,1,0:T(8,128)}, u32[]{:S(2)}, u32[]{:S(2)}) collective-permute-start(f32[8,128,256]{2,1,0:T(8,128)} %get-tuple-element.56), channel_id=1, source_target_pairs={{0,2},{1,3},{2,0},{3,1},{4,6},{5,7},{6,4},{7,5},{8,10},{9,11},{10,... | collective-permute-start | bytes 3145736 | tf_op jit(solution)/shard_map/ppermute | solution.py:195
  1412.7 97.8 %collective-permute-start.8 = (f32[8,128,256]{2,1,0:T(8,128)}, f32[8,128,256]{2,1,0:T(8,128)}, u32[]{:S(2)}, u32[]{:S(2)}) collective-permute-start(f32[8,128,256]{2,1,0:T(8,128)} %get-tuple-element.57), channel_id=1, source_target_pairs={{0,3},{1,0},{2,1},{3,2},{4,7},{5,4},{6,5},{7,6},{8,11},{9,8},{10,9... | collective-permute-start | bytes 3145736 | tf_op jit(solution)/shard_map/ppermute | solution.py:195
  1445.7 10.9 copy-start.2
  1447.4 1.2 copy-start.4
  1448.6 1.2 copy-start.6
  1449.8 1.2 copy-start.8
  1451.0 1.2 copy-start.10
  1471.1 2.2 copy-start.1
  1473.3 14.1 copy-start
  1501.7 8.9 copy-start.3
  1530.1 9.3 all-to-all-start.1
  1590.6 0.8 copy-start.11
  1624.3 1.0 copy-start.12
  1662.7 0.8 copy-start.13
  1666.3 23.4 %all-to-all-start.4 = ((f32[32,17,256]{2,1,0:T(8,128)}), f32[32,17,256]{2,1,0:T(8,128)S(1)}, u32[]{:S(2)}, u32[]{:S(2)}) async-start(f32[32,17,256]{2,1,0:T(8,128)} %bitcast.42), calls=%async_computation.4 | async-start | bytes 1572864 | tf_op jit(solution)/shard_map/all_to_all | solution.py:169

commit v4 on v3

--- a/solution.py
+++ b/solution.py
@@ -8,8 +8,8 @@
 from jax.sharding import PartitionSpec as P
 
 ITERS = 3
-PARTS = (1, 4, 4, 4, 2, 1)
-CARRIER = 1
+PARTS = (1, 2, 4, 4, 4, 1)
+CARRIER = 2
 BF16 = jnp.bfloat16
 F32 = jnp.float32
 
@@ -183,21 +183,44 @@
     mine = occupied_energy.shape[0]
     me = lax.axis_index("vir")
 
-    sent = jnp.concatenate(
-        [right_side.T, jnp.broadcast_to(occupied_energy[:, None], (mine, 128))], axis=1
-    )
-    columns = lax.all_gather(sent, "aux", axis=0, tiled=True)
-    carried = jnp.stack(
-        [columns[:, :width], virtual_energy[None, :] - columns[:, width : width + 1]]
-    )
+    def start_and_gaps(earlier):
+        first, occupied, _ = lax.optimization_barrier((right_side, occupied_energy, earlier))
+        rows = jnp.concatenate(
+            [first.T, jnp.broadcast_to(occupied[:, None], (mine, 128))], axis=1
+        )
+        rows = lax.all_gather(rows, "aux", axis=0, tiled=True)
+        return jnp.stack([rows[:, :width], virtual_energy[None, :] - rows[:, width : width + 1]])
 
     def shifted(array, shift):
         return lax.ppermute(array, "vir", [(z, (z + shift) % groups) for z in range(groups)])
 
+    def by_source(pieces):
+        turned = pieces[:0:-1] + pieces[:1]
+        twice = jnp.concatenate(turned + turned[:-1], axis=1)
+        return lax.dynamic_slice(twice, (0, (groups - 1 - me) * width), (occ, whole))
+
     received = []
-    low_row = 0
+    held = start = None
+    low_row = offset = 0
+
+    def apply_part(k):
+        nonlocal held, offset
+        held = first_part(received[k], start, held, offset, aux_rows // groups)
+        offset += PARTS[k] * unit
+
     for k, share in enumerate(PARTS):
         count = share * unit
+        if k == CARRIER + 2:
+            for n in range(k - 1):
+                apply_part(n)
+        elif k > CARRIER + 2:
+            apply_part(k - 2)
+        if held is not None:
+            total, high, low = held
+            integrals, total, start, gap = lax.optimization_barrier((integrals, total, start, gap))
+            held = total, high, low
+        elif k >= 2:
+            integrals, _ = lax.optimization_barrier((integrals, received[k - 2]))
         blocks = [
             lax.dynamic_slice_in_dim(
                 integrals, low_row + lax.rem(me + shift, groups) * count, count, axis=0
@@ -207,22 +230,17 @@
         low_row += groups * count
         if k == 0:
             blocks, integrals = lax.optimization_barrier((blocks, integrals))
-        elif k >= 2:
-            blocks, _ = lax.optimization_barrier((blocks, received[k - 2]))
-        received.append(blocks[:1] + [shifted(blocks[n], n) for n in range(1, groups)])
+        sent = blocks[1:]
         if k == CARRIER:
-            spread = jnp.zeros((groups,) + carried.shape, F32)
-            for shift in range(groups):
-                piece = carried if shift == 0 else shifted(carried, shift)
-                source = lax.rem(me - shift + groups, groups)
-                spread = lax.dynamic_update_index_in_dim(spread, piece, source, 0)
-    start, gap = (jnp.moveaxis(spread[:, n], 0, 1).reshape(occ, whole) for n in range(2))
-
-    held = None
-    offset = 0
-    for pieces in received:
-        held = first_part(pieces, start, held, offset, aux_rows // groups)
-        offset += pieces[0].shape[0]
+            carried = start_and_gaps(received[0][1])
+            sent = [jnp.concatenate([block, carried], axis=0) for block in sent]
+        arrived = [shifted(block, n) for n, block in enumerate(sent, 1)]
+        received.append(blocks[:1] + arrived)
+        if k == CARRIER:
+            own_and_others = [carried] + [piece[count:] for piece in arrived]
+            start, gap = (by_source([piece[n] for piece in own_and_others]) for n in range(2))
+    for k in range(len(PARTS) - 2, len(PARTS)):
+        apply_part(k)
     total, high, low = held
 
     direction = residual = start

time: 1700 us -> 1770 us (1.041)
  waiting for transfers between devices: 619 us -> 979 us
  starting transfers between devices: 766 us -> 409 us
  blocking collectives: 69.4 us -> 174 us
  local copies, waits for them, and re-layouts: 96.3 us -> 61.8 us
    ppermute x21 -> x18, waiting for transfers between devices: 593 us -> 959 us  [shifted(): lax.ppermute(array, 'vir', [(z, (z + shift) % groups) for z in range(grou...]
    ppermute x21 -> x18, starting transfers between devices: 760 us -> 406 us  [shifted(): lax.ppermute(array, 'vir', [(z, (z + shift) % groups) for z in range(grou...]
    all_to_all x3 -> x4, blocking collectives: 32.7 us -> 135 us  [add_over(): lax.all_to_all(pieces, axes, split_axis=0, concat_axis=0, tiled=True)]
    dynamic_update_slice x4 -> x0, local copies, waits for them, and re-layouts: 26.9 us -> none  [on_device(): spread = lax.dynamic_update_index_in_dim(spread, piece, source, 0)]
    dynamic_slice x4 -> x6, local copies, waits for them, and re-layouts: 46.2 us -> 46.4 us  [on_device(): lax.dynamic_slice_in_dim(integrals, low_row + lax.rem(me + shift, groups)...]
  transfers between devices with their start and end apart: 23 -> 19, of which waited for: 7 -> 10; matrix products, arithmetic and copies ran while one was open for 3% -> 3% of each run, Pallas kernels for 3% -> 3%
where the time goes in v4:
time: 1770 us
  waiting for transfers between devices  979 us (55%)
  starting transfers between devices  409 us (23%)
  blocking collectives  174 us (10%)
  Pallas kernels  135 us (8%)
  local copies, waits for them, and re-layouts  61.8 us (3%)
    ppermute x18, waiting for transfers between devices, shifted(): lax.ppermute(array, 'vir', [(z, (z + shift) % groups) for z in range(grou...  959 us
    ppermute x18, starting transfers between devices, shifted(): lax.ppermute(array, 'vir', [(z, (z + shift) % groups) for z in range(grou...  406 us
    all_to_all x4, blocking collectives, add_over(): lax.all_to_all(pieces, axes, split_axis=0, concat_axis=0, tiled=True)  135 us
    pallas_call x2, Pallas kernels, later_apply(): pl.pallas_call(later_kernel, grid=(held // step,), in_specs=[block, block...  74.8 us
    pallas_call x6, Pallas kernels, first_part(): pl.pallas_call(functools.partial(first_kernel, first, groups), grid=(coun...  60.4 us
    dynamic_slice x6, local copies, waits for them, and re-layouts, on_device(): lax.dynamic_slice_in_dim(integrals, low_row + lax.rem(me + shift, groups)...  46.4 us
  transfers between devices with their start and end apart: 19, of which 10 were waited for; matrix products, arithmetic and copies ran while one was open for 3% of the time, Pallas kernels for 3%

profile of v4, /device:TPU:1, one launch (start us, length us, event | category | flops | bytes accessed | tf_op | source)
XLA Modules:
  0.0 1770.1 jit_solution(7091538412093386089)
XLA Ops:
  0.7 4.3 constant_dynamic-slice_fusion.22
  4.9 2.1 collective-permute-start
  7.1 2.3 collective-permute-start.1
  10.5 6.3 constant_dynamic-slice_fusion.18
  17.2 15.1 collective-permute-done.refs_1_
  32.4 11.5 all_gather.9
  44.0 34.8 %collective-permute-done.1.refs_2_ = f32[8,128,256]{2,1,0:T(8,128)} collective-permute-done((f32[8,128,256]{2,1,0:T(8,128)}, f32[8,128,256]{2,1,0:T(8,128)}, u32[]{:S(2)}, u32[]{:S(2)}) %collective-permute-start.1) | collective-permute-done | bytes 1048608 | tf_op jit(solution)/shard_map/ppermute | solution.py:195
  78.8 8.6 constant_dynamic-slice_fusion.14
  87.3 5.4 pad_maximum_fusion
  92.8 22.1 %collective-permute-start.8 = (f32[34,128,256]{2,1,0:T(8,128)}, f32[34,128,256]{2,1,0:T(8,128)}, u32[]{:S(2)}, u32[]{:S(2)}) collective-permute-start(f32[34,128,256]{2,1,0:T(8,128)} %get-tuple-element.122), channel_id=1, source_target_pairs={{0,3},{1,0},{2,1},{3,2},{4,7},{5,4},{6,5},{7,6},{8,11},{9,8},{10,9... | collective-permute-start | bytes 13369352 | tf_op jit(solution)/shard_map/ppermute | solution.py:195
  114.8 46.1 %collective-permute-start.7 = (f32[34,128,256]{2,1,0:T(8,128)}, f32[34,128,256]{2,1,0:T(8,128)}, u32[]{:S(2)}, u32[]{:S(2)}) collective-permute-start(f32[34,128,256]{2,1,0:T(8,128)} %get-tuple-element.123), channel_id=1, source_target_pairs={{0,2},{1,3},{2,0},{3,1},{4,6},{5,7},{6,4},{7,5},{8,10},{9,11},{10,... | collective-permute-start | bytes 13369352 | tf_op jit(solution)/shard_map/ppermute | solution.py:195
  161.0 1.2 collective-permute-start.4
  162.1 2.1 collective-permute-start.5
  164.2 469.3 %collective-permute-done.4.refs_2_ = f32[16,128,256]{2,1,0:T(8,128)} collective-permute-done((f32[16,128,256]{2,1,0:T(8,128)}, f32[16,128,256]{2,1,0:T(8,128)}, u32[]{:S(2)}, u32[]{:S(2)}) %collective-permute-start.4) | collective-permute-done | bytes 2097184 | tf_op jit(solution)/shard_map/ppermute | solution.py:195
  633.5 12.2 constant_dynamic-slice_fusion.8
  645.8 135.2 %collective-permute-start.9 = (f32[32,128,256]{2,1,0:T(8,128)}, f32[32,128,256]{2,1,0:T(8,128)}, u32[]{:S(2)}, u32[]{:S(2)}) collective-permute-start(f32[32,128,256]{2,1,0:T(8,128)} %get-tuple-element.100), channel_id=1, source_target_pairs={{0,1},{1,2},{2,3},{3,0},{4,5},{5,6},{6,7},{7,4},{8,9},{9,10},{10,1... | collective-permute-start | bytes 12582920 | tf_op jit(solution)/shard_map/ppermute | solution.py:195
  780.9 2.2 collective-permute-start.11
  791.8 5.9 shard_map.59
  797.7 8.6 shard_map.60
  806.3 14.1 shard_map.61
  820.4 12.2 constant_dynamic-slice_fusion
  832.7 1.8 collective-permute-start.16
  834.5 35.3 %collective-permute-done.9.refs_1_ = f32[32,128,256]{2,1,0:T(8,128)} collective-permute-done((f32[32,128,256]{2,1,0:T(8,128)}, f32[32,128,256]{2,1,0:T(8,128)}, u32[]{:S(2)}, u32[]{:S(2)}) %collective-permute-start.9) | collective-permute-done | bytes 4194336 | tf_op jit(solution)/shard_map/ppermute | solution.py:195
  869.8 1.2 collective-permute-start.17
  871.0 95.2 %collective-permute-done.10.refs_2_ = f32[32,128,256]{2,1,0:T(8,128)} collective-permute-done((f32[32,128,256]{2,1,0:T(8,128)}, f32[32,128,256]{2,1,0:T(8,128)}, u32[]{:S(2)}, u32[]{:S(2)}) %collective-permute-start.10) | collective-permute-done | bytes 4194336 | tf_op jit(solution)/shard_map/ppermute | solution.py:195
  966.1 83.5 %collective-permute-done.11.refs_3_ = f32[32,128,256]{2,1,0:T(8,128)} collective-permute-done((f32[32,128,256]{2,1,0:T(8,128)}, f32[32,128,256]{2,1,0:T(8,128)}, u32[]{:S(2)}, u32[]{:S(2)}) %collective-permute-start.11) | collective-permute-done | bytes 4194336 | tf_op jit(solution)/shard_map/ppermute | solution.py:195
  1049.6 2.2 copy-done.1
  1051.8 14.0 shard_map.62
  1065.7 2.8 constant_dynamic-slice_fusion.4
  1068.5 186.5 %collective-permute-start.12 = (f32[8,128,256]{2,1,0:T(8,128)S(1)}, f32[8,128,256]{2,1,0:T(8,128)S(1)}, u32[]{:S(2)}, u32[]{:S(2)}) collective-permute-start(f32[8,128,256]{2,1,0:T(8,128)S(1)} %get-tuple-element.96), channel_id=1, source_target_pairs={{0,1},{1,2},{2,3},{3,0},{4,5},{5,6},{6,7},{7,4},{8,9},{9,10},{10,1... | collective-permute-start | bytes 3145736 | tf_op jit(solution)/shard_map/ppermute | solution.py:195
  1255.0 2.2 collective-permute-start.14
  1257.1 111.7 %collective-permute-done.16.refs_2_ = f32[32,128,256]{2,1,0:T(8,128)} collective-permute-done((f32[32,128,256]{2,1,0:T(8,128)}, f32[32,128,256]{2,1,0:T(8,128)}, u32[]{:S(2)}, u32[]{:S(2)}) %collective-permute-start.16) | collective-permute-done | bytes 4194336 | tf_op jit(solution)/shard_map/ppermute | solution.py:195
  1368.8 14.1 shard_map.63
  1382.9 98.2 %collective-permute-done.13.refs_2_ = f32[8,128,256]{2,1,0:T(8,128)S(1)} collective-permute-done((f32[8,128,256]{2,1,0:T(8,128)S(1)}, f32[8,128,256]{2,1,0:T(8,128)S(1)}, u32[]{:S(2)}, u32[]{:S(2)}) %collective-permute-start.13) | collective-permute-done | bytes 1048608 | tf_op jit(solution)/shard_map/ppermute | solution.py:195
  1481.1 16.1 collective-permute-done.14.refs_3_
  1497.2 3.8 shard_map.64
  1501.0 15.6 all_to_all.25
  1516.7 100.1 %all_to_all.26 = f32[4,16,1024]{2,1,0:T(8,128)S(1)} all-to-all(f32[4,16,1024]{2,1,0:T(8,128)S(1)} %broadcast_in_dim.9), channel_id=1, replica_groups=mesh['aux'=8,'vir'=4] {'vir'}, dimensions={0} | all-to-all | bytes 524288 | tf_op jit(solution)/shard_map/all_to_all | solution.py:169
  1616.8 13.3 all_gather.10.summed
  1630.1 37.4 %shard_map.65 = (f32[128,1024]{1,0:T(8,128)S(1)}, f32[128,1024]{1,0:T(8,128)S(1)}, f32[128,1024]{1,0:T(8,128)S(1)}, f32[128,1024]{1,0:T(8,128)S(1)}) custom-call(bf16[128,128,1024]{2,1,0:T(8,128)(2,1)} %get-tuple-element.76.high_ref, bf16[128,128,1024]{2,1,0:T(8,128)(2,1)} %get-tuple-element.77.low_ref, f32[128,1024]{1,0:T(8,128)S(1)} %all_gather.10.summed, ...), custom_call_target="tpu_custom_call" | custom-call | tf_op jit(solution)/shard_map/pallas_call | solution.py:157
  1667.5 11.1 all_to_all.27
  1678.7 8.4 all_to_all.28
  1687.2 13.5 all_gather.11.summed
  1701.7 37.4 %shard_map.66 = (f32[128,1024]{1,0:T(8,128)S(1)}, f32[128,1024]{1,0:T(8,128)S(1)}, f32[128,1024]{1,0:T(8,128)S(1)}, f32[128,1024]{1,0:T(8,128)S(1)}) custom-call(bf16[128,128,1024]{2,1,0:T(8,128)(2,1)} %get-tuple-element.76.high_ref, bf16[128,128,1024]{2,1,0:T(8,128)(2,1)} %get-tuple-element.77.low_ref, f32[128,1024]{1,0:T(8,128)S(1)} %all_gather.11.summed, ...), custom_call_target="tpu_custom_call" | custom-call | tf_op jit(solution)/shard_map/pallas_call | solution.py:157
  1741.1 1.6 concatenate.30.clone
  1742.7 2.6 all-to-all-start.4
  1746.1 20.1 %all-to-all-done.4 = f32[32,17,256]{2,1,0:T(8,128)S(1)} async-done(((f32[32,17,256]{2,1,0:T(8,128)}), f32[32,17,256]{2,1,0:T(8,128)S(1)}, u32[]{:S(2)}, u32[]{:S(2)}) %all-to-all-start.4) | async-done | bytes 557088 | tf_op jit(solution)/shard_map/all_to_all | solution.py:169
  1768.8 1.3 fusion.15
  (69 shorter events, 15.0 us)
Async XLA Ops:
  4.9 27.3 %collective-permute-start = (f32[8,128,256]{2,1,0:T(8,128)}, f32[8,128,256]{2,1,0:T(8,128)S(1)}, u32[]{:S(2)}, u32[]{:S(2)}) collective-permute-start(f32[8,128,256]{2,1,0:T(8,128)} %get-tuple-element.47), channel_id=1, source_target_pairs={{0,1},{1,2},{2,3},{3,0},{4,5},{5,6},{6,7},{7,4},{8,9},{9,10},{10,1... | collective-permute-start | bytes 3145736 | tf_op jit(solution)/shard_map/ppermute | solution.py:195
  7.1 71.6 %collective-permute-start.1 = (f32[8,128,256]{2,1,0:T(8,128)}, f32[8,128,256]{2,1,0:T(8,128)}, u32[]{:S(2)}, u32[]{:S(2)}) collective-permute-start(f32[8,128,256]{2,1,0:T(8,128)} %get-tuple-element.48), channel_id=1, source_target_pairs={{0,2},{1,3},{2,0},{3,1},{4,6},{5,7},{6,4},{7,5},{8,10},{9,11},{10,... | collective-permute-start | bytes 3145736 | tf_op jit(solution)/shard_map/ppermute | solution.py:195
  9.4 69.3 %collective-permute-start.2 = (f32[8,128,256]{2,1,0:T(8,128)}, f32[8,128,256]{2,1,0:T(8,128)}, u32[]{:S(2)}, u32[]{:S(2)}) collective-permute-start(f32[8,128,256]{2,1,0:T(8,128)} %get-tuple-element.49), channel_id=1, source_target_pairs={{0,3},{1,0},{2,1},{3,2},{4,7},{5,4},{6,5},{7,6},{8,11},{9,8},{10,9... | collective-permute-start | bytes 3145736 | tf_op jit(solution)/shard_map/ppermute | solution.py:195
  10.5 21.8 %copy-start.11 = (f32[16]{0:T(128)S(1)}, f32[16]{0:T(128)}, u32[]{:S(2)}) copy-start(f32[16]{0:T(128)} %param.5) | copy-start | bytes 196
  10.5 21.9 %copy-start.9 = (f32[256,16]{0,1:T(8,128)S(1)}, f32[256,16]{0,1:T(8,128)}, u32[]{:S(2)}) copy-start(f32[256,16]{0,1:T(8,128)} %param.7) | copy-start | bytes 49156
  10.5 68.3 %copy-start.10 = (f32[256]{0:T(256)S(1)}, f32[256]{0:T(256)}, u32[]{:S(2)}) copy-start(f32[256]{0:T(256)} %param.6) | copy-start | bytes 3076
  16.8 145.4 %collective-permute-start.3 = (f32[16,128,256]{2,1,0:T(8,128)}, f32[16,128,256]{2,1,0:T(8,128)}, u32[]{:S(2)}, u32[]{:S(2)}) collective-permute-start(f32[16,128,256]{2,1,0:T(8,128)} %get-tuple-element.108), channel_id=1, source_target_pairs={{0,1},{1,2},{2,3},{3,0},{4,5},{5,6},{6,7},{7,4},{8,9},{9,10},{10,1... | collective-permute-start | bytes 6291464 | tf_op jit(solution)/shard_map/ppermute | solution.py:195
  32.3 55.1 %copy-start.4 = (f32[8,128,256]{2,1,0:T(8,128)}, f32[8,128,256]{2,1,0:T(8,128)S(1)}, u32[]{:S(2)}) copy-start(f32[8,128,256]{2,1,0:T(8,128)S(1)} %collective-permute-done.refs_1_) | copy-start | bytes 3145732
  92.8 688.2 %collective-permute-start.8 = (f32[34,128,256]{2,1,0:T(8,128)}, f32[34,128,256]{2,1,0:T(8,128)}, u32[]{:S(2)}, u32[]{:S(2)}) collective-permute-start(f32[34,128,256]{2,1,0:T(8,128)} %get-tuple-element.122), channel_id=1, source_target_pairs={{0,3},{1,0},{2,1},{3,2},{4,7},{5,4},{6,5},{7,6},{8,11},{9,8},{10,9... | collective-permute-start | bytes 13369352 | tf_op jit(solution)/shard_map/ppermute | solution.py:195
  114.8 669.2 %collective-permute-start.7 = (f32[34,128,256]{2,1,0:T(8,128)}, f32[34,128,256]{2,1,0:T(8,128)}, u32[]{:S(2)}, u32[]{:S(2)}) collective-permute-start(f32[34,128,256]{2,1,0:T(8,128)} %get-tuple-element.123), channel_id=1, source_target_pairs={{0,2},{1,3},{2,0},{3,1},{4,6},{5,7},{6,4},{7,5},{8,10},{9,11},{10,... | collective-permute-start | bytes 13369352 | tf_op jit(solution)/shard_map/ppermute | solution.py:195
  161.0 624.0 %collective-permute-start.6 = (f32[34,128,256]{2,1,0:T(8,128)}, f32[34,128,256]{2,1,0:T(8,128)}, u32[]{:S(2)}, u32[]{:S(2)}) collective-permute-start(f32[34,128,256]{2,1,0:T(8,128)} %get-tuple-element.124), channel_id=1, source_target_pairs={{0,1},{1,2},{2,3},{3,0},{4,5},{5,6},{6,7},{7,4},{8,9},{9,10},{10,1... | collective-permute-start | bytes 13369352 | tf_op jit(solution)/shard_map/ppermute | solution.py:195
  161.0 472.5 %collective-permute-start.4 = (f32[16,128,256]{2,1,0:T(8,128)}, f32[16,128,256]{2,1,0:T(8,128)}, u32[]{:S(2)}, u32[]{:S(2)}) collective-permute-start(f32[16,128,256]{2,1,0:T(8,128)} %get-tuple-element.107), channel_id=1, source_target_pairs={{0,2},{1,3},{2,0},{3,1},{4,6},{5,7},{6,4},{7,5},{8,10},{9,11},{10,... | collective-permute-start | bytes 6291464 | tf_op jit(solution)/shard_map/ppermute | solution.py:195
  162.1 471.4 %collective-permute-start.5 = (f32[16,128,256]{2,1,0:T(8,128)}, f32[16,128,256]{2,1,0:T(8,128)}, u32[]{:S(2)}, u32[]{:S(2)}) collective-permute-start(f32[16,128,256]{2,1,0:T(8,128)} %get-tuple-element.106), channel_id=1, source_target_pairs={{0,3},{1,0},{2,1},{3,2},{4,7},{5,4},{6,5},{7,6},{8,11},{9,8},{10,9... | collective-permute-start | bytes 6291464 | tf_op jit(solution)/shard_map/ppermute | solution.py:195
  645.7 146.0 %copy-start.3 = (f32[8,128,256]{2,1,0:T(8,128)S(1)}, f32[8,128,256]{2,1,0:T(8,128)}, u32[]{:S(2)}) copy-start(f32[8,128,256]{2,1,0:T(8,128)} %get-tuple-element.46.refs_0_) | copy-start | bytes 3145732
  645.8 146.0 %copy-start.5 = (f32[8,128,256]{2,1,0:T(8,128)S(1)}, f32[8,128,256]{2,1,0:T(8,128)}, u32[]{:S(2)}) copy-start(f32[8,128,256]{2,1,0:T(8,128)} %copy-done.4) | copy-start | bytes 3145732
  645.8 224.0 %collective-permute-start.9 = (f32[32,128,256]{2,1,0:T(8,128)}, f32[32,128,256]{2,1,0:T(8,128)}, u32[]{:S(2)}, u32[]{:S(2)}) collective-permute-start(f32[32,128,256]{2,1,0:T(8,128)} %get-tuple-element.100), channel_id=1, source_target_pairs={{0,1},{1,2},{2,3},{3,0},{4,5},{5,6},{6,7},{7,4},{8,9},{9,10},{10,1... | collective-permute-start | bytes 12582920 | tf_op jit(solution)/shard_map/ppermute | solution.py:195
  780.9 185.2 %collective-permute-start.10 = (f32[32,128,256]{2,1,0:T(8,128)}, f32[32,128,256]{2,1,0:T(8,128)}, u32[]{:S(2)}, u32[]{:S(2)}) collective-permute-start(f32[32,128,256]{2,1,0:T(8,128)} %get-tuple-element.99), channel_id=1, source_target_pairs={{0,2},{1,3},{2,0},{3,1},{4,6},{5,7},{6,4},{7,5},{8,10},{9,11},{10,... | collective-permute-start | bytes 12582920 | tf_op jit(solution)/shard_map/ppermute | solution.py:195
  780.9 268.6 %collective-permute-start.11 = (f32[32,128,256]{2,1,0:T(8,128)}, f32[32,128,256]{2,1,0:T(8,128)}, u32[]{:S(2)}, u32[]{:S(2)}) collective-permute-start(f32[32,128,256]{2,1,0:T(8,128)} %get-tuple-element.98), channel_id=1, source_target_pairs={{0,3},{1,0},{2,1},{3,2},{4,7},{5,4},{6,5},{7,6},{8,11},{9,8},{10,9... | collective-permute-start | bytes 12582920 | tf_op jit(solution)/shard_map/ppermute | solution.py:195
  797.7 8.6 copy-start
  832.7 422.3 %collective-permute-start.15 = (f32[32,128,256]{2,1,0:T(8,128)}, f32[32,128,256]{2,1,0:T(8,128)}, u32[]{:S(2)}, u32[]{:S(2)}) collective-permute-start(f32[32,128,256]{2,1,0:T(8,128)} %get-tuple-element.92), channel_id=1, source_target_pairs={{0,1},{1,2},{2,3},{3,0},{4,5},{5,6},{6,7},{7,4},{8,9},{9,10},{10,1... | collective-permute-start | bytes 12582920 | tf_op jit(solution)/shard_map/ppermute | solution.py:195
  832.7 536.2 %collective-permute-start.16 = (f32[32,128,256]{2,1,0:T(8,128)}, f32[32,128,256]{2,1,0:T(8,128)}, u32[]{:S(2)}, u32[]{:S(2)}) collective-permute-start(f32[32,128,256]{2,1,0:T(8,128)} %get-tuple-element.91), channel_id=1, source_target_pairs={{0,2},{1,3},{2,0},{3,1},{4,6},{5,7},{6,4},{7,5},{8,10},{9,11},{10,... | collective-permute-start | bytes 12582920 | tf_op jit(solution)/shard_map/ppermute | solution.py:195
  869.8 499.1 %collective-permute-start.17 = (f32[32,128,256]{2,1,0:T(8,128)}, f32[32,128,256]{2,1,0:T(8,128)}, u32[]{:S(2)}, u32[]{:S(2)}) collective-permute-start(f32[32,128,256]{2,1,0:T(8,128)} %get-tuple-element.90), channel_id=1, source_target_pairs={{0,3},{1,0},{2,1},{3,2},{4,7},{5,4},{6,5},{7,6},{8,11},{9,8},{10,9... | collective-permute-start | bytes 12582920 | tf_op jit(solution)/shard_map/ppermute | solution.py:195
  1049.6 2.2 copy-start.1
  1065.7 303.1 %copy-start.2 = (f32[32,128,256]{2,1,0:T(8,128)S(1)}, f32[32,128,256]{2,1,0:T(8,128)}, u32[]{:S(2)}) copy-start(f32[32,128,256]{2,1,0:T(8,128)} %get-tuple-element.93.refs_0_) | copy-start | bytes 12582916
  1068.5 314.4 %collective-permute-start.12 = (f32[8,128,256]{2,1,0:T(8,128)S(1)}, f32[8,128,256]{2,1,0:T(8,128)S(1)}, u32[]{:S(2)}, u32[]{:S(2)}) collective-permute-start(f32[8,128,256]{2,1,0:T(8,128)S(1)} %get-tuple-element.96), channel_id=1, source_target_pairs={{0,1},{1,2},{2,3},{3,0},{4,5},{5,6},{6,7},{7,4},{8,9},{9,10},{10,1... | collective-permute-start | bytes 3145736 | tf_op jit(solution)/shard_map/ppermute | solution.py:195
  1255.0 226.2 %collective-permute-start.13 = (f32[8,128,256]{2,1,0:T(8,128)S(1)}, f32[8,128,256]{2,1,0:T(8,128)S(1)}, u32[]{:S(2)}, u32[]{:S(2)}) collective-permute-start(f32[8,128,256]{2,1,0:T(8,128)S(1)} %get-tuple-element.95), channel_id=1, source_target_pairs={{0,2},{1,3},{2,0},{3,1},{4,6},{5,7},{6,4},{7,5},{8,10},{9,11},{10,... | collective-permute-start | bytes 3145736 | tf_op jit(solution)/shard_map/ppermute | solution.py:195
  1255.0 242.3 %collective-permute-start.14 = (f32[8,128,256]{2,1,0:T(8,128)S(1)}, f32[8,128,256]{2,1,0:T(8,128)S(1)}, u32[]{:S(2)}, u32[]{:S(2)}) collective-permute-start(f32[8,128,256]{2,1,0:T(8,128)S(1)} %get-tuple-element.94), channel_id=1, source_target_pairs={{0,3},{1,0},{2,1},{3,2},{4,7},{5,4},{6,5},{7,6},{8,11},{9,8},{10,9... | collective-permute-start | bytes 3145736 | tf_op jit(solution)/shard_map/ppermute | solution.py:195
  1667.5 33.2 %copy-start.6 = (f32[128,1024]{1,0:T(8,128)}, f32[128,1024]{1,0:T(8,128)S(1)}, u32[]{:S(2)}) copy-start(f32[128,1024]{1,0:T(8,128)S(1)} %get-tuple-element.83.iterate) | copy-start | bytes 1572868
  1700.7 1.0 copy-start.7
  1739.1 0.8 copy-start.8
  1742.7 23.5 %all-to-all-start.4 = ((f32[32,17,256]{2,1,0:T(8,128)}), f32[32,17,256]{2,1,0:T(8,128)S(1)}, u32[]{:S(2)}, u32[]{:S(2)}) async-start(f32[32,17,256]{2,1,0:T(8,128)} %bitcast.11), calls=%async_computation.4 | async-start | bytes 1572864 | tf_op jit(solution)/shard_map/all_to_all | solution.py:169

commit v5 on v4

--- a/solution.py
+++ b/solution.py
@@ -8,8 +8,9 @@
 from jax.sharding import PartitionSpec as P
 
 ITERS = 3
-PARTS = (1, 2, 4, 4, 4, 1)
+PARTS = (1, 2, 2, 3, 3, 2, 2, 1)
 CARRIER = 2
+DEPTH = 3
 BF16 = jnp.bfloat16
 F32 = jnp.float32
 
@@ -201,26 +202,18 @@
 
     received = []
     held = start = None
-    low_row = offset = 0
-
-    def apply_part(k):
-        nonlocal held, offset
-        held = first_part(received[k], start, held, offset, aux_rows // groups)
-        offset += PARTS[k] * unit
+    low_row = offset = applied = 0
+
+    def apply_part():
+        nonlocal held, offset, applied
+        held = first_part(received[applied], start, held, offset, aux_rows // groups)
+        offset += PARTS[applied] * unit
+        applied += 1
 
     for k, share in enumerate(PARTS):
         count = share * unit
-        if k == CARRIER + 2:
-            for n in range(k - 1):
-                apply_part(n)
-        elif k > CARRIER + 2:
-            apply_part(k - 2)
-        if held is not None:
-            total, high, low = held
-            integrals, total, start, gap = lax.optimization_barrier((integrals, total, start, gap))
-            held = total, high, low
-        elif k >= 2:
-            integrals, _ = lax.optimization_barrier((integrals, received[k - 2]))
+        if k == CARRIER:
+            integrals, _ = lax.optimization_barrier((integrals, received[0][1]))
         blocks = [
             lax.dynamic_slice_in_dim(
                 integrals, low_row + lax.rem(me + shift, groups) * count, count, axis=0
@@ -234,13 +227,22 @@
         if k == CARRIER:
             carried = start_and_gaps(received[0][1])
             sent = [jnp.concatenate([block, carried], axis=0) for block in sent]
+        if k >= DEPTH:
+            while start is not None and k - DEPTH >= CARRIER and applied <= k - DEPTH:
+                apply_part()
+            if held is None:
+                sent, _ = lax.optimization_barrier((sent, received[k - DEPTH]))
+            else:
+                total, high, low = held
+                sent, total, start, gap = lax.optimization_barrier((sent, total, start, gap))
+                held = total, high, low
         arrived = [shifted(block, n) for n, block in enumerate(sent, 1)]
         received.append(blocks[:1] + arrived)
         if k == CARRIER:
             own_and_others = [carried] + [piece[count:] for piece in arrived]
             start, gap = (by_source([piece[n] for piece in own_and_others]) for n in range(2))
-    for k in range(len(PARTS) - 2, len(PARTS)):
-        apply_part(k)
+    while applied < len(PARTS):
+        apply_part()
     total, high, low = held
 
     direction = residual = start

time: 1770 us -> 1650 us (0.932)
  waiting for transfers between devices: 979 us -> 802 us
  starting transfers between devices: 409 us -> 528 us
  blocking collectives: 174 us -> 102 us
    ppermute x18 -> x24, waiting for transfers between devices: 959 us -> 782 us  [shifted(): lax.ppermute(array, 'vir', [(z, (z + shift) % groups) for z in range(grou...]
    ppermute x18 -> x24, starting transfers between devices: 406 us -> 525 us  [shifted(): lax.ppermute(array, 'vir', [(z, (z + shift) % groups) for z in range(grou...]
    all_to_all x4, blocking collectives: 135 us -> 62.9 us  [add_over(): lax.all_to_all(pieces, axes, split_axis=0, concat_axis=0, tiled=True)]
    pallas_call x6 -> x8, Pallas kernels: 60.4 us -> 67.3 us  [first_part(): pl.pallas_call(functools.partial(first_kernel, first, groups), grid=(coun...]
    dynamic_slice x6 -> x5, local copies, waits for them, and re-layouts: 46.4 us -> 46.9 us  [on_device(): lax.dynamic_slice_in_dim(integrals, low_row + lax.rem(me + shift, groups)...]
  transfers between devices with their start and end apart: 19 -> 25, of which waited for: 10 -> 9; matrix products, arithmetic and copies ran while one was open for 3% -> 4% of each run, Pallas kernels for 3% -> 4%
where the time goes in v5:
time: 1650 us
  waiting for transfers between devices  802 us (49%)
  starting transfers between devices  528 us (32%)
  Pallas kernels  142 us (9%)
  blocking collectives  102 us (6%)
  local copies, waits for them, and re-layouts  64.3 us (4%)
    ppermute x24, waiting for transfers between devices, shifted(): lax.ppermute(array, 'vir', [(z, (z + shift) % groups) for z in range(grou...  782 us
    ppermute x24, starting transfers between devices, shifted(): lax.ppermute(array, 'vir', [(z, (z + shift) % groups) for z in range(grou...  525 us
    pallas_call x2, Pallas kernels, later_apply(): pl.pallas_call(later_kernel, grid=(held // step,), in_specs=[block, block...  74.8 us
    pallas_call x8, Pallas kernels, first_part(): pl.pallas_call(functools.partial(first_kernel, first, groups), grid=(coun...  67.3 us
    all_to_all x4, blocking collectives, add_over(): lax.all_to_all(pieces, axes, split_axis=0, concat_axis=0, tiled=True)  62.9 us
    dynamic_slice x5, local copies, waits for them, and re-layouts, on_device(): lax.dynamic_slice_in_dim(integrals, low_row + lax.rem(me + shift, groups)...  46.9 us
  transfers between devices with their start and end apart: 25, of which 9 were waited for; matrix products, arithmetic and copies ran while one was open for 4% of the time, Pallas kernels for 4%

profile of v5, /device:TPU:1, one launch (start us, length us, event | category | flops | bytes accessed | tf_op | source)
XLA Modules:
  0.0 1649.7 jit_solution(6960460653263472518)
XLA Ops:
  0.7 4.2 constant_dynamic-slice_fusion.30
  4.9 2.1 collective-permute-start
  7.0 6.3 constant_dynamic-slice_fusion.18
  15.7 2.4 collective-permute-start.8
  18.1 14.2 collective-permute-done.refs_1_
  33.4 12.1 all_gather.9
  45.7 16.4 constant_dynamic-slice_fusion
  62.1 5.5 pad_maximum_fusion
  67.6 56.1 %collective-permute-done.7.refs_2_ = f32[8,128,256]{2,1,0:T(8,128)} collective-permute-done((f32[8,128,256]{2,1,0:T(8,128)}, f32[8,128,256]{2,1,0:T(8,128)}, u32[]{:S(2)}, u32[]{:S(2)}) %collective-permute-start.7) | collective-permute-done | bytes 1048608 | tf_op jit(solution)/shard_map/ppermute | solution.py:196
  123.7 111.8 %collective-permute-start.14 = (f32[18,128,256]{2,1,0:T(8,128)}, f32[18,128,256]{2,1,0:T(8,128)}, u32[]{:S(2)}, u32[]{:S(2)}) collective-permute-start(f32[18,128,256]{2,1,0:T(8,128)} %get-tuple-element.172), channel_id=1, source_target_pairs={{0,3},{1,0},{2,1},{3,2},{4,7},{5,4},{6,5},{7,6},{8,11},{9,8},{10,9... | collective-permute-start | bytes 7077896 | tf_op jit(solution)/shard_map/ppermute | solution.py:196
  235.8 17.2 %constant_dynamic-slice_fusion.11 = (f32[24,128,256]{2,1,0:T(8,128)}, f32[24,128,256]{2,1,0:T(8,128)}, f32[24,128,256]{2,1,0:T(8,128)}, f32[24,128,256]{2,1,0:T(...) fusion(f32[512,128,256]{2,1,0:T(8,128)} %param.4, ...), kind=kLoop, calls=%fused_computation.50 | loop fusion | bytes 50331680 | tf_op jit(solution)/shard_map/dynamic_slice | solution.py:218
  253.0 2.1 collective-permute-start.10
  255.1 126.5 %collective-permute-start.11 = (f32[24,128,256]{2,1,0:T(8,128)}, f32[24,128,256]{2,1,0:T(8,128)}, u32[]{:S(2)}, u32[]{:S(2)}) collective-permute-start(f32[24,128,256]{2,1,0:T(8,128)} %get-tuple-element.77), channel_id=1, source_target_pairs={{0,3},{1,0},{2,1},{3,2},{4,7},{5,4},{6,5},{7,6},{8,11},{9,8},{10,9... | collective-permute-start | bytes 9437192 | tf_op jit(solution)/shard_map/ppermute | solution.py:196
  381.6 118.0 %collective-permute-start.9 = (f32[24,128,256]{2,1,0:T(8,128)}, f32[24,128,256]{2,1,0:T(8,128)}, u32[]{:S(2)}, u32[]{:S(2)}) collective-permute-start(f32[24,128,256]{2,1,0:T(8,128)} %get-tuple-element.75), channel_id=1, source_target_pairs={{0,1},{1,2},{2,3},{3,0},{4,5},{5,6},{6,7},{7,4},{8,9},{9,10},{10,1... | collective-permute-start | bytes 9437192 | tf_op jit(solution)/shard_map/ppermute | solution.py:196
  500.5 116.8 %collective-permute-done.13.refs_2_ = f32[18,128,256]{2,1,0:T(8,128)} collective-permute-done((f32[18,128,256]{2,1,0:T(8,128)}, f32[18,128,256]{2,1,0:T(8,128)}, u32[]{:S(2)}, u32[]{:S(2)}) %collective-permute-start.13) | collective-permute-done | bytes 2359328 | tf_op jit(solution)/shard_map/ppermute | solution.py:196
  622.3 197.2 %collective-permute-done.10.refs_2_ = f32[24,128,256]{2,1,0:T(8,128)} collective-permute-done((f32[24,128,256]{2,1,0:T(8,128)}, f32[24,128,256]{2,1,0:T(8,128)}, u32[]{:S(2)}, u32[]{:S(2)}) %collective-permute-start.10) | collective-permute-done | bytes 3145760 | tf_op jit(solution)/shard_map/ppermute | solution.py:196
  825.0 5.9 shard_map.59
  830.9 8.7 shard_map.60
  839.6 8.7 shard_map.61
  848.4 38.8 %collective-permute-start.21 = (f32[16,128,256]{2,1,0:T(8,128)S(1)}, f32[16,128,256]{2,1,0:T(8,128)S(1)}, u32[]{:S(2)}, u32[]{:S(2)}) collective-permute-start(f32[16,128,256]{2,1,0:T(8,128)S(1)} %copy-done.13), channel_id=1, source_target_pairs={{0,1},{1,2},{2,3},{3,0},{4,5},{5,6},{6,7},{7,4},{8,9},{9,10},{10,1... | collective-permute-start | bytes 6291464 | tf_op jit(solution)/shard_map/ppermute | solution.py:196
  887.3 11.4 shard_map.62
  898.7 2.2 collective-permute-start.23
  900.9 143.4 %collective-permute-done.5.refs_2_ = f32[24,128,256]{2,1,0:T(8,128)} collective-permute-done((f32[24,128,256]{2,1,0:T(8,128)}, f32[24,128,256]{2,1,0:T(8,128)}, u32[]{:S(2)}, u32[]{:S(2)}) %collective-permute-start.5) | collective-permute-done | bytes 3145760 | tf_op jit(solution)/shard_map/ppermute | solution.py:196
  1044.3 64.9 %collective-permute-start.18 = (f32[16,128,256]{2,1,0:T(8,128)}, f32[16,128,256]{2,1,0:T(8,128)}, u32[]{:S(2)}, u32[]{:S(2)}) collective-permute-start(f32[16,128,256]{2,1,0:T(8,128)} %get-tuple-element.103), channel_id=1, source_target_pairs={{0,1},{1,2},{2,3},{3,0},{4,5},{5,6},{6,7},{7,4},{8,9},{9,10},{10,1... | collective-permute-start | bytes 6291464 | tf_op jit(solution)/shard_map/ppermute | solution.py:196
  1109.2 3.1 collective-permute-start.19
  1113.7 2.0 collective-permute-start.20
  1115.7 2.7 constant_dynamic-slice_fusion.26
  1118.8 11.6 shard_map.63
  1130.5 116.1 %collective-permute-done.22.refs_2_ = f32[16,128,256]{2,1,0:T(8,128)} collective-permute-done((f32[16,128,256]{2,1,0:T(8,128)}, f32[16,128,256]{2,1,0:T(8,128)}, u32[]{:S(2)}, u32[]{:S(2)}) %collective-permute-start.22) | collective-permute-done | bytes 2097184 | tf_op jit(solution)/shard_map/ppermute | solution.py:196
  1246.6 42.4 %collective-permute-start.15 = (f32[8,128,256]{2,1,0:T(8,128)S(1)}, f32[8,128,256]{2,1,0:T(8,128)S(1)}, u32[]{:S(2)}, u32[]{:S(2)}) collective-permute-start(f32[8,128,256]{2,1,0:T(8,128)S(1)} %get-tuple-element.99), channel_id=1, source_target_pairs={{0,1},{1,2},{2,3},{3,0},{4,5},{5,6},{6,7},{7,4},{8,9},{9,10},{10,1... | collective-permute-start | bytes 3145736 | tf_op jit(solution)/shard_map/ppermute | solution.py:196
  1289.0 3.1 collective-permute-start.16
  1292.1 1.8 collective-permute-start.17
  1293.9 8.4 shard_map.64
  1302.3 79.1 %collective-permute-done.19.refs_2_ = f32[16,128,256]{2,1,0:T(8,128)} collective-permute-done((f32[16,128,256]{2,1,0:T(8,128)}, f32[16,128,256]{2,1,0:T(8,128)}, u32[]{:S(2)}, u32[]{:S(2)}) %collective-permute-start.19) | collective-permute-done | bytes 2097184 | tf_op jit(solution)/shard_map/ppermute | solution.py:196
  1381.4 8.7 shard_map.65
  1390.2 58.6 %collective-permute-done.16.refs_2_ = f32[8,128,256]{2,1,0:T(8,128)S(1)} collective-permute-done((f32[8,128,256]{2,1,0:T(8,128)S(1)}, f32[8,128,256]{2,1,0:T(8,128)S(1)}, u32[]{:S(2)}, u32[]{:S(2)}) %collective-permute-start.16) | collective-permute-done | bytes 1048608 | tf_op jit(solution)/shard_map/ppermute | solution.py:196
  1448.7 3.8 shard_map.66
  1452.5 12.5 all_to_all.25
  1465.1 30.8 %all_to_all.26 = f32[4,16,1024]{2,1,0:T(8,128)S(1)} all-to-all(f32[4,16,1024]{2,1,0:T(8,128)S(1)} %broadcast_in_dim.9), channel_id=1, replica_groups=mesh['aux'=8,'vir'=4] {'vir'}, dimensions={0} | all-to-all | bytes 524288 | tf_op jit(solution)/shard_map/all_to_all | solution.py:170
  1495.9 13.5 all_gather.10.summed
  1509.5 37.4 %shard_map.67 = (f32[128,1024]{1,0:T(8,128)S(1)}, f32[128,1024]{1,0:T(8,128)S(1)}, f32[128,1024]{1,0:T(8,128)S(1)}, f32[128,1024]{1,0:T(8,128)S(1)}) custom-call(bf16[128,128,1024]{2,1,0:T(8,128)(2,1)} %get-tuple-element.118.high_ref, bf16[128,128,1024]{2,1,0:T(8,128)(2,1)} %get-tuple-element.119.low_ref, f32[128,1024]{1,0:T(8,128)S(1)} %all_gather.10.summed, ...), custom_call_target="tpu_custom_call" | custom-call | tf_op jit(solution)/shard_map/pallas_call | solution.py:158
  1546.9 11.1 all_to_all.27
  1558.1 8.4 all_to_all.28
  1566.5 13.3 all_gather.11.summed
  1580.8 37.4 %shard_map.68 = (f32[128,1024]{1,0:T(8,128)S(1)}, f32[128,1024]{1,0:T(8,128)S(1)}, f32[128,1024]{1,0:T(8,128)S(1)}, f32[128,1024]{1,0:T(8,128)S(1)}) custom-call(bf16[128,128,1024]{2,1,0:T(8,128)(2,1)} %get-tuple-element.118.high_ref, bf16[128,128,1024]{2,1,0:T(8,128)(2,1)} %get-tuple-element.119.low_ref, f32[128,1024]{1,0:T(8,128)S(1)} %all_gather.11.summed, ...), custom_call_target="tpu_custom_call" | custom-call | tf_op jit(solution)/shard_map/pallas_call | solution.py:158
  1620.2 1.6 concatenate.30.clone
  1621.8 2.7 all-to-all-start.4
  1625.2 20.1 %all-to-all-done.4 = f32[32,17,256]{2,1,0:T(8,128)S(1)} async-done(((f32[32,17,256]{2,1,0:T(8,128)}), f32[32,17,256]{2,1,0:T(8,128)S(1)}, u32[]{:S(2)}, u32[]{:S(2)}) %all-to-all-start.4) | async-done | bytes 557088 | tf_op jit(solution)/shard_map/all_to_all | solution.py:170
  (92 shorter events, 23.1 us)
Async XLA Ops:
  4.9 27.3 %collective-permute-start = (f32[8,128,256]{2,1,0:T(8,128)}, f32[8,128,256]{2,1,0:T(8,128)S(1)}, u32[]{:S(2)}, u32[]{:S(2)}) collective-permute-start(f32[8,128,256]{2,1,0:T(8,128)} %get-tuple-element.67), channel_id=1, source_target_pairs={{0,1},{1,2},{2,3},{3,0},{4,5},{5,6},{6,7},{7,4},{8,9},{9,10},{10,1... | collective-permute-start | bytes 3145736 | tf_op jit(solution)/shard_map/ppermute | solution.py:196
  7.0 26.3 %copy-start.16 = (f32[16]{0:T(128)S(1)}, f32[16]{0:T(128)}, u32[]{:S(2)}) copy-start(f32[16]{0:T(128)} %param.5) | copy-start | bytes 196
  7.0 26.3 %copy-start.14 = (f32[256,16]{0,1:T(8,128)S(1)}, f32[256,16]{0,1:T(8,128)}, u32[]{:S(2)}) copy-start(f32[256,16]{0,1:T(8,128)} %param.7) | copy-start | bytes 49156
  7.0 38.5 %copy-start.15 = (f32[256]{0:T(256)S(1)}, f32[256]{0:T(256)}, u32[]{:S(2)}) copy-start(f32[256]{0:T(256)} %param.6) | copy-start | bytes 3076
  13.3 222.2 %collective-permute-start.1 = (f32[16,128,256]{2,1,0:T(8,128)}, f32[16,128,256]{2,1,0:T(8,128)}, u32[]{:S(2)}, u32[]{:S(2)}) collective-permute-start(f32[16,128,256]{2,1,0:T(8,128)} %get-tuple-element.154), channel_id=1, source_target_pairs={{0,1},{1,2},{2,3},{3,0},{4,5},{5,6},{6,7},{7,4},{8,9},{9,10},{10,1... | collective-permute-start | bytes 6291464 | tf_op jit(solution)/shard_map/ppermute | solution.py:196
  14.6 109.0 %collective-permute-start.7 = (f32[8,128,256]{2,1,0:T(8,128)}, f32[8,128,256]{2,1,0:T(8,128)}, u32[]{:S(2)}, u32[]{:S(2)}) collective-permute-start(f32[8,128,256]{2,1,0:T(8,128)} %get-tuple-element.73), channel_id=1, source_target_pairs={{0,2},{1,3},{2,0},{3,1},{4,6},{5,7},{6,4},{7,5},{8,10},{9,11},{10,... | collective-permute-start | bytes 3145736 | tf_op jit(solution)/shard_map/ppermute | solution.py:196
  15.7 219.9 %collective-permute-start.8 = (f32[8,128,256]{2,1,0:T(8,128)}, f32[8,128,256]{2,1,0:T(8,128)}, u32[]{:S(2)}, u32[]{:S(2)}) collective-permute-start(f32[8,128,256]{2,1,0:T(8,128)} %get-tuple-element.74), channel_id=1, source_target_pairs={{0,3},{1,0},{2,1},{3,2},{4,7},{5,4},{6,5},{7,6},{8,11},{9,8},{10,9... | collective-permute-start | bytes 3145736 | tf_op jit(solution)/shard_map/ppermute | solution.py:196
  18.0 235.0 %collective-permute-start.2 = (f32[16,128,256]{2,1,0:T(8,128)}, f32[16,128,256]{2,1,0:T(8,128)}, u32[]{:S(2)}, u32[]{:S(2)}) collective-permute-start(f32[16,128,256]{2,1,0:T(8,128)} %get-tuple-element.153), channel_id=1, source_target_pairs={{0,2},{1,3},{2,0},{3,1},{4,6},{5,7},{6,4},{7,5},{8,10},{9,11},{10,... | collective-permute-start | bytes 6291464 | tf_op jit(solution)/shard_map/ppermute | solution.py:196
  32.2 29.9 %copy-start.8 = (f32[8,128,256]{2,1,0:T(8,128)}, f32[8,128,256]{2,1,0:T(8,128)S(1)}, u32[]{:S(2)}) copy-start(f32[8,128,256]{2,1,0:T(8,128)S(1)} %collective-permute-done.refs_1_) | copy-start | bytes 3145732
  32.2 222.9 %collective-permute-start.3 = (f32[16,128,256]{2,1,0:T(8,128)}, f32[16,128,256]{2,1,0:T(8,128)}, u32[]{:S(2)}, u32[]{:S(2)}) collective-permute-start(f32[16,128,256]{2,1,0:T(8,128)} %get-tuple-element.152), channel_id=1, source_target_pairs={{0,3},{1,0},{2,1},{3,2},{4,7},{5,4},{6,5},{7,6},{8,11},{9,8},{10,9... | collective-permute-start | bytes 6291464 | tf_op jit(solution)/shard_map/ppermute | solution.py:196
  123.7 257.9 %collective-permute-start.14 = (f32[18,128,256]{2,1,0:T(8,128)}, f32[18,128,256]{2,1,0:T(8,128)}, u32[]{:S(2)}, u32[]{:S(2)}) collective-permute-start(f32[18,128,256]{2,1,0:T(8,128)} %get-tuple-element.172), channel_id=1, source_target_pairs={{0,3},{1,0},{2,1},{3,2},{4,7},{5,4},{6,5},{7,6},{8,11},{9,8},{10,9... | collective-permute-start | bytes 7077896 | tf_op jit(solution)/shard_map/ppermute | solution.py:196
  235.5 381.8 %collective-permute-start.13 = (f32[18,128,256]{2,1,0:T(8,128)}, f32[18,128,256]{2,1,0:T(8,128)}, u32[]{:S(2)}, u32[]{:S(2)}) collective-permute-start(f32[18,128,256]{2,1,0:T(8,128)} %get-tuple-element.173), channel_id=1, source_target_pairs={{0,2},{1,3},{2,0},{3,1},{4,6},{5,7},{6,4},{7,5},{8,10},{9,11},{10,... | collective-permute-start | bytes 7077896 | tf_op jit(solution)/shard_map/ppermute | solution.py:196
  235.5 382.7 %collective-permute-start.12 = (f32[18,128,256]{2,1,0:T(8,128)}, f32[18,128,256]{2,1,0:T(8,128)}, u32[]{:S(2)}, u32[]{:S(2)}) collective-permute-start(f32[18,128,256]{2,1,0:T(8,128)} %get-tuple-element.174), channel_id=1, source_target_pairs={{0,1},{1,2},{2,3},{3,0},{4,5},{5,6},{6,7},{7,4},{8,9},{9,10},{10,1... | collective-permute-start | bytes 7077896 | tf_op jit(solution)/shard_map/ppermute | solution.py:196
  253.0 566.6 %collective-permute-start.10 = (f32[24,128,256]{2,1,0:T(8,128)}, f32[24,128,256]{2,1,0:T(8,128)}, u32[]{:S(2)}, u32[]{:S(2)}) collective-permute-start(f32[24,128,256]{2,1,0:T(8,128)} %get-tuple-element.76), channel_id=1, source_target_pairs={{0,2},{1,3},{2,0},{3,1},{4,6},{5,7},{6,4},{7,5},{8,10},{9,11},{10,... | collective-permute-start | bytes 9437192 | tf_op jit(solution)/shard_map/ppermute | solution.py:196
  255.1 593.3 %collective-permute-start.11 = (f32[24,128,256]{2,1,0:T(8,128)}, f32[24,128,256]{2,1,0:T(8,128)}, u32[]{:S(2)}, u32[]{:S(2)}) collective-permute-start(f32[24,128,256]{2,1,0:T(8,128)} %get-tuple-element.77), channel_id=1, source_target_pairs={{0,3},{1,0},{2,1},{3,2},{4,7},{5,4},{6,5},{7,6},{8,11},{9,8},{10,9... | collective-permute-start | bytes 9437192 | tf_op jit(solution)/shard_map/ppermute | solution.py:196
  381.6 505.6 %collective-permute-start.9 = (f32[24,128,256]{2,1,0:T(8,128)}, f32[24,128,256]{2,1,0:T(8,128)}, u32[]{:S(2)}, u32[]{:S(2)}) collective-permute-start(f32[24,128,256]{2,1,0:T(8,128)} %get-tuple-element.75), channel_id=1, source_target_pairs={{0,1},{1,2},{2,3},{3,0},{4,5},{5,6},{6,7},{7,4},{8,9},{9,10},{10,1... | collective-permute-start | bytes 9437192 | tf_op jit(solution)/shard_map/ppermute | solution.py:196
  617.3 281.4 %collective-permute-start.4 = (f32[24,128,256]{2,1,0:T(8,128)}, f32[24,128,256]{2,1,0:T(8,128)}, u32[]{:S(2)}, u32[]{:S(2)}) collective-permute-start(f32[24,128,256]{2,1,0:T(8,128)} %get-tuple-element.69), channel_id=1, source_target_pairs={{0,1},{1,2},{2,3},{3,0},{4,5},{5,6},{6,7},{7,4},{8,9},{9,10},{10,1... | collective-permute-start | bytes 9437192 | tf_op jit(solution)/shard_map/ppermute | solution.py:196
  618.2 426.1 %collective-permute-start.5 = (f32[24,128,256]{2,1,0:T(8,128)}, f32[24,128,256]{2,1,0:T(8,128)}, u32[]{:S(2)}, u32[]{:S(2)}) collective-permute-start(f32[24,128,256]{2,1,0:T(8,128)} %get-tuple-element.70), channel_id=1, source_target_pairs={{0,2},{1,3},{2,0},{3,1},{4,6},{5,7},{6,4},{7,5},{8,10},{9,11},{10,... | collective-permute-start | bytes 9437192 | tf_op jit(solution)/shard_map/ppermute | solution.py:196
  819.6 289.6 %collective-permute-start.6 = (f32[24,128,256]{2,1,0:T(8,128)}, f32[24,128,256]{2,1,0:T(8,128)}, u32[]{:S(2)}, u32[]{:S(2)}) collective-permute-start(f32[24,128,256]{2,1,0:T(8,128)} %get-tuple-element.71), channel_id=1, source_target_pairs={{0,3},{1,0},{2,1},{3,2},{4,7},{5,4},{6,5},{7,6},{8,11},{9,8},{10,9... | collective-permute-start | bytes 9437192 | tf_op jit(solution)/shard_map/ppermute | solution.py:196
  822.6 1.2 copy-start.5
  823.8 1.2 copy-start.9
  830.9 8.7 copy-start.4
  839.6 8.8 copy-start.13
  839.6 47.6 %copy-start.1 = (f32[24,128,256]{2,1,0:T(8,128)S(1)}, f32[24,128,256]{2,1,0:T(8,128)}, u32[]{:S(2)}) copy-start(f32[24,128,256]{2,1,0:T(8,128)} %get-tuple-element.147.refs_0_) | copy-start | bytes 9437188
  848.4 263.9 %collective-permute-start.21 = (f32[16,128,256]{2,1,0:T(8,128)S(1)}, f32[16,128,256]{2,1,0:T(8,128)S(1)}, u32[]{:S(2)}, u32[]{:S(2)}) collective-permute-start(f32[16,128,256]{2,1,0:T(8,128)S(1)} %copy-done.13), channel_id=1, source_target_pairs={{0,1},{1,2},{2,3},{3,0},{4,5},{5,6},{6,7},{7,4},{8,9},{9,10},{10,1... | collective-permute-start | bytes 6291464 | tf_op jit(solution)/shard_map/ppermute | solution.py:196
  887.3 359.3 %collective-permute-start.22 = (f32[16,128,256]{2,1,0:T(8,128)}, f32[16,128,256]{2,1,0:T(8,128)}, u32[]{:S(2)}, u32[]{:S(2)}) collective-permute-start(f32[16,128,256]{2,1,0:T(8,128)} %get-tuple-element.107), channel_id=1, source_target_pairs={{0,2},{1,3},{2,0},{3,1},{4,6},{5,7},{6,4},{7,5},{8,10},{9,11},{10,... | collective-permute-start | bytes 6291464 | tf_op jit(solution)/shard_map/ppermute | solution.py:196
  898.7 390.3 %collective-permute-start.23 = (f32[16,128,256]{2,1,0:T(8,128)}, f32[16,128,256]{2,1,0:T(8,128)}, u32[]{:S(2)}, u32[]{:S(2)}) collective-permute-start(f32[16,128,256]{2,1,0:T(8,128)} %get-tuple-element.108), channel_id=1, source_target_pairs={{0,3},{1,0},{2,1},{3,2},{4,7},{5,4},{6,5},{7,6},{8,11},{9,8},{10,9... | collective-permute-start | bytes 6291464 | tf_op jit(solution)/shard_map/ppermute | solution.py:196
  1044.3 247.8 %collective-permute-start.18 = (f32[16,128,256]{2,1,0:T(8,128)}, f32[16,128,256]{2,1,0:T(8,128)}, u32[]{:S(2)}, u32[]{:S(2)}) collective-permute-start(f32[16,128,256]{2,1,0:T(8,128)} %get-tuple-element.103), channel_id=1, source_target_pairs={{0,1},{1,2},{2,3},{3,0},{4,5},{5,6},{6,7},{7,4},{8,9},{9,10},{10,1... | collective-permute-start | bytes 6291464 | tf_op jit(solution)/shard_map/ppermute | solution.py:196
  1109.2 272.2 %collective-permute-start.19 = (f32[16,128,256]{2,1,0:T(8,128)}, f32[16,128,256]{2,1,0:T(8,128)}, u32[]{:S(2)}, u32[]{:S(2)}) collective-permute-start(f32[16,128,256]{2,1,0:T(8,128)} %get-tuple-element.104), channel_id=1, source_target_pairs={{0,2},{1,3},{2,0},{3,1},{4,6},{5,7},{6,4},{7,5},{8,10},{9,11},{10,... | collective-permute-start | bytes 6291464 | tf_op jit(solution)/shard_map/ppermute | solution.py:196
  1112.3 1.4 copy-start.6
  1113.7 267.7 %collective-permute-start.20 = (f32[16,128,256]{2,1,0:T(8,128)}, f32[16,128,256]{2,1,0:T(8,128)}, u32[]{:S(2)}, u32[]{:S(2)}) collective-permute-start(f32[16,128,256]{2,1,0:T(8,128)} %get-tuple-element.105), channel_id=1, source_target_pairs={{0,3},{1,0},{2,1},{3,2},{4,7},{5,4},{6,5},{7,6},{8,11},{9,8},{10,9... | collective-permute-start | bytes 6291464 | tf_op jit(solution)/shard_map/ppermute | solution.py:196
  1115.7 3.2 copy-start
  1118.8 175.1 %copy-start.3 = (f32[16,128,256]{2,1,0:T(8,128)S(1)}, f32[16,128,256]{2,1,0:T(8,128)}, u32[]{:S(2)}) copy-start(f32[16,128,256]{2,1,0:T(8,128)} %get-tuple-element.132.refs_0_) | copy-start | bytes 6291460
  1118.8 175.1 %copy-start.7 = (f32[16,128,256]{2,1,0:T(8,128)S(1)}, f32[16,128,256]{2,1,0:T(8,128)}, u32[]{:S(2)}) copy-start(f32[16,128,256]{2,1,0:T(8,128)} %copy-done.6) | copy-start | bytes 6291460
  1246.6 143.6 %collective-permute-start.15 = (f32[8,128,256]{2,1,0:T(8,128)S(1)}, f32[8,128,256]{2,1,0:T(8,128)S(1)}, u32[]{:S(2)}, u32[]{:S(2)}) collective-permute-start(f32[8,128,256]{2,1,0:T(8,128)S(1)} %get-tuple-element.99), channel_id=1, source_target_pairs={{0,1},{1,2},{2,3},{3,0},{4,5},{5,6},{6,7},{7,4},{8,9},{9,10},{10,1... | collective-permute-start | bytes 3145736 | tf_op jit(solution)/shard_map/ppermute | solution.py:196
  1289.0 159.8 %collective-permute-start.16 = (f32[8,128,256]{2,1,0:T(8,128)S(1)}, f32[8,128,256]{2,1,0:T(8,128)S(1)}, u32[]{:S(2)}, u32[]{:S(2)}) collective-permute-start(f32[8,128,256]{2,1,0:T(8,128)S(1)} %get-tuple-element.100), channel_id=1, source_target_pairs={{0,2},{1,3},{2,0},{3,1},{4,6},{5,7},{6,4},{7,5},{8,10},{9,11},{10,... | collective-permute-start | bytes 3145736 | tf_op jit(solution)/shard_map/ppermute | solution.py:196
  1292.1 156.7 %collective-permute-start.17 = (f32[8,128,256]{2,1,0:T(8,128)S(1)}, f32[8,128,256]{2,1,0:T(8,128)S(1)}, u32[]{:S(2)}, u32[]{:S(2)}) collective-permute-start(f32[8,128,256]{2,1,0:T(8,128)S(1)} %get-tuple-element.101), channel_id=1, source_target_pairs={{0,3},{1,0},{2,1},{3,2},{4,7},{5,4},{6,5},{7,6},{8,11},{9,8},{10,9... | collective-permute-start | bytes 3145736 | tf_op jit(solution)/shard_map/ppermute | solution.py:196
  1293.9 87.5 %copy-start.2 = (f32[16,128,256]{2,1,0:T(8,128)S(1)}, f32[16,128,256]{2,1,0:T(8,128)}, u32[]{:S(2)}) copy-start(f32[16,128,256]{2,1,0:T(8,128)} %get-tuple-element.133.refs_0_) | copy-start | bytes 6291460
  1546.9 32.9 %copy-start.10 = (f32[128,1024]{1,0:T(8,128)}, f32[128,1024]{1,0:T(8,128)S(1)}, u32[]{:S(2)}) copy-start(f32[128,1024]{1,0:T(8,128)S(1)} %get-tuple-element.125.iterate) | copy-start | bytes 1572868
  1579.8 1.0 copy-start.11
  1618.2 0.8 copy-start.12
  1621.8 23.5 %all-to-all-start.4 = ((f32[32,17,256]{2,1,0:T(8,128)}), f32[32,17,256]{2,1,0:T(8,128)S(1)}, u32[]{:S(2)}, u32[]{:S(2)}) async-start(f32[32,17,256]{2,1,0:T(8,128)} %bitcast.51), calls=%async_computation.4 | async-start | bytes 1572864 | tf_op jit(solution)/shard_map/all_to_all | solution.py:170

commit v6 on v5

--- a/solution.py
+++ b/solution.py
@@ -9,7 +9,6 @@
 
 ITERS = 3
 PARTS = (1, 2, 2, 3, 3, 2, 2, 1)
-CARRIER = 2
 DEPTH = 3
 BF16 = jnp.bfloat16
 F32 = jnp.float32
@@ -184,13 +183,12 @@
     mine = occupied_energy.shape[0]
     me = lax.axis_index("vir")
 
-    def start_and_gaps(earlier):
-        first, occupied, _ = lax.optimization_barrier((right_side, occupied_energy, earlier))
+    def start_and_gaps(known):
         rows = jnp.concatenate(
-            [first.T, jnp.broadcast_to(occupied[:, None], (mine, 128))], axis=1
+            [known[:mine], jnp.broadcast_to(occupied_energy[:, None], (mine, 128))], axis=1
         )
         rows = lax.all_gather(rows, "aux", axis=0, tiled=True)
-        return jnp.stack([rows[:, :width], virtual_energy[None, :] - rows[:, width : width + 1]])
+        return rows[:, :whole], known[mine:] - rows[:, whole : whole + 1]
 
     def shifted(array, shift):
         return lax.ppermute(array, "vir", [(z, (z + shift) % groups) for z in range(groups)])
@@ -198,7 +196,10 @@
     def by_source(pieces):
         turned = pieces[:0:-1] + pieces[:1]
         twice = jnp.concatenate(turned + turned[:-1], axis=1)
-        return lax.dynamic_slice(twice, (0, (groups - 1 - me) * width), (occ, whole))
+        return lax.dynamic_slice(twice, (0, (groups - 1 - me) * width), (mine + 1, whole))
+
+    rows = jnp.concatenate([right_side.T, virtual_energy[None, :]], axis=0)
+    known = by_source([rows] + [shifted(rows, n) for n in range(1, groups)])
 
     received = []
     held = start = None
@@ -212,7 +213,7 @@
 
     for k, share in enumerate(PARTS):
         count = share * unit
-        if k == CARRIER:
+        if k == 2:
             integrals, _ = lax.optimization_barrier((integrals, received[0][1]))
         blocks = [
             lax.dynamic_slice_in_dim(
@@ -224,23 +225,16 @@
         if k == 0:
             blocks, integrals = lax.optimization_barrier((blocks, integrals))
         sent = blocks[1:]
-        if k == CARRIER:
-            carried = start_and_gaps(received[0][1])
-            sent = [jnp.concatenate([block, carried], axis=0) for block in sent]
+        if k == 2:
+            sent, known = lax.optimization_barrier((sent, known))
+        if k == DEPTH:
+            start, gap = start_and_gaps(known)
         if k >= DEPTH:
-            while start is not None and k - DEPTH >= CARRIER and applied <= k - DEPTH:
-                apply_part()
-            if held is None:
-                sent, _ = lax.optimization_barrier((sent, received[k - DEPTH]))
-            else:
-                total, high, low = held
-                sent, total, start, gap = lax.optimization_barrier((sent, total, start, gap))
-                held = total, high, low
-        arrived = [shifted(block, n) for n, block in enumerate(sent, 1)]
-        received.append(blocks[:1] + arrived)
-        if k == CARRIER:
-            own_and_others = [carried] + [piece[count:] for piece in arrived]
-            start, gap = (by_source([piece[n] for piece in own_and_others]) for n in range(2))
+            apply_part()
+            total, high, low = held
+            sent, total, start, gap = lax.optimization_barrier((sent, total, start, gap))
+            held = total, high, low
+        received.append(blocks[:1] + [shifted(block, n) for n, block in enumerate(sent, 1)])
     while applied < len(PARTS):
         apply_part()
     total, high, low = held

time: 1650 us -> 1640 us (level)
  waiting for transfers between devices: 802 us -> 478 us
  starting transfers between devices: 528 us -> 844 us
    ppermute x24 -> x27, waiting for transfers between devices: 782 us -> 458 us  [shifted(): lax.ppermute(array, 'vir', [(z, (z + shift) % groups) for z in range(grou...]
    ppermute x24 -> x27, starting transfers between devices: 525 us -> 841 us  [shifted(): lax.ppermute(array, 'vir', [(z, (z + shift) % groups) for z in range(grou...]
  transfers between devices with their start and end apart: 25 -> 28, of which waited for: 9 -> 7; matrix products, arithmetic and copies ran while one was open for 4% -> 3% of each run, Pallas kernels for 4% -> 4%
where the time goes in v6:
time: 1640 us; the launch traced here: 1630 us
  starting transfers between devices  844 us (51%)
  waiting for transfers between devices  478 us (29%)
  Pallas kernels  142 us (9%)
  blocking collectives  105 us (6%)
  local copies, waits for them, and re-layouts  55.9 us (3%)
    ppermute x27, starting transfers between devices, shifted(): lax.ppermute(array, 'vir', [(z, (z + shift) % groups) for z in range(grou...  841 us
    ppermute x27, waiting for transfers between devices, shifted(): lax.ppermute(array, 'vir', [(z, (z + shift) % groups) for z in range(grou...  458 us
    pallas_call x2, Pallas kernels, later_apply(): pl.pallas_call(later_kernel, grid=(held // step,), in_specs=[block, block...  74.8 us
    pallas_call x8, Pallas kernels, first_part(): pl.pallas_call(functools.partial(first_kernel, first, groups), grid=(coun...  66.9 us
    all_to_all x4, blocking collectives, add_over(): lax.all_to_all(pieces, axes, split_axis=0, concat_axis=0, tiled=True)  62.5 us
    dynamic_slice x5, local copies, waits for them, and re-layouts, on_device(): lax.dynamic_slice_in_dim(integrals, low_row + lax.rem(me + shift, groups)...  47 us
  transfers between devices with their start and end apart: 28, of which 7 were waited for; matrix products, arithmetic and copies ran while one was open for 3% of the time, Pallas kernels for 4%

profile of v6, /device:TPU:1, one launch (start us, length us, event | category | flops | bytes accessed | tf_op | source)
XLA Modules:
  0.0 1630.9 jit_solution(16522879646567834842)
XLA Ops:
  1.4 4.2 collective-permute-start.6
  6.0 3.9 constant_dynamic-slice_fusion.29
  9.9 2.2 collective-permute-start
  13.0 7.0 constant_dynamic-slice_fusion.17
  21.5 1.5 collective-permute-start.2
  23.0 12.1 collective-permute-done.refs_1_
  36.3 17.1 %constant_dynamic-slice_fusion = (f32[16,128,256]{2,1,0:T(8,128)}, f32[16,128,256]{2,1,0:T(8,128)}, f32[16,128,256]{2,1,0:T(8,128)}, f32[16,128,256]{2,1,0:T(8,1...) fusion(f32[512,128,256]{2,1,0:T(8,128)} %param.4, ...), kind=kLoop, calls=%fused_computation.20 | loop fusion | bytes 50331696 | tf_op jit(solution)/shard_map/dynamic_slice | solution.py:219
  53.6 15.5 all_gather.9
  69.4 16.2 constant_dynamic-slice_fusion.6
  85.6 38.9 %collective-permute-start.15 = (f32[16,128,256]{2,1,0:T(8,128)}, f32[16,128,256]{2,1,0:T(8,128)S(1)}, u32[]{:S(2)}, u32[]{:S(2)}) collective-permute-start(f32[16,128,256]{2,1,0:T(8,128)} %get-tuple-element.94), channel_id=1, source_target_pairs={{0,1},{1,2},{2,3},{3,0},{4,5},{5,6},{6,7},{7,4},{8,9},{9,10},{10,1... | collective-permute-start | bytes 6291464 | tf_op jit(solution)/shard_map/ppermute | solution.py:194
  125.8 5.9 shard_map.59
  131.7 70.2 %collective-permute-start.12 = (f32[24,128,256]{2,1,0:T(8,128)}, f32[24,128,256]{2,1,0:T(8,128)}, u32[]{:S(2)}, u32[]{:S(2)}) collective-permute-start(f32[24,128,256]{2,1,0:T(8,128)} %get-tuple-element.91), channel_id=1, source_target_pairs={{0,1},{1,2},{2,3},{3,0},{4,5},{5,6},{6,7},{7,4},{8,9},{9,10},{10,1... | collective-permute-start | bytes 9437192 | tf_op jit(solution)/shard_map/ppermute | solution.py:194
  201.9 35.9 %collective-permute-start.16 = (f32[16,128,256]{2,1,0:T(8,128)}, f32[16,128,256]{2,1,0:T(8,128)}, u32[]{:S(2)}, u32[]{:S(2)}) collective-permute-start(f32[16,128,256]{2,1,0:T(8,128)} %get-tuple-element.95), channel_id=1, source_target_pairs={{0,2},{1,3},{2,0},{3,1},{4,6},{5,7},{6,4},{7,5},{8,10},{9,11},{10,... | collective-permute-start | bytes 6291464 | tf_op jit(solution)/shard_map/ppermute | solution.py:194
  237.8 158.9 %collective-permute-done.2.refs_2_ = f32[16,128,256]{2,1,0:T(8,128)} collective-permute-done((f32[16,128,256]{2,1,0:T(8,128)}, f32[16,128,256]{2,1,0:T(8,128)}, u32[]{:S(2)}, u32[]{:S(2)}) %collective-permute-start.2) | collective-permute-done | bytes 2097184 | tf_op jit(solution)/shard_map/ppermute | solution.py:194
  396.7 44.2 %collective-permute-start.13 = (f32[24,128,256]{2,1,0:T(8,128)}, f32[24,128,256]{2,1,0:T(8,128)}, u32[]{:S(2)}, u32[]{:S(2)}) collective-permute-start(f32[24,128,256]{2,1,0:T(8,128)} %get-tuple-element.92), channel_id=1, source_target_pairs={{0,2},{1,3},{2,0},{3,1},{4,6},{5,7},{6,4},{7,5},{8,10},{9,11},{10,... | collective-permute-start | bytes 9437192 | tf_op jit(solution)/shard_map/ppermute | solution.py:194
  442.2 3.1 collective-permute-start.14
  445.3 8.7 shard_map.60
  454.0 100.1 %collective-permute-done.16.refs_2_ = f32[16,128,256]{2,1,0:T(8,128)} collective-permute-done((f32[16,128,256]{2,1,0:T(8,128)}, f32[16,128,256]{2,1,0:T(8,128)}, u32[]{:S(2)}, u32[]{:S(2)}) %collective-permute-start.16) | collective-permute-done | bytes 2097184 | tf_op jit(solution)/shard_map/ppermute | solution.py:194
  554.1 179.0 %collective-permute-start.11 = (f32[24,128,256]{2,1,0:T(8,128)}, f32[24,128,256]{2,1,0:T(8,128)}, u32[]{:S(2)}, u32[]{:S(2)}) collective-permute-start(f32[24,128,256]{2,1,0:T(8,128)} %get-tuple-element.90), channel_id=1, source_target_pairs={{0,3},{1,0},{2,1},{3,2},{4,7},{5,4},{6,5},{7,6},{8,11},{9,8},{10,9... | collective-permute-start | bytes 9437192 | tf_op jit(solution)/shard_map/ppermute | solution.py:194
  733.7 8.4 shard_map.61
  742.1 123.1 %collective-permute-start.24 = (f32[16,128,256]{2,1,0:T(8,128)S(1)}, f32[16,128,256]{2,1,0:T(8,128)S(1)}, u32[]{:S(2)}, u32[]{:S(2)}) collective-permute-start(f32[16,128,256]{2,1,0:T(8,128)S(1)} %copy-done.15), channel_id=1, source_target_pairs={{0,1},{1,2},{2,3},{3,0},{4,5},{5,6},{6,7},{7,4},{8,9},{9,10},{10,1... | collective-permute-start | bytes 6291464 | tf_op jit(solution)/shard_map/ppermute | solution.py:194
  865.2 3.1 collective-permute-start.25
  868.3 11.4 shard_map.62
  879.7 100.6 %collective-permute-start.26 = (f32[16,128,256]{2,1,0:T(8,128)}, f32[16,128,256]{2,1,0:T(8,128)}, u32[]{:S(2)}, u32[]{:S(2)}) collective-permute-start(f32[16,128,256]{2,1,0:T(8,128)} %get-tuple-element.124), channel_id=1, source_target_pairs={{0,3},{1,0},{2,1},{3,2},{4,7},{5,4},{6,5},{7,6},{8,11},{9,8},{10,9... | collective-permute-start | bytes 6291464 | tf_op jit(solution)/shard_map/ppermute | solution.py:194
  980.3 158.4 %collective-permute-start.21 = (f32[16,128,256]{2,1,0:T(8,128)}, f32[16,128,256]{2,1,0:T(8,128)}, u32[]{:S(2)}, u32[]{:S(2)}) collective-permute-start(f32[16,128,256]{2,1,0:T(8,128)} %get-tuple-element.119), channel_id=1, source_target_pairs={{0,1},{1,2},{2,3},{3,0},{4,5},{5,6},{6,7},{7,4},{8,9},{9,10},{10,1... | collective-permute-start | bytes 6291464 | tf_op jit(solution)/shard_map/ppermute | solution.py:194
  1140.0 2.1 collective-permute-start.23
  1142.1 2.7 constant_dynamic-slice_fusion.25
  1145.2 11.6 shard_map.63
  1156.8 71.5 %collective-permute-done.25.refs_2_ = f32[16,128,256]{2,1,0:T(8,128)} collective-permute-done((f32[16,128,256]{2,1,0:T(8,128)}, f32[16,128,256]{2,1,0:T(8,128)}, u32[]{:S(2)}, u32[]{:S(2)}) %collective-permute-start.25) | collective-permute-done | bytes 2097184 | tf_op jit(solution)/shard_map/ppermute | solution.py:194
  1228.3 66.7 %collective-permute-start.19 = (f32[8,128,256]{2,1,0:T(8,128)S(1)}, f32[8,128,256]{2,1,0:T(8,128)S(1)}, u32[]{:S(2)}, u32[]{:S(2)}) collective-permute-start(f32[8,128,256]{2,1,0:T(8,128)S(1)} %get-tuple-element.116), channel_id=1, source_target_pairs={{0,2},{1,3},{2,0},{3,1},{4,6},{5,7},{6,4},{7,5},{8,10},{9,11},{10,... | collective-permute-start | bytes 3145736 | tf_op jit(solution)/shard_map/ppermute | solution.py:194
  1295.0 3.3 collective-permute-start.20
  1298.3 8.4 shard_map.64
  1306.7 56.5 %collective-permute-done.22.refs_2_ = f32[16,128,256]{2,1,0:T(8,128)} collective-permute-done((f32[16,128,256]{2,1,0:T(8,128)}, f32[16,128,256]{2,1,0:T(8,128)}, u32[]{:S(2)}, u32[]{:S(2)}) %collective-permute-start.22) | collective-permute-done | bytes 2097184 | tf_op jit(solution)/shard_map/ppermute | solution.py:194
  1363.2 8.7 shard_map.65
  1371.9 58.6 %collective-permute-done.19.refs_2_ = f32[8,128,256]{2,1,0:T(8,128)S(1)} collective-permute-done((f32[8,128,256]{2,1,0:T(8,128)S(1)}, f32[8,128,256]{2,1,0:T(8,128)S(1)}, u32[]{:S(2)}, u32[]{:S(2)}) %collective-permute-start.19) | collective-permute-done | bytes 1048608 | tf_op jit(solution)/shard_map/ppermute | solution.py:194
  1430.5 3.8 shard_map.66
  1434.2 12.5 all_to_all.25
  1446.8 30.4 %all_to_all.26 = f32[4,16,1024]{2,1,0:T(8,128)S(1)} all-to-all(f32[4,16,1024]{2,1,0:T(8,128)S(1)} %broadcast_in_dim.12), channel_id=1, replica_groups=mesh['aux'=8,'vir'=4] {'vir'}, dimensions={0} | all-to-all | bytes 524288 | tf_op jit(solution)/shard_map/all_to_all | solution.py:169
  1477.3 13.5 all_gather.10.summed
  1490.9 37.4 %shard_map.67 = (f32[128,1024]{1,0:T(8,128)S(1)}, f32[128,1024]{1,0:T(8,128)S(1)}, f32[128,1024]{1,0:T(8,128)S(1)}, f32[128,1024]{1,0:T(8,128)S(1)}) custom-call(bf16[128,128,1024]{2,1,0:T(8,128)(2,1)} %get-tuple-element.134.high_ref, bf16[128,128,1024]{2,1,0:T(8,128)(2,1)} %get-tuple-element.135.low_ref, f32[128,1024]{1,0:T(8,128)S(1)} %all_gather.10.summed, ...), custom_call_target="tpu_custom_call" | custom-call | tf_op jit(solution)/shard_map/pallas_call | solution.py:157
  1528.3 11.1 all_to_all.27
  1539.4 8.4 all_to_all.28
  1547.9 13.3 all_gather.11.summed
  1562.2 37.4 %shard_map.68 = (f32[128,1024]{1,0:T(8,128)S(1)}, f32[128,1024]{1,0:T(8,128)S(1)}, f32[128,1024]{1,0:T(8,128)S(1)}, f32[128,1024]{1,0:T(8,128)S(1)}) custom-call(bf16[128,128,1024]{2,1,0:T(8,128)(2,1)} %get-tuple-element.134.high_ref, bf16[128,128,1024]{2,1,0:T(8,128)(2,1)} %get-tuple-element.135.low_ref, f32[128,1024]{1,0:T(8,128)S(1)} %all_gather.11.summed, ...), custom_call_target="tpu_custom_call" | custom-call | tf_op jit(solution)/shard_map/pallas_call | solution.py:157
  1601.6 1.6 concatenate.15.clone
  1603.2 2.6 all-to-all-start.4
  1606.6 20.1 %all-to-all-done.4 = f32[32,17,256]{2,1,0:T(8,128)S(1)} async-done(((f32[32,17,256]{2,1,0:T(8,128)}), f32[32,17,256]{2,1,0:T(8,128)S(1)}, u32[]{:S(2)}, u32[]{:S(2)}) %all-to-all-start.4) | async-done | bytes 557088 | tf_op jit(solution)/shard_map/all_to_all | solution.py:169
  1629.1 1.3 fusion.3
  (99 shorter events, 14.4 us)
Async XLA Ops:
  1.4 18.6 %collective-permute-start.6 = (f32[17,256]{1,0:T(8,128)S(1)}, f32[17,256]{1,0:T(8,128)S(1)}, u32[]{:S(2)}, u32[]{:S(2)}) collective-permute-start(f32[17,256]{1,0:T(8,128)S(1)} %pad_maximum_fusion.1), channel_id=1, source_target_pairs={{0,3},{1,0},{2,1},{3,2},{4,7},{5,4},{6,5},{7,6},{8,11},{9,8},{10,9... | collective-permute-start | bytes 52232 | tf_op jit(solution)/shard_map/ppermute | solution.py:194
  5.5 15.7 collective-permute-start.7
  5.5 16.0 collective-permute-start.8
  9.9 25.2 %collective-permute-start = (f32[8,128,256]{2,1,0:T(8,128)}, f32[8,128,256]{2,1,0:T(8,128)S(1)}, u32[]{:S(2)}, u32[]{:S(2)}) collective-permute-start(f32[8,128,256]{2,1,0:T(8,128)} %get-tuple-element.75), channel_id=1, source_target_pairs={{0,1},{1,2},{2,3},{3,0},{4,5},{5,6},{6,7},{7,4},{8,9},{9,10},{10,1... | collective-permute-start | bytes 3145736 | tf_op jit(solution)/shard_map/ppermute | solution.py:194
  12.1 73.5 %collective-permute-start.4 = (f32[8,128,256]{2,1,0:T(8,128)}, f32[8,128,256]{2,1,0:T(8,128)}, u32[]{:S(2)}, u32[]{:S(2)}) collective-permute-start(f32[8,128,256]{2,1,0:T(8,128)} %get-tuple-element.78), channel_id=1, source_target_pairs={{0,2},{1,3},{2,0},{3,1},{4,6},{5,7},{6,4},{7,5},{8,10},{9,11},{10,... | collective-permute-start | bytes 3145736 | tf_op jit(solution)/shard_map/ppermute | solution.py:194
  13.0 10.0 copy-start.16
  13.0 10.0 copy-start.17
  20.0 104.6 %collective-permute-start.5 = (f32[8,128,256]{2,1,0:T(8,128)}, f32[8,128,256]{2,1,0:T(8,128)}, u32[]{:S(2)}, u32[]{:S(2)}) collective-permute-start(f32[8,128,256]{2,1,0:T(8,128)} %get-tuple-element.79), channel_id=1, source_target_pairs={{0,3},{1,0},{2,1},{3,2},{4,7},{5,4},{6,5},{7,6},{8,11},{9,8},{10,9... | collective-permute-start | bytes 3145736 | tf_op jit(solution)/shard_map/ppermute | solution.py:194
  21.2 180.7 %collective-permute-start.1 = (f32[16,128,256]{2,1,0:T(8,128)}, f32[16,128,256]{2,1,0:T(8,128)}, u32[]{:S(2)}, u32[]{:S(2)}) collective-permute-start(f32[16,128,256]{2,1,0:T(8,128)} %get-tuple-element.170), channel_id=1, source_target_pairs={{0,1},{1,2},{2,3},{3,0},{4,5},{5,6},{6,7},{7,4},{8,9},{9,10},{10,1... | collective-permute-start | bytes 6291464 | tf_op jit(solution)/shard_map/ppermute | solution.py:194
  21.5 375.2 %collective-permute-start.2 = (f32[16,128,256]{2,1,0:T(8,128)}, f32[16,128,256]{2,1,0:T(8,128)}, u32[]{:S(2)}, u32[]{:S(2)}) collective-permute-start(f32[16,128,256]{2,1,0:T(8,128)} %get-tuple-element.169), channel_id=1, source_target_pairs={{0,2},{1,3},{2,0},{3,1},{4,6},{5,7},{6,4},{7,5},{8,10},{9,11},{10,... | collective-permute-start | bytes 6291464 | tf_op jit(solution)/shard_map/ppermute | solution.py:194
  35.1 18.3 %copy-start.9 = (f32[8,128,256]{2,1,0:T(8,128)}, f32[8,128,256]{2,1,0:T(8,128)S(1)}, u32[]{:S(2)}) copy-start(f32[8,128,256]{2,1,0:T(8,128)S(1)} %collective-permute-done.refs_1_) | copy-start | bytes 3145732
  35.1 18.4 %copy-start.18 = (f32[16]{0:T(128)S(1)}, f32[16]{0:T(128)}, u32[]{:S(2)}) copy-start(f32[16]{0:T(128)} %param.5) | copy-start | bytes 196
  35.1 361.6 %collective-permute-start.3 = (f32[16,128,256]{2,1,0:T(8,128)}, f32[16,128,256]{2,1,0:T(8,128)}, u32[]{:S(2)}, u32[]{:S(2)}) collective-permute-start(f32[16,128,256]{2,1,0:T(8,128)} %get-tuple-element.168), channel_id=1, source_target_pairs={{0,3},{1,0},{2,1},{3,2},{4,7},{5,4},{6,5},{7,6},{8,11},{9,8},{10,9... | collective-permute-start | bytes 6291464 | tf_op jit(solution)/shard_map/ppermute | solution.py:194
  85.6 359.7 %copy-start.1 = (f32[16,128,256]{2,1,0:T(8,128)S(1)}, f32[16,128,256]{2,1,0:T(8,128)}, u32[]{:S(2)}) copy-start(f32[16,128,256]{2,1,0:T(8,128)} %get-tuple-element.171.refs_0_) | copy-start | bytes 6291460
  85.6 355.3 %collective-permute-start.15 = (f32[16,128,256]{2,1,0:T(8,128)}, f32[16,128,256]{2,1,0:T(8,128)S(1)}, u32[]{:S(2)}, u32[]{:S(2)}) collective-permute-start(f32[16,128,256]{2,1,0:T(8,128)} %get-tuple-element.94), channel_id=1, source_target_pairs={{0,1},{1,2},{2,3},{3,0},{4,5},{5,6},{6,7},{7,4},{8,9},{9,10},{10,1... | collective-permute-start | bytes 6291464 | tf_op jit(solution)/shard_map/ppermute | solution.py:194
  124.6 1.2 copy-start.10
  131.7 601.4 %collective-permute-start.12 = (f32[24,128,256]{2,1,0:T(8,128)}, f32[24,128,256]{2,1,0:T(8,128)}, u32[]{:S(2)}, u32[]{:S(2)}) collective-permute-start(f32[24,128,256]{2,1,0:T(8,128)} %get-tuple-element.91), channel_id=1, source_target_pairs={{0,1},{1,2},{2,3},{3,0},{4,5},{5,6},{6,7},{7,4},{8,9},{9,10},{10,1... | collective-permute-start | bytes 9437192 | tf_op jit(solution)/shard_map/ppermute | solution.py:194
  201.9 352.2 %collective-permute-start.16 = (f32[16,128,256]{2,1,0:T(8,128)}, f32[16,128,256]{2,1,0:T(8,128)}, u32[]{:S(2)}, u32[]{:S(2)}) collective-permute-start(f32[16,128,256]{2,1,0:T(8,128)} %get-tuple-element.95), channel_id=1, source_target_pairs={{0,2},{1,3},{2,0},{3,1},{4,6},{5,7},{6,4},{7,5},{8,10},{9,11},{10,... | collective-permute-start | bytes 6291464 | tf_op jit(solution)/shard_map/ppermute | solution.py:194
  396.7 157.4 %collective-permute-start.17 = (f32[16,128,256]{2,1,0:T(8,128)}, f32[16,128,256]{2,1,0:T(8,128)}, u32[]{:S(2)}, u32[]{:S(2)}) collective-permute-start(f32[16,128,256]{2,1,0:T(8,128)} %get-tuple-element.96), channel_id=1, source_target_pairs={{0,3},{1,0},{2,1},{3,2},{4,7},{5,4},{6,5},{7,6},{8,11},{9,8},{10,9... | collective-permute-start | bytes 6291464 | tf_op jit(solution)/shard_map/ppermute | solution.py:194
  396.7 345.4 %collective-permute-start.13 = (f32[24,128,256]{2,1,0:T(8,128)}, f32[24,128,256]{2,1,0:T(8,128)}, u32[]{:S(2)}, u32[]{:S(2)}) collective-permute-start(f32[24,128,256]{2,1,0:T(8,128)} %get-tuple-element.92), channel_id=1, source_target_pairs={{0,2},{1,3},{2,0},{3,1},{4,6},{5,7},{6,4},{7,5},{8,10},{9,11},{10,... | collective-permute-start | bytes 9437192 | tf_op jit(solution)/shard_map/ppermute | solution.py:194
  440.9 1.3 copy-start.7
  442.2 423.0 %collective-permute-start.14 = (f32[24,128,256]{2,1,0:T(8,128)}, f32[24,128,256]{2,1,0:T(8,128)}, u32[]{:S(2)}, u32[]{:S(2)}) collective-permute-start(f32[24,128,256]{2,1,0:T(8,128)} %get-tuple-element.93), channel_id=1, source_target_pairs={{0,3},{1,0},{2,1},{3,2},{4,7},{5,4},{6,5},{7,6},{8,11},{9,8},{10,9... | collective-permute-start | bytes 9437192 | tf_op jit(solution)/shard_map/ppermute | solution.py:194
  445.3 288.3 %copy-start.4 = (f32[16,128,256]{2,1,0:T(8,128)S(1)}, f32[16,128,256]{2,1,0:T(8,128)}, u32[]{:S(2)}) copy-start(f32[16,128,256]{2,1,0:T(8,128)} %get-tuple-element.150.refs_0_) | copy-start | bytes 6291460
  445.3 288.3 %copy-start.8 = (f32[16,128,256]{2,1,0:T(8,128)S(1)}, f32[16,128,256]{2,1,0:T(8,128)}, u32[]{:S(2)}) copy-start(f32[16,128,256]{2,1,0:T(8,128)} %copy-done.7) | copy-start | bytes 6291460
  554.1 325.6 %collective-permute-start.10 = (f32[24,128,256]{2,1,0:T(8,128)}, f32[24,128,256]{2,1,0:T(8,128)S(1)}, u32[]{:S(2)}, u32[]{:S(2)}) collective-permute-start(f32[24,128,256]{2,1,0:T(8,128)} %get-tuple-element.89), channel_id=1, source_target_pairs={{0,2},{1,3},{2,0},{3,1},{4,6},{5,7},{6,4},{7,5},{8,10},{9,11},{10,... | collective-permute-start | bytes 9437192 | tf_op jit(solution)/shard_map/ppermute | solution.py:194
  554.1 426.2 %collective-permute-start.11 = (f32[24,128,256]{2,1,0:T(8,128)}, f32[24,128,256]{2,1,0:T(8,128)}, u32[]{:S(2)}, u32[]{:S(2)}) collective-permute-start(f32[24,128,256]{2,1,0:T(8,128)} %get-tuple-element.90), channel_id=1, source_target_pairs={{0,3},{1,0},{2,1},{3,2},{4,7},{5,4},{6,5},{7,6},{8,11},{9,8},{10,9... | collective-permute-start | bytes 9437192 | tf_op jit(solution)/shard_map/ppermute | solution.py:194
  733.1 405.5 %collective-permute-start.9 = (f32[24,128,256]{2,1,0:T(8,128)}, f32[24,128,256]{2,1,0:T(8,128)}, u32[]{:S(2)}, u32[]{:S(2)}) collective-permute-start(f32[24,128,256]{2,1,0:T(8,128)} %get-tuple-element.88), channel_id=1, source_target_pairs={{0,1},{1,2},{2,3},{3,0},{4,5},{5,6},{6,7},{7,4},{8,9},{9,10},{10,1... | collective-permute-start | bytes 9437192 | tf_op jit(solution)/shard_map/ppermute | solution.py:194
  733.7 8.4 copy-start.15
  742.1 396.6 %collective-permute-start.24 = (f32[16,128,256]{2,1,0:T(8,128)S(1)}, f32[16,128,256]{2,1,0:T(8,128)S(1)}, u32[]{:S(2)}, u32[]{:S(2)}) collective-permute-start(f32[16,128,256]{2,1,0:T(8,128)S(1)} %copy-done.15), channel_id=1, source_target_pairs={{0,1},{1,2},{2,3},{3,0},{4,5},{5,6},{6,7},{7,4},{8,9},{9,10},{10,1... | collective-permute-start | bytes 6291464 | tf_op jit(solution)/shard_map/ppermute | solution.py:194
  865.2 363.1 %collective-permute-start.25 = (f32[16,128,256]{2,1,0:T(8,128)}, f32[16,128,256]{2,1,0:T(8,128)}, u32[]{:S(2)}, u32[]{:S(2)}) collective-permute-start(f32[16,128,256]{2,1,0:T(8,128)} %get-tuple-element.123), channel_id=1, source_target_pairs={{0,2},{1,3},{2,0},{3,1},{4,6},{5,7},{6,4},{7,5},{8,10},{9,11},{10,... | collective-permute-start | bytes 6291464 | tf_op jit(solution)/shard_map/ppermute | solution.py:194
  879.7 259.0 %copy-start.14 = (f32[24,128,256]{2,1,0:T(8,128)}, f32[24,128,256]{2,1,0:T(8,128)S(1)}, u32[]{:S(2)}) copy-start(f32[24,128,256]{2,1,0:T(8,128)S(1)} %collective-permute-done.10.refs_2_) | copy-start | bytes 9437188
  879.7 348.6 %collective-permute-start.26 = (f32[16,128,256]{2,1,0:T(8,128)}, f32[16,128,256]{2,1,0:T(8,128)}, u32[]{:S(2)}, u32[]{:S(2)}) collective-permute-start(f32[16,128,256]{2,1,0:T(8,128)} %get-tuple-element.124), channel_id=1, source_target_pairs={{0,3},{1,0},{2,1},{3,2},{4,7},{5,4},{6,5},{7,6},{8,11},{9,8},{10,9... | collective-permute-start | bytes 6291464 | tf_op jit(solution)/shard_map/ppermute | solution.py:194
  980.3 314.7 %collective-permute-start.21 = (f32[16,128,256]{2,1,0:T(8,128)}, f32[16,128,256]{2,1,0:T(8,128)}, u32[]{:S(2)}, u32[]{:S(2)}) collective-permute-start(f32[16,128,256]{2,1,0:T(8,128)} %get-tuple-element.119), channel_id=1, source_target_pairs={{0,1},{1,2},{2,3},{3,0},{4,5},{5,6},{6,7},{7,4},{8,9},{9,10},{10,1... | collective-permute-start | bytes 6291464 | tf_op jit(solution)/shard_map/ppermute | solution.py:194
  1138.7 224.5 %collective-permute-start.22 = (f32[16,128,256]{2,1,0:T(8,128)}, f32[16,128,256]{2,1,0:T(8,128)}, u32[]{:S(2)}, u32[]{:S(2)}) collective-permute-start(f32[16,128,256]{2,1,0:T(8,128)} %get-tuple-element.120), channel_id=1, source_target_pairs={{0,2},{1,3},{2,0},{3,1},{4,6},{5,7},{6,4},{7,5},{8,10},{9,11},{10,... | collective-permute-start | bytes 6291464 | tf_op jit(solution)/shard_map/ppermute | solution.py:194
  1138.7 1.3 copy-start.5
  1140.0 223.2 %collective-permute-start.23 = (f32[16,128,256]{2,1,0:T(8,128)}, f32[16,128,256]{2,1,0:T(8,128)}, u32[]{:S(2)}, u32[]{:S(2)}) collective-permute-start(f32[16,128,256]{2,1,0:T(8,128)} %get-tuple-element.121), channel_id=1, source_target_pairs={{0,3},{1,0},{2,1},{3,2},{4,7},{5,4},{6,5},{7,6},{8,11},{9,8},{10,9... | collective-permute-start | bytes 6291464 | tf_op jit(solution)/shard_map/ppermute | solution.py:194
  1142.1 3.2 copy-start
  1145.2 153.1 %copy-start.3 = (f32[16,128,256]{2,1,0:T(8,128)S(1)}, f32[16,128,256]{2,1,0:T(8,128)}, u32[]{:S(2)}) copy-start(f32[16,128,256]{2,1,0:T(8,128)} %get-tuple-element.148.refs_0_) | copy-start | bytes 6291460
  1145.2 153.1 %copy-start.6 = (f32[16,128,256]{2,1,0:T(8,128)S(1)}, f32[16,128,256]{2,1,0:T(8,128)}, u32[]{:S(2)}) copy-start(f32[16,128,256]{2,1,0:T(8,128)} %copy-done.5) | copy-start | bytes 6291460
  1228.3 143.6 %collective-permute-start.18 = (f32[8,128,256]{2,1,0:T(8,128)S(1)}, f32[8,128,256]{2,1,0:T(8,128)S(1)}, u32[]{:S(2)}, u32[]{:S(2)}) collective-permute-start(f32[8,128,256]{2,1,0:T(8,128)S(1)} %get-tuple-element.115), channel_id=1, source_target_pairs={{0,1},{1,2},{2,3},{3,0},{4,5},{5,6},{6,7},{7,4},{8,9},{9,10},{10,1... | collective-permute-start | bytes 3145736 | tf_op jit(solution)/shard_map/ppermute | solution.py:194
  1228.3 202.2 %collective-permute-start.19 = (f32[8,128,256]{2,1,0:T(8,128)S(1)}, f32[8,128,256]{2,1,0:T(8,128)S(1)}, u32[]{:S(2)}, u32[]{:S(2)}) collective-permute-start(f32[8,128,256]{2,1,0:T(8,128)S(1)} %get-tuple-element.116), channel_id=1, source_target_pairs={{0,2},{1,3},{2,0},{3,1},{4,6},{5,7},{6,4},{7,5},{8,10},{9,11},{10,... | collective-permute-start | bytes 3145736 | tf_op jit(solution)/shard_map/ppermute | solution.py:194
  1295.0 135.5 %collective-permute-start.20 = (f32[8,128,256]{2,1,0:T(8,128)S(1)}, f32[8,128,256]{2,1,0:T(8,128)S(1)}, u32[]{:S(2)}, u32[]{:S(2)}) collective-permute-start(f32[8,128,256]{2,1,0:T(8,128)S(1)} %get-tuple-element.117), channel_id=1, source_target_pairs={{0,3},{1,0},{2,1},{3,2},{4,7},{5,4},{6,5},{7,6},{8,11},{9,8},{10,9... | collective-permute-start | bytes 3145736 | tf_op jit(solution)/shard_map/ppermute | solution.py:194
  1298.3 64.9 %copy-start.2 = (f32[16,128,256]{2,1,0:T(8,128)S(1)}, f32[16,128,256]{2,1,0:T(8,128)}, u32[]{:S(2)}) copy-start(f32[16,128,256]{2,1,0:T(8,128)} %get-tuple-element.149.refs_0_) | copy-start | bytes 6291460
  1528.3 32.9 %copy-start.11 = (f32[128,1024]{1,0:T(8,128)}, f32[128,1024]{1,0:T(8,128)S(1)}, u32[]{:S(2)}) copy-start(f32[128,1024]{1,0:T(8,128)S(1)} %get-tuple-element.141.iterate) | copy-start | bytes 1572868
  1561.2 1.0 copy-start.12
  1599.6 0.8 copy-start.13
  1603.2 23.5 %all-to-all-start.4 = ((f32[32,17,256]{2,1,0:T(8,128)}), f32[32,17,256]{2,1,0:T(8,128)S(1)}, u32[]{:S(2)}, u32[]{:S(2)}) async-start(f32[32,17,256]{2,1,0:T(8,128)} %bitcast.15), calls=%async_computation.4 | async-start | bytes 1572864 | tf_op jit(solution)/shard_map/all_to_all | solution.py:169
